TPU v7x, 32 devices: a whole 2x2x4 slice. The times are simulated.
32 devices in a mesh: fsdp: 16 (over z, y, x), rep: 2 (over core).
Axes of the slice: x: 2, y: 2, z: 4, core: 2. Of those that a mesh axis runs over, the one named last changes fastest.
Arguments:
- frames: bfloat16 [64, 16, 5, 3, 49], P(('fsdp', 'rep')), may hold values from -6 to 6
- features: bfloat16 [64, 16, 49, 2048], P(('fsdp', 'rep')), may hold values from -6 to 6
- seg_counts: int32 [64], P(('fsdp', 'rep')), may hold values from 8 to 16, as said below
- stem_weight: bfloat16 [64, 588], P('fsdp'), may hold values from -0.25 to 0.25
- stem_gain: bfloat16 [64], P('fsdp'), may hold values from 0.5 to 1.5
- stem_shift: bfloat16 [64], P('fsdp'), may hold values from -3 to 3
- lateral: bfloat16 [64, 2048], P('fsdp'), may hold values from -0.75 to 0.75
- reduce_weight: bfloat16 [2048, 512], P('fsdp'), may hold values from -0.125 to 0.125
- gain_one: bfloat16 [512], P('fsdp'), may hold values from 0.5 to 1.5
- shift_one: bfloat16 [512], P('fsdp'), may hold values from -3 to 3
- diff_weight: bfloat16 [2, 4608, 512], P(None, 'fsdp'), may hold values from -0.09375 to 0.09375
- gate_shift: bfloat16 [512], P('fsdp'), may hold values from -3 to 3
- mid_weight: bfloat16 [4608, 512], P('fsdp'), may hold values from -0.09375 to 0.09375
- gain_two: bfloat16 [512], P('fsdp'), may hold values from 0.5 to 1.5
- shift_two: bfloat16 [512], P('fsdp'), may hold values from -3 to 3
- expand_weight: bfloat16 [512, 2048], P('fsdp'), may hold values from -0.25 to 0.25
- gain_three: bfloat16 [2048], P('fsdp'), may hold values from 0.5 to 1.5
- shift_three: bfloat16 [2048], P('fsdp'), may hold values from -3 to 3
- pooled_grad: bfloat16 [64, 49, 2048], P(('fsdp', 'rep')), may hold values from -6 to 6
Outputs:
- pooled: bfloat16 [64, 49, 2048], P(('fsdp', 'rep'))
- features_grad: float32 [64, 16, 49, 2048], P(('fsdp', 'rep'))
- stem_weight_grad: float32 [64, 588], P('fsdp')
- stem_gain_grad: float32 [64], P('fsdp')
- stem_shift_grad: float32 [64], P('fsdp')
- lateral_grad: float32 [64, 2048], P('fsdp')
- reduce_grad: float32 [2048, 512], P('fsdp')
- gain_one_grad: float32 [512], P('fsdp')
- shift_one_grad: float32 [512], P('fsdp')
- diff_grad: float32 [2, 4608, 512], P(None, 'fsdp')
- gate_grad: float32 [512], P('fsdp')
- mid_grad: float32 [4608, 512], P('fsdp')
- gain_two_grad: float32 [512], P('fsdp')
- shift_two_grad: float32 [512], P('fsdp')
- expand_grad: float32 [512, 2048], P('fsdp')
- gain_three_grad: float32 [2048], P('fsdp')
- shift_three_grad: float32 [2048], P('fsdp')
Inputs may be any that keep to these rules, and one draw needn't show every extreme that they name: `seg_counts`: each clip has 8 or 16 true segments, both counts occurring in every draw.
All inputs are finite; a program needn't handle non-finite values.
Results may differ from a plain program's by a relative error of at most 0.015.
Values may be sent and summed in bfloat16 or wider, within the bound.
A program may use at most 448 MiB of HBM per device.

v0:
```python
import functools

import jax
import jax.numpy as jnp
from jax import lax
from jax.experimental import pallas as pl
from jax.experimental.pallas import tpu as pltpu
from jax.sharding import PartitionSpec as P

GRID = 7
LANES = 128
PIXELS = GRID * GRID
epsilon = 1e-05
MESH = pl.DeviceIdType.MESH
ANY = pl.BlockSpec(memory_space=pl.ANY)
IN_VMEM = pl.BlockSpec(memory_space=pltpu.VMEM)
VMEM_LIMIT = 60 * 1024 * 1024
bf16 = jnp.bfloat16
f32 = jnp.float32
DMA = pltpu.SemaphoreType.DMA


def factor_three(size):
    best = None
    for b in range(1, size + 1):
        for c in range(1, b + 1):
            if size % (b * c) == 0 and size // (b * c) >= b:
                a = size // (b * c)
                if best is None or a + b + c < sum(best):
                    best = (a, b, c)
    return best


class Place:
    def __init__(self, dims, reps, rep=None):
        self.dims, self.reps = dims, reps
        size_a, size_b, size_c = dims
        self.me = lax.axis_index("fsdp")
        self.rep = lax.axis_index("rep") if rep is None else rep
        ib, ic = (self.me // size_c) % size_b, self.me % size_c
        self.ia = self.me // (size_b * size_c)
        odd = self.rep % 2 if size_b == size_c else 0
        self.stride_u = size_c * (1 - odd) + odd
        self.stride_v = (1 - odd) + size_c * odd
        self.iu = ib * (1 - odd) + ic * odd
        self.iv = ic * (1 - odd) + ib * odd

    def at(self, da, du, dv):
        size_a, size_b, size_c = self.dims
        a = (self.ia + da + size_a) % size_a
        u = (self.iu + du + size_b) % size_b
        v = (self.iv + dv + size_c) % size_c
        return a * (size_b * size_c) + u * self.stride_u + v * self.stride_v

    def greet(self):
        size_a, size_b, size_c = self.dims
        peers = [(self.at(d, 0, 0), self.rep) for d in range(1, size_a)]
        peers += [(self.at(0, d, 0), self.rep) for d in range(1, size_b)]
        peers += [(self.at(0, 0, d), self.rep) for d in range(1, size_c)]
        peers += [(self.me, (self.rep + d) % self.reps) for d in range(1, self.reps)]
        greet(peers)


def greet(peers):
    barrier = pltpu.get_barrier_semaphore()
    for target, rep in peers:
        pl.semaphore_signal(
            barrier, inc=1, device_id={"fsdp": target, "rep": rep}, device_id_type=MESH
        )
    pl.semaphore_wait(barrier, len(peers))


def remote(src, dst, sems, target, rep):
    return pltpu.make_async_remote_copy(
        src_ref=src,
        dst_ref=dst,
        send_sem=sems.at[0],
        recv_sem=sems.at[1],
        device_id={"fsdp": target, "rep": rep},
        device_id_type=MESH,
    )


def columns(width, which):
    start = which * width
    return pl.ds(start if isinstance(start, int) else pl.multiple_of(start, width), width)


def views(refs):
    out = []
    for ref, stacked in refs:
        out += [ref.at[j] for j in range(ref.shape[0])] if stacked else [ref]
    return out


def gather_kernel(dims, reps, stacked, *refs):
    number = len(stacked)
    shards = views(zip(refs[:number], stacked))
    fulls = views(zip(refs[number : 2 * number], stacked))
    own_sem, a_sem, b_sem, c_sem, r_sem = refs[2 * number :]
    count = len(shards)
    size_a, size_b, size_c = dims
    place = Place(dims, reps)
    me, rep = place.me, place.rep
    place.greet()
    waits = []

    def slot(k, index, which):
        return fulls[k].at[index, :, columns(fulls[k].shape[-1] // reps, which)]

    def push(k, da, du, dv, target, target_rep, sems):
        index = place.at(-da, -du, -dv)
        if (da, du, dv) == (0, 0, 0):
            source = shards[k].at[:, columns(shards[k].shape[-1] // reps, rep)]
        else:
            source = slot(k, index, rep)
        copy = remote(source, slot(k, index, rep), sems, target, target_rep)
        copy.start()
        waits.append(copy)

    def landed(k, da, du, dv, which, sems):
        there = slot(k, place.at(-da, -du, -dv), which)
        remote(there, there, sems, me, rep).wait_recv()

    def forward(k, da, du, dv):
        if dv == 0 and du == 0:
            for d in range(1, size_b):
                push(k, da, 0, 0, place.at(0, d, 0), rep, b_sem.at[k, da, d - 1])
        if dv == 0:
            for d in range(1, size_c):
                push(k, da, du, 0, place.at(0, 0, d), rep, c_sem.at[k, da, du, d - 1])
        if (da, du, dv) != (0, 0, 0):
            for d in range(1, reps):
                push(k, da, du, dv, me, (rep + d) % reps, r_sem.at[k, da, du, dv, d - 1])

    local = []
    for k in range(count):
        copy = pltpu.make_async_copy(shards[k], fulls[k].at[me], own_sem.at[k])
        copy.start()
        local.append(copy)
    for k in range(count):
        for d in range(1, size_a):
            push(k, 0, 0, 0, place.at(d, 0, 0), rep, a_sem.at[k, d - 1])
        forward(k, 0, 0, 0)
    for step in range(count + 2):
        if step < count:
            for da in range(1, size_a):
                landed(step, da, 0, 0, rep, a_sem.at[step, da - 1])
                forward(step, da, 0, 0)
        if 0 <= step - 1 < count:
            for du in range(1, size_b):
                for da in range(size_a):
                    landed(step - 1, da, du, 0, rep, b_sem.at[step - 1, da, du - 1])
                    forward(step - 1, da, du, 0)
        if 0 <= step - 2 < count:
            for dv in range(1, size_c):
                for du in range(size_b):
                    for da in range(size_a):
                        landed(step - 2, da, du, dv, rep, c_sem.at[step - 2, da, du, dv - 1])
                        forward(step - 2, da, du, dv)
    for k in range(count):
        for dv in range(size_c):
            for du in range(size_b):
                for da in range(size_a):
                    if (da, du, dv) != (0, 0, 0):
                        for d in range(1, reps):
                            landed(k, da, du, dv, (rep + reps - d) % reps, r_sem.at[k, da, du, dv, d - 1])
    for copy in waits:
        copy.wait_send()
    for copy in local:
        copy.wait()


def gather_all(shards, fsdp, reps, collective_id, name):
    dims = factor_three(fsdp)
    size_a, size_b, size_c = dims
    stacked = [s.ndim == 3 for s in shards]
    count = sum(s.shape[0] if s.ndim == 3 else 1 for s in shards)
    return pl.pallas_call(
        functools.partial(gather_kernel, dims, reps, stacked),
        out_shape=[
            jax.ShapeDtypeStruct(s.shape[:-2] + (fsdp,) + s.shape[-2:], s.dtype) for s in shards
        ],
        in_specs=[ANY] * len(shards),
        out_specs=[ANY] * len(shards),
        scratch_shapes=[
            DMA((count,)),
            DMA((count, max(size_a - 1, 1), 2)),
            DMA((count, size_a, max(size_b - 1, 1), 2)),
            DMA((count, size_a, size_b, max(size_c - 1, 1), 2)),
            DMA((count, size_a, size_b, size_c, max(reps - 1, 1), 2)),
        ],
        compiler_params=pltpu.CompilerParams(
            collective_id=collective_id, has_side_effects=True, vmem_limit_bytes=VMEM_LIMIT
        ),
        name=name,
    )(*shards)


def scatter_kernel(dims, reps, stacked, *refs):
    number = len(stacked)
    partials = views(zip(refs[:number], stacked))
    totals = views(zip(refs[number : 2 * number], stacked))
    count = len(partials)
    rest = refs[2 * number :]
    held, from_rep, from_v, from_u, from_a, share = (rest[i * count : (i + 1) * count] for i in range(6))
    own_sem, r_sem, v_sem, u_sem, a_sem, s_sem = rest[6 * count :]
    size_a, size_b, size_c = dims
    place = Place(dims, reps)
    me, rep = place.me, place.rep
    place.greet()
    waits = []

    def push(source, there, sems, target, target_rep):
        copy = remote(source, there, sems, target, target_rep)
        copy.start()
        waits.append(copy)

    def landed(there, sems):
        remote(there, there, sems, me, rep).wait_recv()

    def order():
        for dv in list(range(1, size_c)) + [0]:
            for du in list(range(1, size_b)) + [0]:
                for da in list(range(1, size_a)) + [0]:
                    yield da, du, dv

    local = {}
    for k in range(count):
        width = partials[k].shape[-1] // reps
        for da, du, dv in order():
            for d in range(1, reps):
                other = (rep + d) % reps
                index = Place(dims, reps, other).at(da, du, dv)
                push(
                    partials[k].at[index, :, columns(width, other)],
                    from_rep[k].at[d - 1, index],
                    r_sem.at[k, da, du, dv, d - 1],
                    me,
                    other,
                )
            index = place.at(da, du, dv)
            copy = pltpu.make_async_copy(
                partials[k].at[index, :, columns(width, rep)],
                held[k].at[index],
                own_sem.at[k, da, du, dv],
            )
            copy.start()
            local[k, da, du, dv] = copy

    def handle(k, da, du, dv):
        index = place.at(da, du, dv)
        local[k, da, du, dv].wait()
        total = held[k][index].astype(f32)
        for d in range(1, reps):
            landed(from_rep[k].at[d - 1, index], r_sem.at[k, da, du, dv, d - 1])
            total = total + from_rep[k][d - 1, index].astype(f32)
        if dv == 0:
            for e in range(1, size_c):
                landed(from_v[k].at[e - 1, da, du], v_sem.at[k, da, du, e - 1])
                total = total + from_v[k][e - 1, da, du].astype(f32)
            if du == 0:
                for e in range(1, size_b):
                    landed(from_u[k].at[e - 1, da], u_sem.at[k, da, e - 1])
                    total = total + from_u[k][e - 1, da].astype(f32)
                if da == 0:
                    for e in range(1, size_a):
                        landed(from_a[k].at[e - 1], a_sem.at[k, e - 1])
                        total = total + from_a[k][e - 1].astype(f32)
        if (da, du, dv) == (0, 0, 0):
            share[k][rep] = total.astype(bf16)
            for d in range(1, reps):
                push(share[k].at[rep], share[k].at[rep], s_sem.at[k, d - 1], me, (rep + d) % reps)
            return
        held[k][index] = total.astype(bf16)
        if dv:
            push(held[k].at[index], from_v[k].at[dv - 1, da, du], v_sem.at[k, da, du, dv - 1], place.at(0, 0, dv), rep)
        elif du:
            push(held[k].at[index], from_u[k].at[du - 1, da], u_sem.at[k, da, du - 1], place.at(0, du, 0), rep)
        else:
            push(held[k].at[index], from_a[k].at[da - 1], a_sem.at[k, da - 1], place.at(da, 0, 0), rep)

    for step in range(count + 3):
        for lag in range(4):
            k = step - lag
            for da, du, dv in order() if 0 <= k < count else ():
                if lag == (0 if dv else 1 if du else 2 if da else 3):
                    handle(k, da, du, dv)
    for k in range(count):
        width = partials[k].shape[-1] // reps
        for d in range(1, reps):
            landed(share[k].at[(rep + reps - d) % reps], s_sem.at[k, d - 1])
        for which in range(reps):
            totals[k][:, which * width : (which + 1) * width] = share[k][which].astype(f32)
    for copy in waits:
        copy.wait_send()


def scatter_all(partials, fsdp, reps, collective_id, name):
    dims = factor_three(fsdp)
    size_a, size_b, size_c = dims
    stacked = [p.ndim == 4 for p in partials]
    shapes = []
    for p in partials:
        shapes += [(p.shape[-2], p.shape[-1] // reps)] * (p.shape[0] if p.ndim == 4 else 1)
    count = len(shapes)

    def buffers(*lead):
        return [pltpu.VMEM(lead + shape, bf16) for shape in shapes]

    return pl.pallas_call(
        functools.partial(scatter_kernel, dims, reps, stacked),
        out_shape=[
            jax.ShapeDtypeStruct(p.shape[:-3] + p.shape[-2:], f32) for p in partials
        ],
        in_specs=[ANY] * len(partials),
        out_specs=[IN_VMEM] * len(partials),
        scratch_shapes=buffers(fsdp)
        + buffers(max(reps - 1, 1), fsdp)
        + buffers(max(size_c - 1, 1), size_a, size_b)
        + buffers(max(size_b - 1, 1), size_a)
        + buffers(max(size_a - 1, 1))
        + buffers(reps)
        + [
            DMA((count, size_a, size_b, size_c)),
            DMA((count, size_a, size_b, size_c, max(reps - 1, 1), 2)),
            DMA((count, size_a, size_b, max(size_c - 1, 1), 2)),
            DMA((count, size_a, max(size_b - 1, 1), 2)),
            DMA((count, max(size_a - 1, 1), 2)),
            DMA((count, max(reps - 1, 1), 2)),
        ],
        compiler_params=pltpu.CompilerParams(
            collective_id=collective_id, has_side_effects=True, vmem_limit_bytes=VMEM_LIMIT
        ),
        name=name,
    )(*partials)


def stage_sizes(devices):
    sizes = []
    while devices > 1:
        size = next(s for s in (8, 4, 2, 7, 5, 3, devices) if devices % s == 0)
        sizes.append(size)
        devices //= size
    return sizes


def exchange_kernel(sizes, reps, moments, width, *refs):
    number = 3 if moments else 2
    sources, results = refs[:number], refs[number : 2 * number]
    mine, slots, sems = refs[2 * number], refs[2 * number + 1 : -1], refs[-1]
    place = lax.axis_index("fsdp") * reps + lax.axis_index("rep")
    stages = []
    stride = 1
    for size in sizes:
        position = (place // stride) % size
        peers = []
        for d in range(1, size):
            target = place + ((position + d) % size - position) * stride
            peers.append((target // reps, target % reps))
        stages.append((size, position, peers))
        stride *= size
    greet([peer for stage in stages for peer in stage[2]])
    spans = [(0, width), (width, width), (2 * width, LANES)][:number]
    current = [source[...] for source in sources]
    waits = []
    for index, (size, position, peers) in enumerate(stages):
        for (start, length), value in zip(spans, current):
            mine[index, :, start : start + length] = value
        for d, (target, rep) in enumerate(peers, 1):
            copy = remote(mine.at[index], slots[index].at[position], sems.at[index, d - 1], target, rep)
            copy.start()
            waits.append(copy)
        slots[index][position] = mine[index]
        for d, (target, rep) in enumerate(peers, 1):
            there = slots[index].at[(position + size - d) % size]
            remote(there, there, sems.at[index, d - 1], target, rep).wait_recv()
        parts = [
            [slots[index][j, :, start : start + length] for start, length in spans] for j in range(size)
        ]
        current = [functools.reduce(jnp.add, [part[row] for part in parts]) for row in range(number)]
        if moments:
            centre = current[0] / current[2][:, :1]
            squares = current[1]
            for part in parts:
                count = part[2][:, :1]
                off = part[0] / count - centre
                squares = squares + count * off * off
            current[1] = squares
    for result, value in zip(results, current):
        result[...] = value
    for copy in waits:
        copy.wait_send()


def exchange(rows, fsdp, reps, moments, collective_id, name):
    sizes = stage_sizes(fsdp * reps)
    width = rows[0].shape[-1]
    padded = -(-width // LANES) * LANES
    rows = [jnp.pad(row.reshape(1, -1), ((0, 0), (0, padded - width))) for row in rows[:2]] + [
        jnp.broadcast_to(row.reshape(1, 1), (1, LANES)) for row in rows[2:]
    ]
    total = sum(row.shape[1] for row in rows)
    results = pl.pallas_call(
        functools.partial(exchange_kernel, sizes, reps, moments, padded),
        out_shape=[jax.ShapeDtypeStruct(row.shape, f32) for row in rows],
        in_specs=[IN_VMEM] * len(rows),
        out_specs=[IN_VMEM] * len(rows),
        scratch_shapes=[pltpu.VMEM((len(sizes), 1, total), f32)]
        + [pltpu.VMEM((size, 1, total), f32) for size in sizes]
        + [DMA((len(sizes), max(max(sizes) - 1, 1), 2))],
        compiler_params=pltpu.CompilerParams(
            collective_id=collective_id, has_side_effects=True, vmem_limit_bytes=4 * 1024 * 1024
        ),
        name=name,
    )(*rows)
    return [result[0, :width] for result in results[:2]] + [result[0, 0] for result in results[2:]]


ORDER = ("HWNC", "HWIO", "HWNC")


def pad_of(span):
    return ((span, span), (span, span))


def convolve(source, weight, span, stride):
    side = 2 * span + 1
    kernel = weight.reshape(side, side, source.shape[-1], -1)
    return lax.conv_general_dilated(
        source, kernel, (1, 1), pad_of(span * stride), rhs_dilation=(stride, stride),
        dimension_numbers=ORDER, preferred_element_type=f32,
    )


def convolve_back(grads, weight, span, stride):
    side = 2 * span + 1
    kernel = weight.reshape(side, side, -1, grads.shape[-1])[::-1, ::-1]
    return lax.conv_general_dilated(
        grads, kernel, (1, 1), pad_of(span * stride), rhs_dilation=(stride, stride),
        dimension_numbers=("HWNC", "HWOI", "HWNC"), preferred_element_type=f32,
    )


def convolve_terms(source, grads, span, stride, kind):
    return lax.conv_general_dilated(
        source, grads, (stride, stride), pad_of(span * stride),
        dimension_numbers=("HWCN", "HWIO", "HWNC"), preferred_element_type=kind,
    )


def pool_mean(source):
    total = lax.reduce_window(source, 0.0, lax.add, (3, 3, 1, 1), (1, 1, 1, 1), "SAME")
    return total / 9.0


def project(source, weight):
    return jnp.einsum("yxnc,cd->yxnd", source, weight, preferred_element_type=f32)


def project_back(grads, weight):
    return jnp.einsum("yxnd,cd->yxnc", grads, weight, preferred_element_type=f32)


def project_terms(source, grads, kind):
    return jnp.einsum("yxnc,yxnd->cd", source, grads, preferred_element_type=kind)


def gelu_back(pre_act, grads):
    return jax.vjp(jax.nn.gelu, pre_act)[1](grads)[0]


def make_shards(fsdp, reps):
    def shards(
        frames, features, seg_counts, stem_weight, stem_gain, stem_shift, lateral, reduce_weight,
        gain_one, shift_one, diff_weight, gate_shift, mid_weight, gain_two, shift_two,
        expand_weight, gain_three, shift_three, pooled_grad,
    ):
        clip_count, seg_slots, pixels, feature_width = features.shape
        slots = clip_count * seg_slots
        mid_width = reduce_weight.shape[1]
        stem_rows, stem_depth = stem_weight.shape
        stem_width = stem_rows * fsdp

        seg_index = lax.broadcasted_iota(jnp.int32, (clip_count, seg_slots), 1)
        valid_seg = (seg_index < seg_counts[:, None]).astype(f32)
        pair_seg = valid_seg * jnp.concatenate(
            [valid_seg[:, 1:], jnp.zeros((clip_count, 1), f32)], axis=1
        )
        valid = valid_seg.reshape(1, 1, slots, 1)
        pair = pair_seg.reshape(1, 1, slots, 1)
        count_float = seg_counts.astype(f32)
        local_count = jnp.sum(count_float) * pixels

        vectors = [gain_three, shift_three, gain_one, shift_one, gate_shift, gain_two, shift_two, stem_gain, stem_shift]
        row = jnp.concatenate(vectors)
        small = jnp.concatenate(
            [
                lateral,
                jnp.pad(stem_weight, ((0, 0), (0, feature_width - stem_depth))),
                jnp.pad(row[None], ((0, 15 - 2 * stem_rows), (0, feature_width - row.shape[0]))),
            ]
        )
        small_full, reduce_full, diff_full, mid_full, expand_full = gather_all(
            [small, reduce_weight, diff_weight, mid_weight, expand_weight], fsdp, reps, 1, "gather_weights"
        )
        lateral_full = small_full[:, :stem_rows].reshape(stem_width, feature_width)
        stem_full = small_full[:, stem_rows : 2 * stem_rows, :stem_depth].reshape(stem_width, stem_depth)
        full = []
        start = 0
        for vector in vectors:
            size = vector.shape[0]
            full.append(small_full[:, 2 * stem_rows, start : start + size].reshape(-1).astype(f32))
            start += size
        (gain_three_full, shift_three_full, gain_one_full, shift_one_full, gate_full, gain_two_full,
         shift_two_full, stem_gain_full, stem_shift_full) = full
        reduce_full = reduce_full.reshape(-1, mid_width)
        diff_full = diff_full.reshape(2, -1, mid_width)
        mid_full = mid_full.reshape(-1, mid_width)
        expand_full = expand_full.reshape(mid_width, -1)

        def moments(values, collective_id, name):
            total = jnp.sum(values * valid, axis=(0, 1, 2))
            off = values - total / local_count
            squares = jnp.sum(off * off * valid, axis=(0, 1, 2))
            total, squares, count = exchange(
                [total, squares, local_count], fsdp, reps, True, collective_id, name
            )
            centre = total / count
            return centre, lax.rsqrt(squares / count + epsilon), count

        def norm(values, stats, gain, shift):
            normed = (values - stats[0]) * stats[1]
            return valid * (gain * normed + shift), normed

        def norm_back(grad_out, normed, stats, gain, collective_id, name):
            masked = grad_out * valid
            shift_sum, gain_sum = exchange(
                [jnp.sum(masked, axis=(0, 1, 2)), jnp.sum(masked * normed, axis=(0, 1, 2))],
                fsdp, reps, False, collective_id, name,
            )
            grad_in = valid * stats[1] * gain * (masked - shift_sum / stats[2] - normed * gain_sum / stats[2])
            return grad_in.astype(bf16), gain_sum, shift_sum

        moving = frames.astype(f32)
        motion = (moving[:, :, 1:] - moving[:, :, :-1]) * valid_seg[:, :, None, None, None]
        motion = jnp.transpose(motion.astype(bf16), (4, 0, 1, 2, 3)).reshape(GRID, GRID, slots, -1)
        stem_kernel = jnp.transpose(stem_full.reshape(stem_width, GRID, GRID, -1), (1, 2, 3, 0))
        stem_pre = convolve(motion, stem_kernel, 3, 1)
        stem_stats = moments(stem_pre, 2, "stem_moments")
        stem_norm, stem_normed = norm(stem_pre, stem_stats, stem_gain_full, stem_shift_full)
        pool_low = pool_mean(jax.nn.gelu(stem_norm)).astype(bf16)
        turned = jnp.transpose(features.reshape(slots, GRID, GRID, feature_width), (1, 2, 0, 3))
        block_in = turned.astype(f32) + project(pool_low, lateral_full)
        block_low = block_in.astype(bf16)
        reduced = project(block_low, reduce_full)
        stats_one = moments(reduced, 3, "moments_one")
        zeta_one, normed_one = norm(reduced, stats_one, gain_one_full, shift_one_full)
        act_one = jax.nn.gelu(zeta_one)
        def later_of(values):
            grid = values.reshape(GRID, GRID, clip_count, seg_slots, -1)
            return jnp.pad(grid[:, :, :, 1:], ((0, 0), (0, 0), (0, 0), (0, 1), (0, 0))).reshape(values.shape)

        def earlier_of(values):
            grid = values.reshape(GRID, GRID, clip_count, seg_slots, -1)
            return jnp.pad(grid[:, :, :, :-1], ((0, 0), (0, 0), (0, 0), (1, 0), (0, 0))).reshape(values.shape)

        change = ((later_of(act_one) - act_one) * pair).astype(bf16)
        gate_pre = convolve(change, diff_full[0], 1, 1) + convolve(change, diff_full[1], 1, 2)
        gate = jax.nn.sigmoid(gate_pre + gate_full)
        modulated = (act_one * (1.0 + gate)).astype(bf16)
        middle = convolve(modulated, mid_full, 1, 1)
        stats_two = moments(middle, 4, "moments_two")
        zeta_two, normed_two = norm(middle, stats_two, gain_two_full, shift_two_full)
        act_two = jax.nn.gelu(zeta_two).astype(bf16)
        expanded = project(act_two, expand_full)
        stats_three = moments(expanded, 5, "moments_three")
        zeta_three, normed_three = norm(expanded, stats_three, gain_three_full, shift_three_full)
        pre_out = block_in + zeta_three
        block_out = jax.nn.gelu(pre_out) * valid
        summed = jnp.sum(block_out.reshape(pixels, clip_count, seg_slots, feature_width), axis=2)
        pooled = jnp.transpose((summed / count_float[None, :, None]).astype(bf16), (1, 0, 2))

        spread = jnp.transpose(pooled_grad, (1, 0, 2)).astype(f32)[:, :, None]
        spread = spread * (valid_seg / count_float[:, None])[None, :, :, None]
        grad_pre = gelu_back(pre_out, spread.reshape(pre_out.shape))
        grad_expanded, gain_three_sum, shift_three_sum = norm_back(
            grad_pre, normed_three, stats_three, gain_three_full, 6, "sums_three"
        )
        expand_terms = project_terms(act_two, grad_expanded, bf16)
        grad_act_two = project_back(grad_expanded, expand_full)
        grad_middle, gain_two_sum, shift_two_sum = norm_back(
            gelu_back(zeta_two, grad_act_two), normed_two, stats_two, gain_two_full, 7, "sums_two"
        )
        mid_terms = convolve_terms(modulated, grad_middle, 1, 1, bf16)
        grad_modulated = convolve_back(grad_middle, mid_full, 1, 1)
        grad_gate_pre = grad_modulated * act_one * gate * (1.0 - gate)
        gate_terms = jnp.sum(grad_gate_pre, axis=(0, 1, 2))
        grad_gate = grad_gate_pre.astype(bf16)
        diff_terms = [convolve_terms(change, grad_gate, 1, 1, bf16), convolve_terms(change, grad_gate, 1, 2, bf16)]
        grad_change = convolve_back(grad_gate, diff_full[0], 1, 1) + convolve_back(grad_gate, diff_full[1], 1, 2)
        grad_change = grad_change * pair
        grad_act_one = grad_modulated * (1.0 + gate) + earlier_of(grad_change) - grad_change
        grad_reduced, gain_one_sum, shift_one_sum = norm_back(
            gelu_back(zeta_one, grad_act_one), normed_one, stats_one, gain_one_full, 8, "sums_one"
        )
        reduce_terms = project_terms(block_low, grad_reduced, bf16)
        features_grad = grad_pre + project_back(grad_reduced, reduce_full)
        grad_lateral = features_grad.astype(bf16)
        lateral_terms = project_terms(pool_low, grad_lateral, bf16)
        grad_act = pool_mean(project_back(grad_lateral, lateral_full))
        grad_stem, stem_gain_sum, stem_shift_sum = norm_back(
            gelu_back(stem_norm, grad_act), stem_normed, stem_stats, stem_gain_full, 9, "sums_stem"
        )
        stem_terms = convolve_terms(motion, grad_stem, 3, 1, bf16)
        stem_terms = jnp.transpose(stem_terms, (3, 0, 1, 2)).reshape(fsdp, stem_rows, stem_depth)
        gate_rows = gate_shift.shape[0]
        small_terms = jnp.concatenate(
            [
                lateral_terms.reshape(fsdp, stem_rows, feature_width),
                jnp.pad(stem_terms, ((0, 0), (0, 0), (0, feature_width - stem_depth))),
                jnp.pad(
                    gate_terms.astype(bf16).reshape(fsdp, 1, gate_rows),
                    ((0, 0), (0, 15 - 2 * stem_rows), (0, feature_width - gate_rows)),
                ),
            ],
            axis=1,
        )

        def owned(terms, shard):
            return terms.reshape(shard.shape[:-2] + (fsdp,) + shard.shape[-2:])

        diff_one, diff_two, mid_part, expand_part, reduce_part, small_part = scatter_all(
            [
                owned(diff_terms[0], diff_weight[0]), owned(diff_terms[1], diff_weight[1]),
                owned(mid_terms, mid_weight), owned(expand_terms, expand_weight),
                owned(reduce_terms, reduce_weight), small_terms,
            ],
            fsdp, reps, 10, "scatter_terms",
        )

        def own_share(whole):
            share = whole.shape[0] // fsdp
            return lax.dynamic_slice_in_dim(whole, lax.axis_index("fsdp") * share, share)

        out = jnp.transpose(features_grad, (2, 0, 1, 3)).reshape(features.shape)
        return (
            pooled,
            out,
            small_part[stem_rows : 2 * stem_rows, :stem_depth],
            own_share(stem_gain_sum),
            own_share(stem_shift_sum),
            small_part[:stem_rows],
            reduce_part,
            own_share(gain_one_sum),
            own_share(shift_one_sum),
            jnp.stack([diff_one, diff_two]),
            small_part[2 * stem_rows, :gate_rows],
            mid_part,
            own_share(gain_two_sum),
            own_share(shift_two_sum),
            expand_part,
            own_share(gain_three_sum),
            own_share(shift_three_sum),
        )

    return shards


def solution(mesh):
    whole = ("fsdp", "rep")
    matrix, vector = P("fsdp", None), P("fsdp")
    in_specs = (
        P(whole, None, None, None, None), P(whole, None, None, None), P(whole),
        matrix, vector, vector, matrix, matrix, vector, vector, P(None, "fsdp", None), vector,
        matrix, vector, vector, matrix, vector, vector, P(whole, None, None),
    )
    out_specs = (
        P(whole, None, None), P(whole, None, None, None), matrix, vector, vector, matrix, matrix,
        vector, vector, P(None, "fsdp", None), vector, matrix, vector, vector, matrix, vector, vector,
    )
    body = make_shards(mesh.shape["fsdp"], mesh.shape["rep"])
    return jax.shard_map(body, mesh=mesh, in_specs=in_specs, out_specs=out_specs, check_vma=False)
```

profile of v0, /device:TPU:0, one launch (start us, length us, event | category | flops | bytes accessed | tf_op | source)
XLA Modules:
  0.0 593.4 jit_solution(609583364152833109)
XLA Ops:
  1.5 6.1 %concatenate.12 = bf16[424]{0:T(512)(128)(2,1)S(1)} concatenate(bf16[128]{0:T(256)(128)(2,1)} %param.35, bf16[128]{0:T(256)(128)(2,1)} %param.36, bf16[32]{0:T(256)(128)(2,1)} %param.27, bf16[32]{0:T(256)(128)(2,1)} %param.28, bf16[32]{0:T(256)(128)(2,1)} %param.30, bf16[32]{0:T(256)(128)(2,1)} %param.32, bf16[32]{0:T(256)(128)(2,1)} %param.33, bf16[4]{0:T(256)(128)(2,1)} %param.23, ...), dimensions={0} | concatenate | bytes 1696 | tf_op jit(solution)/shard_map/concatenate | solution.py:496
  7.6 1.4 fusion.75.refs_0_
  9.0 93.2 %gather_weights.1 = (bf16[16,16,2048]{2,1,0:T(8,128)(2,1)}, bf16[16,128,512]{2,1,0:T(8,128)(2,1)}, bf16[2,16,288,512]{3,2,1,0:T(8,128)(2,1)}, bf16[16,288,512]{2,1,0:T(8,128)(2,1)}, bf16[16,32,2048]{2,1,0:T(8,128)(2,1)}) custom-call(bf16[16,2048]{1,0:T(8,128)(2,1)} %fusion.75.refs_0_, bf16[128,512]{1,0:T(8,128)(2,1)} %refs_1_.1, ...), custom_call_target="tpu_custom_call" | custom-call | tf_op jit(solution)/shard_map/gather_weights/pallas_call | solution.py:179
  102.2 9.3 %copy.46 = f32[2,16,49,2048]{3,1,0,2:T(8,128)} copy(bf16[2,16,49,2048]{3,1,2,0:T(8,128)(2,1)} %param.20) | data formatting | bytes 19267584 | tf_op jit(solution)/shard_map/convert_element_type | solution.py:554
  113.7 5.7 multiply_reduce_fusion.12
  122.1 13.3 %stem_moments.1 = (f32[1,128]{1,0:T(1,128)S(1)}, f32[1,128]{1,0:T(1,128)S(1)}, f32[1,128]{1,0:T(1,128)S(1)}) custom-call(f32[1,128]{1,0:T(1,128)S(1)} %pad.40.refs_0_, f32[1,128]{1,0:T(1,128)S(1)} %pad.41.refs_1_, f32[1,128]{1,0:T(1,128)S(1)} %broadcast_in_dim.5.refs_2_), custom_call_target="tpu_custom_call" | custom-call | tf_op jit(solution)/shard_map/stem_moments/pallas_call | solution.py:404
  136.8 1.3 slice.99
  138.2 11.7 %fusion.96 = (bf16[7,7,32,2048]{3,2,1,0:T(8,128)(2,1)S(1)}, f32[7,7,32,2048]{3,2,1,0:T(8,128)}) fusion(f32[7,7,32,2048]{3,2,1,0:T(8,128)} %bitcast.197, bf16[7,7,32,64]{3,2,1,0:T(8,128)(2,1)S(1)} %fusion.37, bf16[64,2048,1,1]{1,0,2,3:T(8,128)(2,1)S(1)} %reshape.605), kind=kOutput, calls=%fused_computation.189 | convolution fusion | flops 417464320 | bytes 32575488 | tf_op jit(solution)/shard_map/yxnc,cd->yxnd/dot_general | solution.py:458
  149.9 5.3 multiply_reduce_fusion.9
  155.3 1.1 convert_reduce_fusion.4
  156.4 2.5 multiply_reduce_fusion.8
  158.9 9.2 %moments_one.1 = (f32[1,512]{1,0:T(1,128)S(1)}, f32[1,512]{1,0:T(1,128)S(1)}, f32[1,128]{1,0:T(1,128)S(1)}) custom-call(f32[1,512]{1,0:T(1,128)S(1)} %bitcast.180, f32[1,512]{1,0:T(1,128)S(1)} %bitcast.182, f32[1,128]{1,0:T(1,128)S(1)} %broadcast_in_dim.5.refs_2_), custom_call_target="tpu_custom_call" | custom-call | tf_op jit(solution)/shard_map/moments_one/pallas_call | solution.py:404
  168.2 5.1 multiply_multiply_fusion.7
  173.4 2.5 slice.122
  175.9 2.1 pad.42
  178.2 4.7 fusion.28
  182.9 6.7 %fusion.93 = (bf16[1,16,288,512]{3,2,1,0:T(8,128)(2,1)S(1)}, bf16[1,16,288,512]{3,2,1,0:T(8,128)(2,1)}) fusion(bf16[2,16,288,512]{3,2,1,0:T(8,128)(2,1)} %get-tuple-element.56), kind=kLoop, calls=%fused_computation.186 | loop fusion | bytes 18874368 | tf_op jit(solution)/shard_map/slice | solution.py:569
  189.6 14.5 %fusion.98 = f32[7,7,32,512]{3,2,1,0:T(8,128)S(1)} fusion(bf16[7,7,32,512]{3,2,1,0:T(8,128)(2,1)S(1)} %fusion.28, bf16[3,3,512,512]{3,2,1,0:T(8,128)(2,1)} %bitcast.207), kind=kOutput, calls=%fused_computation.191 | convolution fusion | flops 6056574976 | bytes 9535488 | tf_op jit(solution)/shard_map/conv_general_dilated | solution.py:430
  204.2 10.3 %multiply_convert_fusion.4 = (bf16[7,7,32,512]{3,2,1,0:T(8,128)(2,1)S(1)}, f32[7,7,32,512]{3,2,1,0:T(8,128)}) fusion(f32[7,7,32,512]{3,2,1,0:T(8,128)S(1)} %copy-done.8, f32[512]{0:T(512)S(1)} %reshape.601, f32[7,7,32,512]{3,2,1,0:T(8,128)S(1)} %fusion.98, bf16[7,7,32,512]{3,2,1,0:T(8,128)(2,1)S(1)} %fusion.28, bf16[3,3,512,512]{3,2,1,0:T(8,128)(2,1)S(1)} %bitcast.202), kind=kOutput, calls=%fused_computation.58 | convolution fusion | flops 4855037952 | bytes 17565696 | tf_op jit(solution)/shard_map/conv_general_dilated | solution.py:430
  214.5 9.5 %multiply_reduce_fusion.7 = (f32[512]{0:T(512)S(1)}, f32[7,7,32,512]{3,2,1,0:T(8,128)}) fusion(f32[32]{0:T(128)S(1)} %reshape.594, bf16[7,7,32,512]{3,2,1,0:T(8,128)(2,1)S(1)} %get-tuple-element.149, bf16[3,3,512,512]{3,2,1,0:T(8,128)(2,1)S(1)} %bitcast.217), kind=kOutput, calls=%fused_computation.57 | convolution fusion | flops 6058180096 | bytes 9537664 | tf_op jit(solution)/shard_map/conv_general_dilated | solution.py:430
  224.1 2.5 multiply_reduce_fusion.6
  226.5 9.2 %moments_two.1 = (f32[1,512]{1,0:T(1,128)S(1)}, f32[1,512]{1,0:T(1,128)S(1)}, f32[1,128]{1,0:T(1,128)S(1)}) custom-call(f32[1,512]{1,0:T(1,128)S(1)} %bitcast.181, f32[1,512]{1,0:T(1,128)S(1)} %bitcast.183, f32[1,128]{1,0:T(1,128)S(1)} %broadcast_in_dim.5.refs_2_), custom_call_target="tpu_custom_call" | custom-call | tf_op jit(solution)/shard_map/moments_two/pallas_call | solution.py:404
  235.9 7.4 %multiply_reduce_fusion.2 = (f32[2048]{0:T(1024)S(1)}, f32[7,7,32,2048]{3,2,1,0:T(8,128)S(1)}) fusion(f32[32]{0:T(128)S(1)} %reshape.594, bf16[512,2048,1,1]{1,0,3,2:T(8,128)(2,1)} %bitcast.262, f32[7,7,32,512]{3,2,1,0:T(8,128)} %get-tuple-element.152, f32[512]{0:T(512)S(1)} %reshape.602, f32[512]{0:T(512)S(1)} %bitcast.247, f32[512]{0:T(512)S(1)} %bitcast.252, ...), kind=kOutput, calls=%fused_computation.14 | convolution fusion | flops 3305994240 | bytes 18169984 | tf_op jit(solution)/shard_map/yxnc,cd->yxnd/dot_general | solution.py:458
  243.3 2.0 multiply_reduce_fusion.1
  245.3 2.6 copy-done.6
  247.8 9.6 %moments_three.1 = (f32[1,2048]{1,0:T(1,128)S(1)}, f32[1,2048]{1,0:T(1,128)S(1)}, f32[1,128]{1,0:T(1,128)S(1)}) custom-call(f32[1,2048]{1,0:T(1,128)S(1)} %bitcast.169, f32[1,2048]{1,0:T(1,128)S(1)} %bitcast.168, f32[1,128]{1,0:T(1,128)S(1)} %broadcast_in_dim.5.refs_2_), custom_call_target="tpu_custom_call" | custom-call | tf_op jit(solution)/shard_map/moments_three/pallas_call | solution.py:404
  258.8 6.3 %mul.705 = f32[49,2,16,2048]{3,2,1,0:T(8,128)} broadcast(f32[49,2,2048]{2,1,0:T(2,128)S(1)} %convert_bitcast_fusion), dimensions={0,1,3} | broadcast | bytes 13647872 | tf_op jit(solution)/shard_map/mul | solution.py:585
  265.3 25.7 %multiply_reduce_fusion = (f32[2048]{0:T(1024)S(1)}, f32[2048]{0:T(1024)S(1)}, f32[7,7,32,2048]{3,2,1,0:T(8,128)}, f32[7,7,32,2048]{3,2,1,0:T(8,128)}) fusion(f32[7,7,32,2048]{3,2,1,0:T(8,128)} %copy-done.6, f32[2048]{0:T(1024)S(1)} %bitcast.229, f32[2048]{0:T(1024)S(1)} %bitcast.239, f32[32]{0:T(128)S(1)} %reshape.594, ...), kind=kLoop, calls=%fused_computation.9 | loop fusion | flops 102756352 | bytes 64274688 | tf_op jit(solution)/shard_map/reduce_sum | solution.py:539
  291.0 8.0 %reduce_sum.180 = f32[49,2,2048]{2,1,0:T(2,128)S(1)} reduce(f32[49,2,16,2048]{3,2,1,0:T(8,128)} %bitcast.199, f32[]{:T(128)} %constant.21.clone.1), dimensions={2}, to_apply=%region_10.11 | reduce | flops 3010560 | bytes 13647876 | tf_op jit(solution)/shard_map/reduce_sum | solution.py:581
  299.0 1.1 fusion.63
  300.1 9.7 %sums_three.1 = (f32[1,2048]{1,0:T(1,128)S(1)}, f32[1,2048]{1,0:T(1,128)S(1)}) custom-call(f32[1,2048]{1,0:T(1,128)S(1)} %bitcast.167, f32[1,2048]{1,0:T(1,128)S(1)} %bitcast.166), custom_call_target="tpu_custom_call" | custom-call | tf_op jit(solution)/shard_map/sums_three/pallas_call | solution.py:404
  310.6 11.2 %multiply_convert_fusion = bf16[7,7,32,2048]{3,2,1,0:T(8,128)(2,1)S(1)} fusion(f32[7,7,32,2048]{3,2,1,0:T(8,128)} %get-tuple-element.129, f32[7,7,32,2048]{3,2,1,0:T(8,128)} %copy-done.6, f32[]{:T(128)S(1)} %bitcast.188, f32[2048]{0:T(1024)S(1)} %bitcast.184, f32[2048]{0:T(1024)S(1)} %bitcast.246, f32[32,2048]{1,0:T(8,128)S(1)} %multiply_multiply_fusion.10, ...), kind=kLoop, calls=%fused_computation.8 | loop fusion | flops 28901376 | bytes 32407684 | tf_op jit(solution)/shard_map/convert_element_type | solution.py:543
  321.8 8.1 %multiply_reduce_fusion.5 = (f32[512]{0:T(512)S(1)}, f32[512]{0:T(512)S(1)}, f32[7,7,32,512]{3,2,1,0:T(8,128)}) fusion(f32[7,7,32,512]{3,2,1,0:T(8,128)S(1)} %copy-done.13, f32[512]{0:T(512)S(1)} %bitcast.248, f32[512]{0:T(512)S(1)} %bitcast.253, f32[512]{0:T(512)S(1)} %reshape.602, f32[512]{0:T(512)S(1)} %reshape.598, f32[32]{0:T(128)S(1)} %reshape.594, ...), kind=kOutput, calls=%fused_computation.52 | convolution fusion | flops 3310812160 | bytes 14954624 | tf_op jit(solution)/shard_map/yxnd,cd->yxnc/dot_general | solution.py:462
  329.9 9.0 %sums_two.1 = (f32[1,512]{1,0:T(1,128)S(1)}, f32[1,512]{1,0:T(1,128)S(1)}) custom-call(f32[1,512]{1,0:T(1,128)S(1)} %bitcast.192, f32[1,512]{1,0:T(1,128)S(1)} %bitcast.191), custom_call_target="tpu_custom_call" | custom-call | tf_op jit(solution)/shard_map/sums_two/pallas_call | solution.py:404
  339.7 3.0 multiply_convert_fusion.2
  342.8 8.7 %fusion.89 = (bf16[512]{0:T(512)(128)(2,1)S(1)}, bf16[7,7,32,512]{3,2,1,0:T(8,128)(2,1)S(1)}, f32[7,7,32,512]{3,2,1,0:T(8,128)S(1)}) fusion(f32[7,7,32,512]{3,2,1,0:T(8,128)S(1)} %copy-done.17, f32[7,7,32,512]{3,2,1,0:T(8,128)S(1)} %copy-done.9, bf16[7,7,32,512]{3,2,1,0:T(8,128)(2,1)S(1)} %multiply_convert_fusion.2, bf16[3,3,512,512]{3,2,1,0:T(8,128)(2,1)S(1)} %bitcast.220), kind=kOutput, calls=%fused_computation.184 | convolution fusion | flops 6061391360 | bytes 17564672 | tf_op jit(solution)/shard_map/conv_general_dilated | solution.py:439
  351.5 7.7 %fusion.99 = f32[7,7,32,512]{3,2,1,0:T(8,128)S(1)} fusion(bf16[7,7,32,512]{3,2,1,0:T(8,128)(2,1)S(1)} %get-tuple-element.132, bf16[3,3,512,512]{3,2,1,0:T(8,128)(2,1)S(1)} %bitcast.210), kind=kOutput, calls=%fused_computation.192 | convolution fusion | flops 6056574976 | bytes 9535488 | tf_op jit(solution)/shard_map/conv_general_dilated | solution.py:439
  359.3 8.0 %add_multiply_fusion = f32[7,7,32,512]{3,2,1,0:T(8,128)S(1)} fusion(f32[7,7,32,512]{3,2,1,0:T(8,128)S(1)} %fusion.99, bf16[7,7,32,512]{3,2,1,0:T(8,128)(2,1)S(1)} %get-tuple-element.132, bf16[3,3,512,512]{3,2,1,0:T(8,128)(2,1)S(1)} %bitcast.205, f32[32]{0:T(128)S(1)} %mul.678), kind=kOutput, calls=%fused_computation.49 | convolution fusion | flops 4850221056 | bytes 12746880 | tf_op jit(solution)/shard_map/conv_general_dilated | solution.py:439
  368.1 1.1 copy-done.7
  369.2 3.8 multiply_reduce_fusion.4
  373.0 8.9 %sums_one.1 = (f32[1,512]{1,0:T(1,128)S(1)}, f32[1,512]{1,0:T(1,128)S(1)}) custom-call(f32[1,512]{1,0:T(1,128)S(1)} %bitcast.171, f32[1,512]{1,0:T(1,128)S(1)} %bitcast.170), custom_call_target="tpu_custom_call" | custom-call | tf_op jit(solution)/shard_map/sums_one/pallas_call | solution.py:404
  383.5 12.0 %fusion.97 = (bf16[7,7,32,2048]{3,2,1,0:T(8,128)(2,1)}, f32[7,7,32,2048]{3,2,1,0:T(8,128)}) fusion(f32[7,7,32,2048]{3,2,1,0:T(8,128)} %get-tuple-element.129, bf16[7,7,32,512]{3,2,1,0:T(8,128)(2,1)S(1)} %multiply_convert_fusion.1, bf16[2048,512,1,1]{1,0,3,2:T(8,128)(2,1)S(1)} %bitcast.224), kind=kOutput, calls=%fused_computation.190 | convolution fusion | flops 3294756864 | bytes 35815424 | tf_op jit(solution)/shard_map/yxnd,cd->yxnc/dot_general | solution.py:462
  395.6 11.8 %copy.59 = f32[2,16,49,2048]{3,1,2,0:T(8,128)} copy(f32[2,16,49,2048]{3,1,0,2:T(8,128)} %bitcast.196) | data formatting | bytes 25690112
  407.3 10.5 %fusion.100 = bf16[3,3,512,512]{3,2,1,0:T(8,128)(2,1)} fusion(bf16[7,7,32,512]{3,2,1,0:T(8,128)(2,1)S(1)} %fusion.28, bf16[7,7,32,512]{3,2,1,0:T(8,128)(2,1)S(1)} %get-tuple-element.132), kind=kOutput, calls=%fused_computation.193 | convolution fusion | flops 6056574976 | bytes 7929856 | tf_op jit(solution)/shard_map/conv_general_dilated | solution.py:446
  417.8 11.0 %fusion.101 = bf16[3,3,512,512]{3,2,1,0:T(8,128)(2,1)} fusion(bf16[7,7,32,512]{3,2,1,0:T(8,128)(2,1)S(1)} %fusion.28, bf16[7,7,32,512]{3,2,1,0:T(8,128)(2,1)S(1)} %get-tuple-element.132), kind=kOutput, calls=%fused_computation.194 | convolution fusion | flops 4848615424 | bytes 7929856 | tf_op jit(solution)/shard_map/conv_general_dilated | solution.py:446
  428.8 10.5 %fusion.102 = bf16[3,3,512,512]{3,2,1,0:T(8,128)(2,1)} fusion(bf16[7,7,32,512]{3,2,1,0:T(8,128)(2,1)S(1)} %copy-done.45, bf16[7,7,32,512]{3,2,1,0:T(8,128)(2,1)S(1)} %copy-done.11), kind=kOutput, calls=%fused_computation.195 | convolution fusion | flops 6056574976 | bytes 7929856 | tf_op jit(solution)/shard_map/conv_general_dilated | solution.py:446
  439.4 6.5 %fusion.10 = bf16[512,2048,1,1]{1,0,3,2:T(8,128)(2,1)} fusion(bf16[7,7,32,2048]{3,2,1,0:T(8,128)(2,1)S(1)} %bitcast.214, f32[7,7,32,512]{3,2,1,0:T(8,128)S(1)} %copy-done.14, f32[512]{0:T(512)S(1)} %reshape.602, f32[512]{0:T(512)S(1)} %bitcast.251, f32[512]{0:T(512)S(1)} %bitcast.255, f32[512]{0:T(512)S(1)} %reshape.598, f32[32]{0:T(128)S(1)} %reshape.594), kind=kOutput, calls=%fused_computation.20 | convolution fusion | flops 3299573760 | bytes 11739264 | tf_op jit(solution)/shard_map/yxnc,yxnd->cd/dot_general | solution.py:466
  445.9 5.3 fusion.8
  451.4 4.7 fusion.65
  456.2 1.0 multiply_reduce_fusion.10
  457.3 8.9 %sums_stem.1 = (f32[1,128]{1,0:T(1,128)S(1)}, f32[1,128]{1,0:T(1,128)S(1)}) custom-call(f32[1,128]{1,0:T(1,128)S(1)} %pad.44.refs_0_, f32[1,128]{1,0:T(1,128)S(1)} %pad.45.refs_1_), custom_call_target="tpu_custom_call" | custom-call | tf_op jit(solution)/shard_map/sums_stem/pallas_call | solution.py:404
  466.4 2.0 fusion.64
  469.5 4.1 fusion.29
  473.8 1.2 fusion.39.refs_5_
  475.0 101.6 %scatter_terms.1 = (f32[288,512]{1,0:T(8,128)}, f32[288,512]{1,0:T(8,128)}, f32[288,512]{1,0:T(8,128)}, f32[32,2048]{1,0:T(8,128)}, f32[128,512]{1,0:T(8,128)}, /*index=5*/f32[16,2048]{1,0:T(8,128)}) custom-call(bf16[16,288,512]{2,1,0:T(8,128)(2,1)} %bitcast.221, bf16[16,288,512]{2,1,0:T(8,128)(2,1)} %bitcast.206, bf16[16,288,512]{2,1,0:T(8,128)(2,1)} %bitcast.222, ...), custom_call_target="tpu_custom_call" | custom-call | tf_op jit(solution)/shard_map/scatter_terms/pallas_call | solution.py:311
  576.6 1.4 slice.117
  579.2 1.5 slice.118
  581.8 2.3 pad_maximum_fusion
  584.2 1.2 slice_bitcast_fusion
  585.3 1.2 fusion.81
  586.5 1.2 fusion.82
  587.7 1.2 fusion.83
  588.9 1.2 fusion.84
  590.0 1.7 copy.89
  (186 shorter events, 18.0 us)
Async XLA Ops:
  102.2 9.3 %copy-start.33 = (bf16[2,16,5,3,49]{4,1,3,2,0:T(8,128)(2,1)S(1)}, bf16[2,16,5,3,49]{4,1,3,2,0:T(8,128)(2,1)}, u32[]{:S(2)}) copy-start(bf16[2,16,5,3,49]{4,1,3,2,0:T(8,128)(2,1)} %param.19) | copy-start | bytes 141124
  111.4 9.1 %copy-start.42 = (s32[2]{0:T(128)S(1)}, s32[2]{0:T(128)}, u32[]{:S(2)}) copy-start(s32[2]{0:T(128)} %param.21) | copy-start | bytes 28
  112.0 24.1 %copy-start.28 = (bf16[7,7,32,12]{2,3,1,0:T(8,128)(2,1)}, bf16[7,7,32,12]{2,3,1,0:T(8,128)(2,1)S(1)}, u32[]{:S(2)}) copy-start(bf16[7,7,32,12]{2,3,1,0:T(8,128)(2,1)S(1)} %reshape.612) | copy-start | bytes 112900
  119.4 30.5 %copy-start.15 = (f32[7,7,32,64]{3,2,1,0:T(8,128)}, f32[7,7,32,64]{3,2,1,0:T(8,128)S(1)}, u32[]{:S(2)}) copy-start(f32[7,7,32,64]{3,2,1,0:T(8,128)S(1)} %get-tuple-element.144) | copy-start | bytes 1204228
  120.5 15.6 %copy-start.40 = (f32[64]{0:T(128)}, f32[64]{0:T(128)S(1)}, u32[]{:S(2)}) copy-start(f32[64]{0:T(128)S(1)} %reshape.596) | copy-start | bytes 772
  135.4 0.5 copy-start.4
  136.0 13.9 %copy-start.34 = (f32[64]{0:T(128)}, f32[64]{0:T(128)S(1)}, u32[]{:S(2)}) copy-start(f32[64]{0:T(128)S(1)} %get-tuple-element.160) | copy-start | bytes 772
  136.0 13.9 %copy-start.38 = (f32[64]{0:T(128)}, f32[64]{0:T(128)S(1)}, u32[]{:S(2)}) copy-start(f32[64]{0:T(128)S(1)} %get-tuple-element.161) | copy-start | bytes 772
  136.1 13.8 %copy-start.36 = (f32[64]{0:T(128)}, f32[64]{0:T(128)S(1)}, u32[]{:S(2)}) copy-start(f32[64]{0:T(128)S(1)} %reshape.595) | copy-start | bytes 772
  136.8 13.1 %copy-start.22 = (bf16[7,7,32,64]{3,2,1,0:T(8,128)(2,1)}, bf16[7,7,32,64]{3,2,1,0:T(8,128)(2,1)S(1)}, u32[]{:S(2)}) copy-start(bf16[7,7,32,64]{3,2,1,0:T(8,128)(2,1)S(1)} %fusion.37) | copy-start | bytes 602116
  138.1 11.8 %copy-start.26 = (bf16[64,2048,1,1]{1,0,2,3:T(8,128)(2,1)}, bf16[64,2048,1,1]{1,0,2,3:T(8,128)(2,1)S(1)}, u32[]{:S(2)}) copy-start(bf16[64,2048,1,1]{1,0,2,3:T(8,128)(2,1)S(1)} %reshape.605) | copy-start | bytes 786436
  138.2 11.8 %copy-start.24 = (bf16[16,128,512]{2,1,0:T(8,128)(2,1)S(1)}, bf16[16,128,512]{2,1,0:T(8,128)(2,1)}, u32[]{:S(2)}) copy-start(bf16[16,128,512]{2,1,0:T(8,128)(2,1)} %get-tuple-element.52) | copy-start | bytes 6291460
  149.9 5.4 copy-start.20
  189.6 14.5 %copy-start.12 = (bf16[1,16,288,512]{3,2,1,0:T(8,128)(2,1)}, bf16[1,16,288,512]{3,2,1,0:T(8,128)(2,1)S(1)}, u32[]{:S(2)}) copy-start(bf16[1,16,288,512]{3,2,1,0:T(8,128)(2,1)S(1)} %get-tuple-element.133) | copy-start | bytes 14155780
  189.6 14.5 %copy-start.8 = (f32[7,7,32,512]{3,2,1,0:T(8,128)S(1)}, f32[7,7,32,512]{3,2,1,0:T(8,128)}, u32[]{:S(2)}) copy-start(f32[7,7,32,512]{3,2,1,0:T(8,128)} %multiply_multiply_fusion.7) | copy-start | bytes 9633796
  189.6 24.9 %slice-start.8 = ((s8[4718592]{0:T(1024)(128)(4,1)}), s8[4194304]{0:T(1024)(128)(4,1)S(1)}, s32[]{:S(2)}) async-start(s8[4718592]{0:T(1024)(128)(4,1)} %bitcast.215), calls=%async_computation.8 | async-start | bytes 8388608
  204.2 10.3 %slice-start.9 = ((s8[4718592]{0:T(1024)(128)(4,1)}), s8[524288]{0:T(1024)(128)(4,1)S(1)}, s32[]{:S(2)}) async-start(s8[4718592]{0:T(1024)(128)(4,1)} %bitcast.215), calls=%async_computation.9 | async-start | bytes 1048576
  214.5 9.5 %copy-start.44 = (bf16[7,7,32,512]{3,2,1,0:T(8,128)(2,1)}, bf16[7,7,32,512]{3,2,1,0:T(8,128)(2,1)S(1)}, u32[]{:S(2)}) copy-start(bf16[7,7,32,512]{3,2,1,0:T(8,128)(2,1)S(1)} %get-tuple-element.149) | copy-start | bytes 4816900
  243.2 4.6 copy-start.6
  243.3 15.1 %copy-start.31 = (bf16[2,49,2048]{2,0,1:T(2,128)(2,1)S(1)}, bf16[2,49,2048]{2,0,1:T(2,128)(2,1)}, u32[]{:S(2)}) copy-start(bf16[2,49,2048]{2,0,1:T(2,128)(2,1)} %param.37) | copy-start | bytes 1204228
  309.8 0.6 copy-start
  309.8 0.7 copy-start.1
  310.5 11.2 %copy-start.13 = (f32[7,7,32,512]{3,2,1,0:T(8,128)S(1)}, f32[7,7,32,512]{3,2,1,0:T(8,128)}, u32[]{:S(2)}) copy-start(f32[7,7,32,512]{3,2,1,0:T(8,128)} %get-tuple-element.152) | copy-start | bytes 9633796
  310.6 11.2 %copy-start.43 = (bf16[16,32,2048]{2,1,0:T(8,128)(2,1)S(1)}, bf16[16,32,2048]{2,1,0:T(8,128)(2,1)}, u32[]{:S(2)}) copy-start(bf16[16,32,2048]{2,1,0:T(8,128)(2,1)} %get-tuple-element.61) | copy-start | bytes 6291460
  310.6 32.2 %slice-start.10 = ((s8[4718592]{0:T(1024)(128)(4,1)}), s8[4194304]{0:T(1024)(128)(4,1)S(1)}, s32[]{:S(2)}) async-start(s8[4718592]{0:T(1024)(128)(4,1)} %bitcast.218), calls=%async_computation.10 | async-start | bytes 8388608
  321.8 8.2 %copy-start.21 = (bf16[7,7,32,2048]{3,2,1,0:T(8,128)(2,1)}, bf16[7,7,32,2048]{3,2,1,0:T(8,128)(2,1)S(1)}, u32[]{:S(2)}) copy-start(bf16[7,7,32,2048]{3,2,1,0:T(8,128)(2,1)S(1)} %multiply_convert_fusion) | copy-start | bytes 19267588
  321.8 21.0 %copy-start.17 = (f32[7,7,32,512]{3,2,1,0:T(8,128)S(1)}, f32[7,7,32,512]{3,2,1,0:T(8,128)}, u32[]{:S(2)}) copy-start(f32[7,7,32,512]{3,2,1,0:T(8,128)} %get-tuple-element.150) | copy-start | bytes 9633796
  321.8 21.0 %slice-start.11 = ((s8[4718592]{0:T(1024)(128)(4,1)}), s8[524288]{0:T(1024)(128)(4,1)S(1)}, s32[]{:S(2)}) async-start(s8[4718592]{0:T(1024)(128)(4,1)} %bitcast.218), calls=%async_computation.11 | async-start | bytes 1048576
  339.0 0.6 copy-start.3
  339.0 0.7 copy-start.2
  339.7 3.1 copy-start.9
  339.7 11.8 %slice-start.2 = ((s8[4718592]{0:T(1024)(128)(4,1)}), s8[4194304]{0:T(1024)(128)(4,1)S(1)}, s32[]{:S(2)}) async-start(s8[4718592]{0:T(1024)(128)(4,1)} %bitcast.208), calls=%async_computation.2 | async-start | bytes 8388608
  342.8 8.7 %copy-start.10 = (bf16[7,7,32,512]{3,2,1,0:T(8,128)(2,1)}, bf16[7,7,32,512]{3,2,1,0:T(8,128)(2,1)S(1)}, u32[]{:S(2)}) copy-start(bf16[7,7,32,512]{3,2,1,0:T(8,128)(2,1)S(1)} %multiply_convert_fusion.2) | copy-start | bytes 4816900
  342.8 8.7 %slice-start.3 = ((s8[4718592]{0:T(1024)(128)(4,1)}), s8[524288]{0:T(1024)(128)(4,1)S(1)}, s32[]{:S(2)}) async-start(s8[4718592]{0:T(1024)(128)(4,1)} %bitcast.208), calls=%async_computation.3 | async-start | bytes 1048576
  342.8 16.4 %slice-start = ((s8[4718592]{0:T(1024)(128)(4,1)}), s8[524288]{0:T(1024)(128)(4,1)S(1)}, s32[]{:S(2)}) async-start(s8[4718592]{0:T(1024)(128)(4,1)} %bitcast.203), calls=%async_computation | async-start | bytes 1048576
  351.5 7.7 %slice-start.1 = ((s8[4718592]{0:T(1024)(128)(4,1)}), s8[4194304]{0:T(1024)(128)(4,1)S(1)}, s32[]{:S(2)}) async-start(s8[4718592]{0:T(1024)(128)(4,1)} %bitcast.203), calls=%async_computation.1 | async-start | bytes 8388608
  367.3 1.9 copy-start.7
  382.0 1.6 copy-start.25
  383.5 12.0 %copy-start.18 = (bf16[7,7,32,512]{3,2,1,0:T(8,128)(2,1)}, bf16[7,7,32,512]{3,2,1,0:T(8,128)(2,1)S(1)}, u32[]{:S(2)}) copy-start(bf16[7,7,32,512]{3,2,1,0:T(8,128)(2,1)S(1)} %multiply_convert_fusion.1) | copy-start | bytes 4816900
  417.8 11.0 %copy-start.11 = (bf16[7,7,32,512]{3,2,1,0:T(8,128)(2,1)S(1)}, bf16[7,7,32,512]{3,2,1,0:T(8,128)(2,1)}, u32[]{:S(2)}) copy-start(bf16[7,7,32,512]{3,2,1,0:T(8,128)(2,1)} %copy-done.10) | copy-start | bytes 4816900
  417.8 11.0 %copy-start.45 = (bf16[7,7,32,512]{3,2,1,0:T(8,128)(2,1)S(1)}, bf16[7,7,32,512]{3,2,1,0:T(8,128)(2,1)}, u32[]{:S(2)}) copy-start(bf16[7,7,32,512]{3,2,1,0:T(8,128)(2,1)} %copy-done.44) | copy-start | bytes 4816900
  417.8 21.6 %slice-start.6 = ((s8[6422528]{0:T(1024)(128)(4,1)}), s8[4194304]{0:T(1024)(128)(4,1)S(1)}, s32[]{:S(2)}) async-start(s8[6422528]{0:T(1024)(128)(4,1)} %bitcast.213), calls=%async_computation.6 | async-start | bytes 8388608
  428.8 10.5 %copy-start.14 = (f32[7,7,32,512]{3,2,1,0:T(8,128)S(1)}, f32[7,7,32,512]{3,2,1,0:T(8,128)}, u32[]{:S(2)}) copy-start(f32[7,7,32,512]{3,2,1,0:T(8,128)} %get-tuple-element.152) | copy-start | bytes 9633796
  428.8 10.5 %slice-start.7 = ((s8[6422528]{0:T(1024)(128)(4,1)}), s8[2228224]{0:T(1024)(128)(4,1)S(1)}, s32[]{:S(2)}) async-start(s8[6422528]{0:T(1024)(128)(4,1)} %bitcast.213), calls=%async_computation.7 | async-start | bytes 4456448
  428.8 17.1 %slice-start.4 = ((s8[6422528]{0:T(1024)(128)(4,1)}), s8[4194304]{0:T(1024)(128)(4,1)S(1)}, s32[]{:S(2)}) async-start(s8[6422528]{0:T(1024)(128)(4,1)} %bitcast.211), calls=%async_computation.4 | async-start | bytes 8388608
  439.4 6.5 %copy-start.19 = (bf16[7,7,32,512]{3,2,1,0:T(8,128)(2,1)S(1)}, bf16[7,7,32,512]{3,2,1,0:T(8,128)(2,1)}, u32[]{:S(2)}) copy-start(bf16[7,7,32,512]{3,2,1,0:T(8,128)(2,1)} %copy-done.18) | copy-start | bytes 4816900
  439.4 6.5 %slice-start.5 = ((s8[6422528]{0:T(1024)(128)(4,1)}), s8[2228224]{0:T(1024)(128)(4,1)S(1)}, s32[]{:S(2)}) async-start(s8[6422528]{0:T(1024)(128)(4,1)} %bitcast.211), calls=%async_computation.5 | async-start | bytes 4456448
  445.9 5.4 copy-start.27
  451.4 4.8 copy-start.16
  451.4 4.8 copy-start.35
  451.4 4.8 copy-start.37
  451.4 4.8 copy-start.39
  451.4 4.8 copy-start.41
  451.4 14.8 %copy-start.5 = (f32[1,128]{1,0:T(1,128)S(1)}, f32[1,128]{1,0:T(1,128)}, u32[]{:S(2)}) copy-start(f32[1,128]{1,0:T(1,128)} %copy-done.4) | copy-start | bytes 1540
  451.4 15.0 %copy-start.29 = (bf16[7,7,32,12]{2,3,1,0:T(8,128)(2,1)S(1)}, bf16[7,7,32,12]{2,3,1,0:T(8,128)(2,1)}, u32[]{:S(2)}) copy-start(bf16[7,7,32,12]{2,3,1,0:T(8,128)(2,1)} %copy-done.28) | copy-start | bytes 112900
  457.2 12.3 %copy-start.23 = (bf16[7,7,32,64]{3,2,1,0:T(8,128)(2,1)S(1)}, bf16[7,7,32,64]{3,2,1,0:T(8,128)(2,1)}, u32[]{:S(2)}) copy-start(bf16[7,7,32,64]{3,2,1,0:T(8,128)(2,1)} %copy-done.22) | copy-start | bytes 602116
  576.6 15.1 %copy-start.30 = (f32[288,512]{1,0:T(8,128)S(1)}, f32[288,512]{1,0:T(8,128)}, u32[]{:S(2)}) copy-start(f32[288,512]{1,0:T(8,128)} %get-tuple-element.190) | copy-start | bytes 1769476
  576.6 15.9 %copy-start.32 = (f32[32,2048]{1,0:T(8,128)S(1)}, f32[32,2048]{1,0:T(8,128)}, u32[]{:S(2)}) copy-start(f32[32,2048]{1,0:T(8,128)} %get-tuple-element.193) | copy-start | bytes 786436
where the time goes:
time: 603 us; the launch traced here: 593 us
  Pallas kernels  273 us (45%)
  matrix products  164 us (27%)
  other arithmetic  82.8 us (14%)
  local copies, waits for them, and re-layouts  71.8 us (12%)
    pallas_call x1, Pallas kernels, scatter_all(): pl.pallas_call(functools.partial(scatter_kernel, dims, reps, stacked), ou...  102 us
    pallas_call x1, Pallas kernels, gather_all(): pl.pallas_call(functools.partial(gather_kernel, dims, reps, stacked), out...  93.2 us
    pallas_call x8, Pallas kernels, exchange(): pl.pallas_call(functools.partial(exchange_kernel, sizes, reps, moments, p...  77.8 us
    conv_general_dilated x4, matrix products, convolve(): lax.conv_general_dilated(source, kernel, (1, 1), pad_of(span * stride), r...  40 us
    conv_general_dilated x3, matrix products, convolve_terms(): lax.conv_general_dilated(source, grads, (stride, stride), pad_of(span * s...  32 us
    reduce_sum x2, other arithmetic, norm_back(): jnp.sum(masked * normed, axis=(0, 1, 2))  29.5 us
    dot_general x3, matrix products, project_back(): jnp.einsum('yxnd,cd->yxnc', grads, weight, preferred_element_type=f32)  24.9 us
    dot_general x3, matrix products, project(): jnp.einsum('yxnc,cd->yxnd', source, weight, preferred_element_type=f32)  24.4 us

commit v1 on v0

--- a/solution.py
+++ b/solution.py
@@ -345,52 +345,80 @@
     return sizes
 
 
-def exchange_kernel(sizes, reps, moments, width, *refs):
+class Exchange:
+    def __init__(self, sizes, reps, buffers):
+        self.sizes, self.reps = sizes, reps
+        self.mine, self.slots, self.sems = buffers[0], buffers[1:-1], buffers[-1]
+        place = lax.axis_index("fsdp") * reps + lax.axis_index("rep")
+        self.stages = []
+        stride = 1
+        for size in sizes:
+            position = (place // stride) % size
+            peers = []
+            for d in range(1, size):
+                target = place + ((position + d) % size - position) * stride
+                peers.append((target // reps, target % reps))
+            self.stages.append((size, position, peers))
+            stride *= size
+        self.peers = [peer for stage in self.stages for peer in stage[2]]
+        self.waits = []
+
+    def total(self, round, current, moments):
+        number = len(current)
+        spans, start = [], 0
+        for value in current:
+            spans.append((start, value.shape[1]))
+            start += value.shape[1]
+        for index, (size, position, peers) in enumerate(self.stages):
+            used = pl.ds(0, sum(length for _, length in spans))
+            mine = self.mine.at[round, index, :, used]
+            slots = self.slots[index].at[round, :, :, used]
+            for (start, length), value in zip(spans, current):
+                mine[:, start : start + length] = value
+            for d, (target, rep) in enumerate(peers, 1):
+                copy = remote(mine, slots.at[position], self.sems.at[round, index, d - 1], target, rep)
+                copy.start()
+                self.waits.append(copy)
+            slots[position] = mine[...]
+            for d, (target, rep) in enumerate(peers, 1):
+                there = slots.at[(position + size - d) % size]
+                remote(there, there, self.sems.at[round, index, d - 1], target, rep).wait_recv()
+            parts = [
+                [slots[j, :, start : start + length] for start, length in spans] for j in range(size)
+            ]
+            current = [functools.reduce(jnp.add, [part[row] for part in parts]) for row in range(number)]
+            if moments:
+                centre = current[0] / current[2][:, :1]
+                squares = current[1]
+                for part in parts:
+                    count = part[2][:, :1]
+                    off = part[0] / count - centre
+                    squares = squares + count * off * off
+                current[1] = squares
+        return current
+
+    def finish(self):
+        for copy in self.waits:
+            copy.wait_send()
+
+
+def exchange_buffers(sizes, rounds, total):
+    return (
+        [pltpu.VMEM((rounds, len(sizes), 1, total), f32)]
+        + [pltpu.VMEM((rounds, size, 1, total), f32) for size in sizes]
+        + [DMA((rounds, len(sizes), max(max(sizes) - 1, 1), 2))]
+    )
+
+
+def exchange_kernel(sizes, reps, moments, *refs):
     number = 3 if moments else 2
     sources, results = refs[:number], refs[number : 2 * number]
-    mine, slots, sems = refs[2 * number], refs[2 * number + 1 : -1], refs[-1]
-    place = lax.axis_index("fsdp") * reps + lax.axis_index("rep")
-    stages = []
-    stride = 1
-    for size in sizes:
-        position = (place // stride) % size
-        peers = []
-        for d in range(1, size):
-            target = place + ((position + d) % size - position) * stride
-            peers.append((target // reps, target % reps))
-        stages.append((size, position, peers))
-        stride *= size
-    greet([peer for stage in stages for peer in stage[2]])
-    spans = [(0, width), (width, width), (2 * width, LANES)][:number]
-    current = [source[...] for source in sources]
-    waits = []
-    for index, (size, position, peers) in enumerate(stages):
-        for (start, length), value in zip(spans, current):
-            mine[index, :, start : start + length] = value
-        for d, (target, rep) in enumerate(peers, 1):
-            copy = remote(mine.at[index], slots[index].at[position], sems.at[index, d - 1], target, rep)
-            copy.start()
-            waits.append(copy)
-        slots[index][position] = mine[index]
-        for d, (target, rep) in enumerate(peers, 1):
-            there = slots[index].at[(position + size - d) % size]
-            remote(there, there, sems.at[index, d - 1], target, rep).wait_recv()
-        parts = [
-            [slots[index][j, :, start : start + length] for start, length in spans] for j in range(size)
-        ]
-        current = [functools.reduce(jnp.add, [part[row] for part in parts]) for row in range(number)]
-        if moments:
-            centre = current[0] / current[2][:, :1]
-            squares = current[1]
-            for part in parts:
-                count = part[2][:, :1]
-                off = part[0] / count - centre
-                squares = squares + count * off * off
-            current[1] = squares
+    over = Exchange(sizes, reps, refs[2 * number :])
+    greet(over.peers)
+    current = over.total(0, [source[...] for source in sources], moments)
     for result, value in zip(results, current):
         result[...] = value
-    for copy in waits:
-        copy.wait_send()
+    over.finish()
 
 
 def exchange(rows, fsdp, reps, moments, collective_id, name):
@@ -400,21 +428,473 @@
     rows = [jnp.pad(row.reshape(1, -1), ((0, 0), (0, padded - width))) for row in rows[:2]] + [
         jnp.broadcast_to(row.reshape(1, 1), (1, LANES)) for row in rows[2:]
     ]
-    total = sum(row.shape[1] for row in rows)
     results = pl.pallas_call(
-        functools.partial(exchange_kernel, sizes, reps, moments, padded),
+        functools.partial(exchange_kernel, sizes, reps, moments),
         out_shape=[jax.ShapeDtypeStruct(row.shape, f32) for row in rows],
         in_specs=[IN_VMEM] * len(rows),
         out_specs=[IN_VMEM] * len(rows),
-        scratch_shapes=[pltpu.VMEM((len(sizes), 1, total), f32)]
-        + [pltpu.VMEM((size, 1, total), f32) for size in sizes]
-        + [DMA((len(sizes), max(max(sizes) - 1, 1), 2))],
+        scratch_shapes=exchange_buffers(sizes, 1, sum(row.shape[1] for row in rows)),
         compiler_params=pltpu.CompilerParams(
             collective_id=collective_id, has_side_effects=True, vmem_limit_bytes=4 * 1024 * 1024
         ),
         name=name,
     )(*rows)
     return [result[0, :width] for result in results[:2]] + [result[0, 0] for result in results[2:]]
+
+
+def dot(left, right):
+    return jnp.dot(left, right, preferred_element_type=f32)
+
+
+def dot_t(left, right):
+    return lax.dot_general(left, right, (((1,), (1,)), ((), ())), preferred_element_type=f32)
+
+
+class Scatter:
+    def __init__(self, dims, reps, terms, rows, buffers):
+        count = len(terms)
+        self.dims, self.reps, self.terms, self.rows = dims, reps, terms, rows
+        self.from_rep, self.from_v, self.from_u, self.from_a, self.share = (
+            buffers[i * count : (i + 1) * count] for i in range(5)
+        )
+        self.r_sem, self.v_sem, self.u_sem, self.a_sem, self.s_sem = buffers[5 * count :]
+        self.place = Place(dims, reps)
+        self.waits = []
+
+    def push(self, source, there, sems, target, target_rep):
+        copy = remote(source, there, sems, target, target_rep)
+        copy.start()
+        self.waits.append(copy)
+
+    def landed(self, there, sems):
+        remote(there, there, sems, self.place.me, self.place.rep).wait_recv()
+
+    def part(self, k, index, which):
+        rows = self.rows[k]
+        start = pl.multiple_of(index * rows, rows)
+        return self.terms[k].at[pl.ds(start, rows), columns(self.terms[k].shape[1] // self.reps, which)]
+
+    def order(self):
+        size_a, size_b, size_c = self.dims
+        for dv in list(range(1, size_c)) + [0]:
+            for du in list(range(1, size_b)) + [0]:
+                for da in list(range(1, size_a)) + [0]:
+                    yield da, du, dv
+
+    def cores(self, k):
+        place = self.place
+        for da, du, dv in self.order():
+            for d in range(1, self.reps):
+                other = (place.rep + d) % self.reps
+                index = Place(self.dims, self.reps, other).at(da, du, dv)
+                self.push(
+                    self.part(k, index, other), self.from_rep[k].at[d - 1, index],
+                    self.r_sem.at[k, da, du, dv, d - 1], place.me, other,
+                )
+
+    def hop(self, k, lag):
+        if 0 <= k < len(self.terms):
+            for da, du, dv in self.order():
+                if lag == (0 if dv else 1 if du else 2 if da else 3):
+                    self.handle(k, da, du, dv)
+
+    def handle(self, k, da, du, dv):
+        size_a, size_b, size_c = self.dims
+        place, reps, rep = self.place, self.reps, self.place.rep
+        index = place.at(da, du, dv)
+        mine = self.part(k, index, rep)
+        total = mine[...].astype(f32)
+        for d in range(1, reps):
+            self.landed(self.from_rep[k].at[d - 1, index], self.r_sem.at[k, da, du, dv, d - 1])
+            total = total + self.from_rep[k][d - 1, index].astype(f32)
+        if dv == 0:
+            for e in range(1, size_c):
+                self.landed(self.from_v[k].at[e - 1, da, du], self.v_sem.at[k, da, du, e - 1])
+                total = total + self.from_v[k][e - 1, da, du].astype(f32)
+            if du == 0:
+                for e in range(1, size_b):
+                    self.landed(self.from_u[k].at[e - 1, da], self.u_sem.at[k, da, e - 1])
+                    total = total + self.from_u[k][e - 1, da].astype(f32)
+                if da == 0:
+                    for e in range(1, size_a):
+                        self.landed(self.from_a[k].at[e - 1], self.a_sem.at[k, e - 1])
+                        total = total + self.from_a[k][e - 1].astype(f32)
+        if (da, du, dv) == (0, 0, 0):
+            self.share[k][rep] = total.astype(bf16)
+            for d in range(1, reps):
+                self.push(self.share[k].at[rep], self.share[k].at[rep], self.s_sem.at[k, d - 1], place.me, (rep + d) % reps)
+            return
+        mine[...] = total.astype(bf16)
+        if dv:
+            self.push(mine, self.from_v[k].at[dv - 1, da, du], self.v_sem.at[k, da, du, dv - 1], place.at(0, 0, dv), rep)
+        elif du:
+            self.push(mine, self.from_u[k].at[du - 1, da], self.u_sem.at[k, da, du - 1], place.at(0, du, 0), rep)
+        else:
+            self.push(mine, self.from_a[k].at[da - 1], self.a_sem.at[k, da - 1], place.at(da, 0, 0), rep)
+
+    def finish(self, totals):
+        for k, total in enumerate(totals):
+            width = self.terms[k].shape[1] // self.reps
+            for d in range(1, self.reps):
+                self.landed(self.share[k].at[(self.place.rep + self.reps - d) % self.reps], self.s_sem.at[k, d - 1])
+            for which in range(self.reps):
+                total[:, which * width : (which + 1) * width] = self.share[k][which].astype(f32)
+        for copy in self.waits:
+            copy.wait_send()
+
+
+def scatter_buffers(dims, reps, shapes):
+    size_a, size_b, size_c = dims
+    count = len(shapes)
+    others = max(reps - 1, 1)
+
+    def buffers(*lead):
+        return [pltpu.VMEM(lead + (rows, width // reps), bf16) for rows, width in shapes]
+
+    return (
+        buffers(others, size_a * size_b * size_c)
+        + buffers(max(size_c - 1, 1), size_a, size_b)
+        + buffers(max(size_b - 1, 1), size_a)
+        + buffers(max(size_a - 1, 1))
+        + buffers(reps)
+        + [
+            DMA((count, size_a, size_b, size_c, others, 2)),
+            DMA((count, size_a, size_b, max(size_c - 1, 1), 2)),
+            DMA((count, size_a, max(size_b - 1, 1), 2)),
+            DMA((count, max(size_a - 1, 1), 2)),
+            DMA((count, others, 2)),
+        ]
+    )
+
+
+def terms_kernel(dims, reps, rows, *refs):
+    (small, block_low, grad_reduced, act_two, grad_expanded, modulated, grad_middle, change, grad_gate) = refs[:9]
+    totals = refs[9:15]
+    terms = refs[15:21]
+    pads, line, turned, chunk, pad_sem, line_sem, chunk_sem, small_sem = refs[21:29]
+    scatter = Scatter(dims, reps, terms, rows, refs[29:])
+    slots, mid_width = modulated.shape[2:]
+    lines = block_low.shape[0]
+    width = block_low.shape[2]
+    step = chunk.shape[-1]
+    chunks = width // step
+    ring = 2
+
+    place = scatter.place
+    small_copy = pltpu.make_async_copy(small, terms[0], small_sem)
+    small_copy.start()
+    sources = [(block_low, j) for j in range(chunks)] + [(grad_expanded, j) for j in range(chunks)]
+
+    def load(number):
+        source, j = sources[number]
+        return pltpu.make_async_copy(
+            source.at[:, :, j * step : (j + 1) * step], chunk.at[number % 2], chunk_sem.at[number % 2]
+        )
+
+    gradients = [grad_reduced, act_two, grad_middle, grad_gate]
+
+    def turn(number):
+        pltpu.make_async_copy(gradients[number], line, line_sem).wait()
+        turned[...] = jnp.transpose(line[...].reshape(-1, mid_width))
+        if number + 1 < len(gradients):
+            pltpu.make_async_copy(gradients[number + 1], line, line_sem).start()
+
+    load(0).start()
+    pltpu.make_async_copy(gradients[0], line, line_sem).start()
+    inner = pl.ds(ring, GRID)
+    for index, source in enumerate((modulated, change)):
+        for side in (slice(0, ring), slice(GRID + ring, GRID + 2 * ring)):
+            pads[index, side] = jnp.zeros((ring, GRID + 2 * ring, slots, mid_width), bf16)
+            pads[index, ring : GRID + ring, side] = jnp.zeros((GRID, ring, slots, mid_width), bf16)
+        pltpu.make_async_copy(source, pads.at[index, inner, inner], pad_sem.at[index]).start()
+    place.greet()
+
+    small_copy.wait()
+    scatter.cores(0)
+    turn(0)
+    for j in range(chunks):
+        if j + 1 < len(sources):
+            load(j + 1).start()
+        load(j).wait()
+        values = dot(turned[...], chunk[j % 2].reshape(-1, step))
+        terms[1][j * step : (j + 1) * step, :] = jnp.transpose(values).astype(bf16)
+    scatter.cores(1)
+    scatter.hop(0, 0)
+    turn(1)
+    for j in range(chunks):
+        number = chunks + j
+        if number + 1 < len(sources):
+            load(number + 1).start()
+        load(number).wait()
+        terms[2][:, j * step : (j + 1) * step] = dot(turned[...], chunk[number % 2].reshape(-1, step)).astype(bf16)
+    scatter.cores(2)
+    scatter.hop(1, 0)
+    scatter.hop(0, 1)
+
+    def taps(k, pad, stride):
+        def tap(t, _):
+            top = ring + (t // 3 - 1) * stride
+            left = ring + (t % 3 - 1) * stride
+            source = pads[pad, pl.ds(top, GRID), pl.ds(left, GRID)].reshape(-1, mid_width)
+            values = dot(turned[...], source)
+            start = pl.multiple_of(t * mid_width, mid_width)
+            terms[k][pl.ds(start, mid_width), :] = jnp.transpose(values).astype(bf16)
+            return 0
+
+        lax.fori_loop(0, 9, tap, 0)
+        scatter.cores(k)
+
+    for k, pad, stride in ((3, 0, 1), (4, 1, 1), (5, 1, 2)):
+        if k < 5:
+            turn(k - 1)
+            pltpu.make_async_copy((modulated, change)[pad], pads.at[pad, inner, inner], pad_sem.at[pad]).wait()
+        taps(k, pad, stride)
+        for lag in range(4):
+            scatter.hop(k - 1 - lag, lag)
+    for k in range(6, 10):
+        for lag in range(4):
+            scatter.hop(k - 1 - lag, lag)
+    scatter.finish(totals)
+
+
+def terms_all(small, block_low, grad_reduced, act_two, grad_expanded, modulated, grad_middle, change, grad_gate, rows, fsdp, reps, collective_id):
+    dims = factor_three(fsdp)
+    lines, line_rows, width = block_low.shape
+    mid_width = act_two.shape[-1]
+    slots = modulated.shape[2]
+    shapes = [(rows[0], width), (rows[1], mid_width), (rows[2], width)] + [(rows[3], mid_width)] * 3
+    rows = [rows[0], rows[1], rows[2], rows[3], rows[3], rows[3]]
+    side = GRID + 4
+    return pl.pallas_call(
+        functools.partial(terms_kernel, dims, reps, rows),
+        out_shape=[jax.ShapeDtypeStruct(shape, f32) for shape in shapes],
+        in_specs=[ANY] * 9,
+        out_specs=[IN_VMEM] * 6,
+        scratch_shapes=[pltpu.VMEM((fsdp * a, b), bf16) for a, b in shapes]
+        + [
+            pltpu.VMEM((2, side, side, slots, mid_width), bf16),
+            pltpu.VMEM((lines, line_rows, mid_width), bf16),
+            pltpu.VMEM((mid_width, lines * line_rows), bf16),
+            pltpu.VMEM((2, lines, line_rows, 256), bf16),
+            DMA((2,)), DMA(()), DMA((2,)), DMA(()),
+        ]
+        + scatter_buffers(dims, reps, shapes),
+        compiler_params=pltpu.CompilerParams(
+            collective_id=collective_id, has_side_effects=True, vmem_limit_bytes=VMEM_LIMIT
+        ),
+        name="terms",
+    )(small, block_low, grad_reduced, act_two, grad_expanded, modulated, grad_middle, change, grad_gate)
+
+
+TANH_SCALE = 0.7978845608028654
+CUBIC = 0.044715
+
+
+def gelu_parts(x):
+    square = x * x
+    bend = jnp.tanh(TANH_SCALE * x * (1.0 + CUBIC * square))
+    half = 0.5 * (1.0 + bend)
+    slope = half + 0.5 * x * (1.0 - bend * bend) * (TANH_SCALE * (1.0 + 3.0 * CUBIC * square))
+    return x * half, slope
+
+
+def fold_rows(values):
+    groups, slots, width = values.shape
+    return jnp.sum(values.reshape(groups * slots // 8, 8, width), axis=0)
+
+
+def whole_row(values):
+    return jnp.sum(values, axis=0, keepdims=True)
+
+
+def tail_kernel(sizes, reps, clip_count, *refs):
+    (middle, expand, valid, spread, count, gain_two, shift_two, gain_three, shift_three, pooled_grad, block_in) = refs[:11]
+    (pooled, grad_pre, grad_expanded, act_two, grad_middle, gain_three_sum, shift_three_sum, gain_two_sum, shift_two_sum) = refs[11:20]
+    (wide, wide_grad, narrow, narrow_grad, block, low, totals, first, block_sem, pre_sem, low_sem) = refs[20:31]
+    over = Exchange(sizes, reps, refs[31:])
+    lines, rows, mid_width = middle.shape
+    width = expand.shape[1]
+    slots = valid.shape[0]
+    segs = slots // clip_count
+    groups = rows // slots
+    step = 256
+    chunks = width // step
+
+    barrier = pltpu.get_barrier_semaphore()
+    for target, rep in over.peers:
+        pl.semaphore_signal(barrier, inc=1, device_id={"fsdp": target, "rep": rep}, device_id_type=MESH)
+
+    def fetch(y, slot):
+        return pltpu.make_async_copy(block_in.at[y], block.at[slot], block_sem.at[slot])
+
+    fetch(0, 0).start()
+    mask = valid[:, :1].reshape(1, slots, 1)
+    own = count[:, :1]
+
+    def grouped(values):
+        return values.reshape(groups, slots, values.shape[-1])
+
+    def moments(carry, origin):
+        away, squares = whole_row(carry[0]), whole_row(carry[1])
+        return away + own * origin, jnp.maximum(squares - away * away / own, 0.0)
+
+    def gather_moments(carry, values, origin):
+        off = (grouped(values) - origin.reshape(1, 1, -1)) * mask
+        return carry[0] + fold_rows(off), carry[1] + fold_rows(off * off)
+
+    def blank(n):
+        return jnp.zeros((8, n), f32), jnp.zeros((8, n), f32)
+
+    origin = middle[0, 0:1, :]
+    carry = lax.fori_loop(0, lines, lambda y, c: gather_moments(c, middle[y], origin), blank(mid_width))
+    pl.semaphore_wait(barrier, len(over.peers))
+    total, squares, number = over.total(0, list(moments(carry, origin)) + [count[...]], True)
+    number = number[:, :1]
+    centre_two, inverse_two = total / number, lax.rsqrt(squares / number + epsilon)
+    gain2, shift2 = gain_two[...], shift_two[...]
+
+    def zeta_two(normed):
+        return mask * (grouped(normed) * gain2.reshape(1, 1, -1) + shift2.reshape(1, 1, -1))
+
+    def forward_two(y, _):
+        normed = (middle[y] - centre_two) * inverse_two
+        narrow[y] = normed
+        act_two[y] = gelu_parts(zeta_two(normed))[0].astype(bf16).reshape(rows, mid_width)
+        return 0
+
+    lax.fori_loop(0, lines, forward_two, 0)
+
+    def expand_chunk(j, _):
+        cols = pl.ds(pl.multiple_of(j * step, step), step)
+        weight = expand[:, cols]
+        origin = dot(act_two[0, 0:16, :], weight)[0:1]
+
+        def line(y, carry):
+            values = dot(act_two[y], weight)
+            wide[y, :, cols] = values
+            return gather_moments(carry, values, origin)
+
+        total, squares = moments(lax.fori_loop(0, lines, line, blank(step)), origin)
+        totals[0, :, cols] = total
+        totals[1, :, cols] = squares
+        return 0
+
+    lax.fori_loop(0, chunks, expand_chunk, 0)
+    total, squares, _ = over.total(1, [totals[0], totals[1], count[...]], True)
+    totals[0] = total / number
+    totals[1] = lax.rsqrt(squares / number + epsilon)
+    for index in range(2):
+        first[index] = jnp.zeros((8, width), f32)
+
+    def out_pre(y):
+        return pltpu.make_async_copy(wide_grad.at[y], grad_pre.at[y], pre_sem.at[y])
+
+    def forward_three(y, _):
+        slot = y % 2
+        fetch(y, slot).wait()
+
+        @pl.when(y + 1 < lines)
+        def _():
+            fetch(y + 1, 1 - slot).start()
+
+        def chunk(j, _):
+            cols = pl.ds(pl.multiple_of(j * step, step), step)
+            normed = (wide[y, :, cols] - totals[0, :, cols]) * totals[1, :, cols]
+            wide[y, :, cols] = normed
+            normed = grouped(normed)
+            scaled = mask * (gain_three[:, cols].reshape(1, 1, step) * normed + shift_three[:, cols].reshape(1, 1, step))
+            out, slope = gelu_parts(grouped(block[slot, :, cols]) + scaled)
+            grads = []
+            for clip in range(clip_count):
+                span = slice(clip * segs, (clip + 1) * segs)
+                share = spread[span, :1].reshape(1, segs, 1)
+                pixels = pl.ds(y * groups, groups)
+                pooled[clip, pixels, :, cols] = jnp.sum(out[:, span] * share, axis=1, keepdims=True)
+                grads.append(slope[:, span] * (pooled_grad[clip, pixels, :, cols] * share))
+            grad = jnp.concatenate(grads, axis=1)
+            wide_grad[y, :, cols] = grad.reshape(rows, step)
+            first[0, :, cols] += fold_rows(grad)
+            first[1, :, cols] += fold_rows(grad * normed)
+            return 0
+
+        lax.fori_loop(0, chunks, chunk, 0)
+        out_pre(y).start()
+        return 0
+
+    lax.fori_loop(0, lines, forward_three, 0)
+    shift_sum, gain_sum = over.total(2, [whole_row(first[0]), whole_row(first[1])], False)
+    shift_three_sum[...] = shift_sum
+    gain_three_sum[...] = gain_sum
+    totals[2] = shift_sum / number
+    totals[3] = gain_sum / number
+    totals[1] = totals[1] * gain_three[...]
+
+    def out_low(y):
+        return pltpu.make_async_copy(low.at[y % 2], grad_expanded.at[y], low_sem.at[y % 2])
+
+    def back_three(y, carry):
+        slot = y % 2
+
+        @pl.when(y >= 2)
+        def _():
+            out_low(y - 2).wait()
+
+        def chunk(j, _):
+            cols = pl.ds(pl.multiple_of(j * step, step), step)
+            grad = wide_grad[y, :, cols] - totals[2, :, cols] - wide[y, :, cols] * totals[3, :, cols]
+            low[slot, :, cols] = (mask * grouped(grad * totals[1, :, cols])).astype(bf16).reshape(rows, step)
+            return 0
+
+        lax.fori_loop(0, chunks, chunk, 0)
+        out_low(y).start()
+        normed = narrow[y]
+        grad = grouped(dot_t(low[slot], expand[...])) * gelu_parts(zeta_two(normed))[1] * mask
+        narrow_grad[y] = grad.reshape(rows, mid_width)
+        return carry[0] + fold_rows(grad), carry[1] + fold_rows(grad * grouped(normed))
+
+    carry = lax.fori_loop(0, lines, back_three, blank(mid_width))
+    shift_sum, gain_sum = over.total(3, [whole_row(carry[0]), whole_row(carry[1])], False)
+    shift_two_sum[...] = shift_sum
+    gain_two_sum[...] = gain_sum
+    shift_mean, gain_mean, scale = shift_sum / number, gain_sum / number, inverse_two * gain2
+
+    def back_two(y, _):
+        grad = (narrow_grad[y] - shift_mean - narrow[y] * gain_mean) * scale
+        grad_middle[y] = (mask * grouped(grad)).astype(bf16).reshape(rows, mid_width)
+        return 0
+
+    lax.fori_loop(0, lines, back_two, 0)
+    lax.fori_loop(0, lines, lambda y, _: (out_pre(y).wait(), 0)[1], 0)
+    for y in (lines - 2, lines - 1):
+        out_low(y).wait()
+    over.finish()
+
+
+def tail(middle, expand, valid, spread, count, gain_two, shift_two, gain_three, shift_three, pooled_grad, block_in, clip_count, fsdp, reps, collective_id):
+    sizes = stage_sizes(fsdp * reps)
+    lines, rows, mid_width = middle.shape
+    width = expand.shape[1]
+    pixels = pooled_grad.shape[1]
+    shape = jax.ShapeDtypeStruct
+    return pl.pallas_call(
+        functools.partial(tail_kernel, sizes, reps, clip_count),
+        out_shape=[
+            shape((clip_count, pixels, 1, width), f32), shape((lines, rows, width), f32), shape((lines, rows, width), bf16),
+            shape((lines, rows, mid_width), bf16), shape((lines, rows, mid_width), bf16),
+            shape((1, width), f32), shape((1, width), f32), shape((1, mid_width), f32), shape((1, mid_width), f32),
+        ],
+        in_specs=[IN_VMEM] * 10 + [ANY],
+        out_specs=[IN_VMEM, ANY, ANY] + [IN_VMEM] * 6,
+        scratch_shapes=[
+            pltpu.VMEM((lines, rows, width), f32), pltpu.VMEM((lines, rows, width), f32),
+            pltpu.VMEM((lines, rows, mid_width), f32), pltpu.VMEM((lines, rows, mid_width), f32),
+            pltpu.VMEM((2, rows, width), f32), pltpu.VMEM((2, rows, width), bf16),
+            pltpu.VMEM((4, 1, width), f32), pltpu.VMEM((2, 8, width), f32),
+            DMA((2,)), DMA((lines,)), DMA((2,)),
+        ] + exchange_buffers(sizes, 4, 2 * width + LANES),
+        compiler_params=pltpu.CompilerParams(collective_id=collective_id, has_side_effects=True, vmem_limit_bytes=VMEM_LIMIT),
+        name="tail",
+    )(middle, expand, valid, spread, count, gain_two, shift_two, gain_three, shift_three, pooled_grad, block_in)
 
 
 ORDER = ("HWNC", "HWIO", "HWNC")
@@ -570,41 +1050,32 @@
         gate = jax.nn.sigmoid(gate_pre + gate_full)
         modulated = (act_one * (1.0 + gate)).astype(bf16)
         middle = convolve(modulated, mid_full, 1, 1)
-        stats_two = moments(middle, 4, "moments_two")
-        zeta_two, normed_two = norm(middle, stats_two, gain_two_full, shift_two_full)
-        act_two = jax.nn.gelu(zeta_two).astype(bf16)
-        expanded = project(act_two, expand_full)
-        stats_three = moments(expanded, 5, "moments_three")
-        zeta_three, normed_three = norm(expanded, stats_three, gain_three_full, shift_three_full)
-        pre_out = block_in + zeta_three
-        block_out = jax.nn.gelu(pre_out) * valid
-        summed = jnp.sum(block_out.reshape(pixels, clip_count, seg_slots, feature_width), axis=2)
-        pooled = jnp.transpose((summed / count_float[None, :, None]).astype(bf16), (1, 0, 2))
-
-        spread = jnp.transpose(pooled_grad, (1, 0, 2)).astype(f32)[:, :, None]
-        spread = spread * (valid_seg / count_float[:, None])[None, :, :, None]
-        grad_pre = gelu_back(pre_out, spread.reshape(pre_out.shape))
-        grad_expanded, gain_three_sum, shift_three_sum = norm_back(
-            grad_pre, normed_three, stats_three, gain_three_full, 6, "sums_three"
-        )
-        expand_terms = project_terms(act_two, grad_expanded, bf16)
-        grad_act_two = project_back(grad_expanded, expand_full)
-        grad_middle, gain_two_sum, shift_two_sum = norm_back(
-            gelu_back(zeta_two, grad_act_two), normed_two, stats_two, gain_two_full, 7, "sums_two"
-        )
-        mid_terms = convolve_terms(modulated, grad_middle, 1, 1, bf16)
+        flat = (GRID, GRID * slots, -1)
+        lanes = lambda column: jnp.broadcast_to(column.reshape(-1, 1), (column.size, LANES))
+        (pooled, grad_pre, grad_expanded, act_two, grad_middle, gain_three_sum, shift_three_sum, gain_two_sum,
+         shift_two_sum) = tail(
+            middle.reshape(flat), expand_full, lanes(valid_seg), lanes(valid_seg / count_float[:, None]), lanes(local_count),
+            gain_two_full[None], shift_two_full[None], gain_three_full[None], shift_three_full[None],
+            pooled_grad.astype(f32)[:, :, None], block_in.reshape(flat), clip_count, fsdp, reps, 4,
+        )
+        pooled = pooled.reshape(pooled_grad.shape).astype(bf16)
+        gain_three_sum, shift_three_sum, gain_two_sum, shift_two_sum = (
+            row[0] for row in (gain_three_sum, shift_three_sum, gain_two_sum, shift_two_sum)
+        )
+        cube = (GRID, GRID, slots, -1)
+        grad_pre, grad_expanded, act_two, grad_middle = (
+            block.reshape(cube) for block in (grad_pre, grad_expanded, act_two, grad_middle)
+        )
         grad_modulated = convolve_back(grad_middle, mid_full, 1, 1)
         grad_gate_pre = grad_modulated * act_one * gate * (1.0 - gate)
         gate_terms = jnp.sum(grad_gate_pre, axis=(0, 1, 2))
         grad_gate = grad_gate_pre.astype(bf16)
-        diff_terms = [convolve_terms(change, grad_gate, 1, 1, bf16), convolve_terms(change, grad_gate, 1, 2, bf16)]
         grad_change = convolve_back(grad_gate, diff_full[0], 1, 1) + convolve_back(grad_gate, diff_full[1], 1, 2)
         grad_change = grad_change * pair
         grad_act_one = grad_modulated * (1.0 + gate) + earlier_of(grad_change) - grad_change
         grad_reduced, gain_one_sum, shift_one_sum = norm_back(
             gelu_back(zeta_one, grad_act_one), normed_one, stats_one, gain_one_full, 8, "sums_one"
         )
-        reduce_terms = project_terms(block_low, grad_reduced, bf16)
         features_grad = grad_pre + project_back(grad_reduced, reduce_full)
         grad_lateral = features_grad.astype(bf16)
         lateral_terms = project_terms(pool_low, grad_lateral, bf16)
@@ -627,17 +1098,29 @@
             axis=1,
         )
 
-        def owned(terms, shard):
-            return terms.reshape(shard.shape[:-2] + (fsdp,) + shard.shape[-2:])
-
-        diff_one, diff_two, mid_part, expand_part, reduce_part, small_part = scatter_all(
-            [
-                owned(diff_terms[0], diff_weight[0]), owned(diff_terms[1], diff_weight[1]),
-                owned(mid_terms, mid_weight), owned(expand_terms, expand_weight),
-                owned(reduce_terms, reduce_weight), small_terms,
-            ],
-            fsdp, reps, 10, "scatter_terms",
-        )
+        conv_rows = mid_weight.shape[0]
+        if conv_rows % 32 == 0:
+            small_part, reduce_part, expand_part, mid_part, diff_one, diff_two = terms_all(
+                small_terms.reshape(-1, feature_width), block_low.reshape(flat), grad_reduced.reshape(flat),
+                act_two.reshape(flat), grad_expanded.reshape(flat), modulated, grad_middle.reshape(flat), change,
+                grad_gate.reshape(flat),
+                [small_terms.shape[1], reduce_weight.shape[0], expand_weight.shape[0], conv_rows], fsdp, reps, 10,
+            )
+        else:
+            def owned(terms, shard):
+                return terms.reshape((fsdp,) + shard.shape[-2:])
+
+            small_part, reduce_part, expand_part, mid_part, diff_one, diff_two = scatter_all(
+                [
+                    small_terms,
+                    owned(project_terms(block_low, grad_reduced, bf16), reduce_weight),
+                    owned(project_terms(act_two, grad_expanded, bf16), expand_weight),
+                    owned(convolve_terms(modulated, grad_middle, 1, 1, bf16), mid_weight),
+                    owned(convolve_terms(change, grad_gate, 1, 1, bf16), diff_weight),
+                    owned(convolve_terms(change, grad_gate, 1, 2, bf16), diff_weight),
+                ],
+                fsdp, reps, 11, "scatter_terms",
+            )
 
         def own_share(whole):
             share = whole.shape[0] // fsdp

time: 603 us -> 562 us (0.932)
  Pallas kernels: 273 us -> 348 us
  other arithmetic: 82.8 us -> 24.8 us
  matrix products: 164 us -> 112 us
  local copies, waits for them, and re-layouts: 71.8 us -> 65.7 us
    pallas_call x9 -> x6, Pallas kernels: 179 us -> 254 us  [the longest x1 126 us: terms_all(): pl.pallas_call(functools.partial(terms_kernel, dims, reps, rows), out_sha...]
    conv_general_dilated x3 -> x0, matrix products: 32 us -> none  [convolve_terms(): lax.conv_general_dilated(source, grads, (stride, stride), pad_of(span * s...]
    reduce_sum x2 -> x1, other arithmetic: 29.5 us -> 3.95 us  [norm_back(): jnp.sum(masked * normed, axis=(0, 1, 2))]
    dot_general x3 -> x1, matrix products: 16 us -> 1.32 us  [project_terms(): jnp.einsum('yxnc,yxnd->cd', source, grads, preferred_element_type=kind)]
    convert_element_type x3 -> x1, other arithmetic: 15.1 us -> 0.94 us  [norm_back(): return (grad_in.astype(bf16), gain_sum, shift_sum)]
    dot_general x3 -> x2, matrix products: 24.9 us -> 14.1 us  [project_back(): jnp.einsum('yxnd,cd->yxnc', grads, weight, preferred_element_type=f32)]
    dot_general x3 -> x2, matrix products: 24.4 us -> 14.6 us  [project(): jnp.einsum('yxnc,cd->yxnd', source, weight, preferred_element_type=f32)]
    conv_general_dilated x4, matrix products: 40 us -> 49.7 us  [convolve(): lax.conv_general_dilated(source, kernel, (1, 1), pad_of(span * stride), r...]
where the time goes in v1:
time: 562 us; the launch traced here: 552 us
  Pallas kernels  348 us (62%)
  matrix products  112 us (20%)
  local copies, waits for them, and re-layouts  65.7 us (12%)
  other arithmetic  24.8 us (4%)
    pallas_call x1, Pallas kernels, terms_all(): pl.pallas_call(functools.partial(terms_kernel, dims, reps, rows), out_sha...  126 us
    pallas_call x1, Pallas kernels, gather_all(): pl.pallas_call(functools.partial(gather_kernel, dims, reps, stacked), out...  93.2 us
    pallas_call x1, Pallas kernels, tail(): pl.pallas_call(functools.partial(tail_kernel, sizes, reps, clip_count), o...  87.9 us
    conv_general_dilated x4, matrix products, convolve(): lax.conv_general_dilated(source, kernel, (1, 1), pad_of(span * stride), r...  49.7 us
    pallas_call x4, Pallas kernels, exchange(): pl.pallas_call(functools.partial(exchange_kernel, sizes, reps, moments),...  40.3 us
    conv_general_dilated x3, matrix products, convolve_back(): lax.conv_general_dilated(grads, kernel, (1, 1), pad_of(span * stride), rh...  30 us
    unnamed x79, local copies, waits for them, and re-layouts  21 us
    dot_general x2, matrix products, project(): jnp.einsum('yxnc,cd->yxnd', source, weight, preferred_element_type=f32)  14.6 us

profile of v1, /device:TPU:0, one launch (start us, length us, event | category | flops | bytes accessed | tf_op | source)
XLA Modules:
  0.0 552.4 jit_solution(2491064970833810443)
XLA Ops:
  0.7 0.8 fusion.56
  1.5 6.1 %concatenate.12 = bf16[424]{0:T(512)(128)(2,1)S(1)} concatenate(bf16[128]{0:T(256)(128)(2,1)} %param.35, bf16[128]{0:T(256)(128)(2,1)} %param.36, bf16[32]{0:T(256)(128)(2,1)} %param.27, bf16[32]{0:T(256)(128)(2,1)} %param.28, bf16[32]{0:T(256)(128)(2,1)} %param.30, bf16[32]{0:T(256)(128)(2,1)} %param.32, bf16[32]{0:T(256)(128)(2,1)} %param.33, bf16[4]{0:T(256)(128)(2,1)} %param.23, ...), dimensions={0} | concatenate | bytes 1696 | tf_op jit(solution)/shard_map/concatenate | solution.py:976
  7.6 1.4 fusion.55.refs_0_
  9.0 93.2 %gather_weights.1 = (bf16[16,16,2048]{2,1,0:T(8,128)(2,1)}, bf16[16,128,512]{2,1,0:T(8,128)(2,1)}, bf16[2,16,288,512]{3,2,1,0:T(8,128)(2,1)}, bf16[16,288,512]{2,1,0:T(8,128)(2,1)}, bf16[16,32,2048]{2,1,0:T(8,128)(2,1)}) custom-call(bf16[16,2048]{1,0:T(8,128)(2,1)} %fusion.55.refs_0_, bf16[128,512]{1,0:T(8,128)(2,1)} %refs_1_.1, ...), custom_call_target="tpu_custom_call" | custom-call | tf_op jit(solution)/shard_map/gather_weights/pallas_call | solution.py:179
  102.2 1.0 slice.89
  103.2 0.7 reshape_reshape.7
  103.9 0.9 convert_element_type.210
  105.4 5.7 %multiply_reduce_fusion.5 = (f32[64]{0:T(128)S(1)}, f32[7,7,32,64]{3,2,1,0:T(8,128)S(1)}) fusion(f32[32]{0:T(128)S(1)} %reshape.459, bf16[7,7,32,12]{2,3,1,0:T(8,128)(2,1)S(1)} %reshape.475, bf16[64,7,7,12]{3,2,1,0:T(8,128)(2,1)S(1)} %reshape_reshape.7), kind=kOutput, calls=%fused_computation.59 | convolution fusion | flops 67489728 | bytes 514688 | tf_op jit(solution)/shard_map/conv_general_dilated | solution.py:910
  111.1 0.7 convert_reduce_fusion.7
  112.8 13.3 %stem_moments.1 = (f32[1,128]{1,0:T(1,128)S(1)}, f32[1,128]{1,0:T(1,128)S(1)}, f32[1,128]{1,0:T(1,128)S(1)}) custom-call(f32[1,128]{1,0:T(1,128)S(1)} %pad.40.refs_0_, f32[1,128]{1,0:T(1,128)S(1)} %pad.41.refs_1_, f32[1,128]{1,0:T(1,128)S(1)} %broadcast_in_dim.13.refs_2_.refs_4_), custom_call_target="tpu_custom_call" | custom-call | tf_op jit(solution)/shard_map/stem_moments/pallas_call | solution.py:431
  126.2 0.9 convert_reduce_fusion.5
  127.9 1.3 slice.94
  129.3 4.3 copy.44
  133.7 9.0 %fusion.75 = (bf16[7,7,32,2048]{3,2,1,0:T(8,128)(2,1)}, f32[7,7,32,2048]{3,2,1,0:T(8,128)}) fusion(f32[7,7,32,2048]{3,2,1,0:T(8,128)S(1)} %bitcast.145, bf16[7,7,32,64]{3,2,1,0:T(8,128)(2,1)S(1)} %fusion.18, bf16[64,2048,1,1]{1,0,2,3:T(8,128)(2,1)S(1)} %reshape.471), kind=kOutput, calls=%fused_computation.140 | convolution fusion | flops 417464320 | bytes 32575488 | tf_op jit(solution)/shard_map/yxnc,cd->yxnd/dot_general | solution.py:938
  142.7 5.6 %multiply_reduce_fusion.2 = (f32[512]{0:T(512)S(1)}, f32[7,7,32,512]{3,2,1,0:T(8,128)S(1)}) fusion(f32[32]{0:T(128)S(1)} %reshape.459, bf16[7,7,32,2048]{3,2,1,0:T(8,128)(2,1)} %get-tuple-element.135, bf16[2048,512,1,1]{1,0,3,2:T(8,128)(2,1)S(1)} %bitcast.165), kind=kOutput, calls=%fused_computation.27 | convolution fusion | flops 3289939456 | bytes 11733120 | tf_op jit(solution)/shard_map/yxnc,cd->yxnd/dot_general | solution.py:938
  148.4 0.6 multiply_reduce_fusion.1
  149.0 9.2 %moments_one.1 = (f32[1,512]{1,0:T(1,128)S(1)}, f32[1,512]{1,0:T(1,128)S(1)}, f32[1,128]{1,0:T(1,128)S(1)}) custom-call(f32[1,512]{1,0:T(1,128)S(1)} %bitcast.137, f32[1,512]{1,0:T(1,128)S(1)} %bitcast.138, f32[1,128]{1,0:T(1,128)S(1)} %broadcast_in_dim.13.refs_2_.refs_4_), custom_call_target="tpu_custom_call" | custom-call | tf_op jit(solution)/shard_map/moments_one/pallas_call | solution.py:431
  158.3 1.1 convert_reduce_fusion
  159.6 1.5 multiply_multiply_fusion.2
  161.7 1.0 copy-done.7
  162.7 2.1 pad.42
  165.0 4.7 fusion.11.refs_7_
  169.7 7.3 %fusion.72 = (bf16[1,16,288,512]{3,2,1,0:T(8,128)(2,1)}, bf16[1,16,288,512]{3,2,1,0:T(8,128)(2,1)S(1)}) fusion(bf16[2,16,288,512]{3,2,1,0:T(8,128)(2,1)} %get-tuple-element.55), kind=kLoop, calls=%fused_computation.137 | loop fusion | bytes 18874368 | tf_op jit(solution)/shard_map/slice | solution.py:1049
  177.0 9.4 %fusion.77 = f32[7,7,32,512]{3,2,1,0:T(8,128)} fusion(bf16[7,7,32,512]{3,2,1,0:T(8,128)(2,1)S(1)} %fusion.11.refs_7_, bf16[3,3,512,512]{3,2,1,0:T(8,128)(2,1)S(1)} %bitcast.159), kind=kOutput, calls=%fused_computation.142 | convolution fusion | flops 6056574976 | bytes 9535488 | tf_op jit(solution)/shard_map/conv_general_dilated | solution.py:910
  186.5 23.2 %multiply_convert_fusion.1 = (bf16[7,7,32,512]{3,2,1,0:T(8,128)(2,1)S(1)}, f32[7,7,32,512]{3,2,1,0:T(8,128)}) fusion(f32[7,7,32,512]{3,2,1,0:T(8,128)} %copy-done.7, f32[512]{0:T(512)S(1)} %reshape.464, f32[7,7,32,512]{3,2,1,0:T(8,128)} %fusion.77, bf16[7,7,32,512]{3,2,1,0:T(8,128)(2,1)S(1)} %fusion.11.refs_7_, bf16[3,3,512,512]{3,2,1,0:T(8,128)(2,1)} %bitcast.153), kind=kOutput, calls=%fused_computation.22 | convolution fusion | flops 4855037952 | bytes 17565696 | tf_op jit(solution)/shard_map/conv_general_dilated | solution.py:910
  209.7 11.4 %fusion.78 = f32[7,7,32,512]{3,2,1,0:T(8,128)} fusion(bf16[7,7,32,512]{3,2,1,0:T(8,128)(2,1)S(1)} %get-tuple-element.139.refs_5_, bf16[3,3,512,512]{3,2,1,0:T(8,128)(2,1)} %bitcast.157), kind=kOutput, calls=%fused_computation.143 | convolution fusion | flops 6056574976 | bytes 9535488 | tf_op jit(solution)/shard_map/conv_general_dilated | solution.py:910
  221.3 0.7 broadcast_in_dim.15.refs_3_
  221.9 0.7 broadcast_in_dim.14.refs_2_
  222.6 0.7 reshape.465.refs_5_
  223.3 0.7 reshape.466.refs_6_
  223.9 1.4 bitcast_convert_fusion.1
  225.8 1.7 copy.48.refs_9_
  227.5 87.9 %tail.1 = (f32[2,49,1,2048]{3,2,1,0:T(1,128)}, f32[7,224,2048]{2,1,0:T(8,128)}, bf16[7,224,2048]{2,1,0:T(8,128)(2,1)}, bf16[7,224,512]{2,1,0:T(8,128)(2,1)}, bf1...) custom-call(f32[7,224,512]{2,1,0:T(8,128)} %bitcast.163, ...), custom_call_target="tpu_custom_call" | custom-call | tf_op jit(solution)/shard_map/tail/pallas_call | solution.py:879
  315.4 14.4 %fusion.69 = (bf16[512]{0:T(512)(128)(2,1)S(1)}, bf16[7,7,32,512]{3,2,1,0:T(8,128)(2,1)S(1)}, f32[7,7,32,512]{3,2,1,0:T(8,128)S(1)}) fusion(f32[7,7,32,512]{3,2,1,0:T(8,128)} %get-tuple-element.140, f32[7,7,32,512]{3,2,1,0:T(8,128)S(1)} %copy-done.8, bf16[7,7,32,512]{3,2,1,0:T(8,128)(2,1)} %bitcast.151, bf16[3,3,512,512]{3,2,1,0:T(8,128)(2,1)} %bitcast.158), kind=kOutput, calls=%fused_computation.135 | convolution fusion | flops 6061391360 | bytes 17564672 | tf_op jit(solution)/shard_map/conv_general_dilated | solution.py:919
  329.9 7.9 %fusion.79 = f32[7,7,32,512]{3,2,1,0:T(8,128)S(1)} fusion(bf16[7,7,32,512]{3,2,1,0:T(8,128)(2,1)S(1)} %get-tuple-element.124, bf16[3,3,512,512]{3,2,1,0:T(8,128)(2,1)S(1)} %bitcast.162), kind=kOutput, calls=%fused_computation.144 | convolution fusion | flops 6056574976 | bytes 9535488 | tf_op jit(solution)/shard_map/conv_general_dilated | solution.py:919
  337.9 7.7 %add_multiply_fusion = f32[7,7,32,512]{3,2,1,0:T(8,128)S(1)} fusion(f32[7,7,32,512]{3,2,1,0:T(8,128)S(1)} %fusion.79, bf16[7,7,32,512]{3,2,1,0:T(8,128)(2,1)S(1)} %get-tuple-element.124, bf16[3,3,512,512]{3,2,1,0:T(8,128)(2,1)S(1)} %bitcast.156, f32[32]{0:T(128)S(1)} %mul.377), kind=kOutput, calls=%fused_computation.20 | convolution fusion | flops 4850221056 | bytes 12746880 | tf_op jit(solution)/shard_map/conv_general_dilated | solution.py:919
  346.1 1.4 copy-done.4
  347.5 1.0 copy-done.13
  348.5 4.0 multiply_reduce_fusion
  352.4 9.0 %sums_one.1 = (f32[1,512]{1,0:T(1,128)S(1)}, f32[1,512]{1,0:T(1,128)S(1)}) custom-call(f32[1,512]{1,0:T(1,128)S(1)} %bitcast.132, f32[1,512]{1,0:T(1,128)S(1)} %bitcast.131), custom_call_target="tpu_custom_call" | custom-call | tf_op jit(solution)/shard_map/sums_one/pallas_call | solution.py:431
  361.5 0.9 multiply_convert_fusion
  362.5 0.6 copy-done.17
  363.1 9.4 %fusion.76 = (bf16[7,7,32,2048]{3,2,1,0:T(8,128)(2,1)S(1)}, f32[7,7,32,2048]{3,2,1,0:T(8,128)}) fusion(f32[7,7,32,2048]{3,2,1,0:T(8,128)} %bitcast.149, bf16[7,7,32,512]{3,2,1,0:T(8,128)(2,1)S(1)} %multiply_convert_fusion, bf16[2048,512,1,1]{1,0,3,2:T(8,128)(2,1)S(1)} %bitcast.166), kind=kOutput, calls=%fused_computation.141 | convolution fusion | flops 3294756864 | bytes 35815424 | tf_op jit(solution)/shard_map/yxnd,cd->yxnc/dot_general | solution.py:942
  372.5 2.7 copy-done.6
  375.3 1.3 fusion.12
  376.9 4.7 fusion.45
  381.7 1.0 multiply_reduce_fusion.3
  382.7 8.8 %sums_stem.1 = (f32[1,128]{1,0:T(1,128)S(1)}, f32[1,128]{1,0:T(1,128)S(1)}) custom-call(f32[1,128]{1,0:T(1,128)S(1)} %pad.44.refs_0_, f32[1,128]{1,0:T(1,128)S(1)} %pad.45.refs_1_), custom_call_target="tpu_custom_call" | custom-call | tf_op jit(solution)/shard_map/sums_stem/pallas_call | solution.py:431
  391.7 2.0 fusion.44
  395.1 1.5 copy.56
  396.6 126.3 %terms.1 = (f32[16,2048]{1,0:T(8,128)}, f32[128,512]{1,0:T(8,128)}, f32[32,2048]{1,0:T(8,128)}, f32[288,512]{1,0:T(8,128)}, f32[288,512]{1,0:T(8,128)}, /*index=5*/f32[288,512]{1,0:T(8,128)}) custom-call(bf16[256,2048]{1,0:T(8,128)(2,1)} %bitcast.164, bf16[7,224,2048]{2,1,0:T(8,128)(2,1)} %bitcast.150, bf16[7,224,512]{2,1,0:T(8,128)(2,1)} %bitcast.152, ...), custom_call_target="tpu_custom_call" | custom-call | tf_op jit(solution)/shard_map/terms/pallas_call | solution.py:668
  522.9 2.3 pad_maximum_fusion
  525.2 1.5 slice.110
  526.7 1.3 slice.109
  528.0 1.2 slice_bitcast_fusion
  530.4 11.9 %copy.57 = f32[2,16,49,2048]{3,1,2,0:T(8,128)} copy(f32[2,16,49,2048]{3,1,0,2:T(8,128)} %bitcast.143) | data formatting | bytes 25690112
  544.0 1.2 copy.75
  545.1 1.2 fusion.61
  546.3 1.2 fusion.62
  547.5 1.1 fusion.63
  548.6 1.1 fusion.64
  549.7 0.7 copy.79
  550.5 0.8 copy.80
  551.3 0.7 copy.81
  (121 shorter events, 8.9 us)
Async XLA Ops:
  0.7 110.4 %copy-start.31 = (s32[2]{0:T(128)S(1)}, s32[2]{0:T(128)}, u32[]{:S(2)}) copy-start(s32[2]{0:T(128)} %param.21) | copy-start | bytes 28
  1.5 103.3 %copy-start.29 = (f32[2,16]{1,0:T(2,128)}, f32[2,16]{1,0:T(2,128)S(1)}, u32[]{:S(2)}) copy-start(f32[2,16]{1,0:T(2,128)S(1)} %fusion.56) | copy-start | bytes 388
  105.3 28.3 %copy-start.18 = (bf16[7,7,32,12]{2,3,1,0:T(8,128)(2,1)}, bf16[7,7,32,12]{2,3,1,0:T(8,128)(2,1)S(1)}, u32[]{:S(2)}) copy-start(bf16[7,7,32,12]{2,3,1,0:T(8,128)(2,1)S(1)} %reshape.475) | copy-start | bytes 112900
  111.0 22.6 %copy-start.11 = (f32[7,7,32,64]{3,2,1,0:T(8,128)}, f32[7,7,32,64]{3,2,1,0:T(8,128)S(1)}, u32[]{:S(2)}) copy-start(f32[7,7,32,64]{3,2,1,0:T(8,128)S(1)} %get-tuple-element.134) | copy-start | bytes 1204228
  112.7 36.3 %copy-start = (f32[1,128]{1,0:T(1,128)}, f32[1,128]{1,0:T(1,128)S(1)}, u32[]{:S(2)}) copy-start(f32[1,128]{1,0:T(1,128)S(1)} %broadcast_in_dim.13.refs_2_.refs_4_) | copy-start | bytes 1540
  126.2 7.5 %copy-start.25 = (f32[64]{0:T(128)}, f32[64]{0:T(128)S(1)}, u32[]{:S(2)}) copy-start(f32[64]{0:T(128)S(1)} %get-tuple-element.146) | copy-start | bytes 772
  127.3 6.4 %copy-start.27 = (f32[64]{0:T(128)}, f32[64]{0:T(128)S(1)}, u32[]{:S(2)}) copy-start(f32[64]{0:T(128)S(1)} %reshape.462) | copy-start | bytes 772
  127.9 5.8 %copy-start.14 = (bf16[7,7,32,64]{3,2,1,0:T(8,128)(2,1)}, bf16[7,7,32,64]{3,2,1,0:T(8,128)(2,1)S(1)}, u32[]{:S(2)}) copy-start(bf16[7,7,32,64]{3,2,1,0:T(8,128)(2,1)S(1)} %fusion.18) | copy-start | bytes 602116
  133.7 9.0 %copy-start.16 = (bf16[16,128,512]{2,1,0:T(8,128)(2,1)S(1)}, bf16[16,128,512]{2,1,0:T(8,128)(2,1)}, u32[]{:S(2)}) copy-start(bf16[16,128,512]{2,1,0:T(8,128)(2,1)} %get-tuple-element.51) | copy-start | bytes 6291460
  148.4 12.7 %copy-start.3 = (f32[7,7,32,512]{3,2,1,0:T(8,128)}, f32[7,7,32,512]{3,2,1,0:T(8,128)S(1)}, u32[]{:S(2)}) copy-start(f32[7,7,32,512]{3,2,1,0:T(8,128)S(1)} %get-tuple-element.138) | copy-start | bytes 9633796
  161.1 1.7 copy-start.7
  162.7 2.1 copy-start.30
  162.7 2.2 copy-start.32
  169.7 16.8 %copy-start.1 = (bf16[7,7,32,512]{3,2,1,0:T(8,128)(2,1)}, bf16[7,7,32,512]{3,2,1,0:T(8,128)(2,1)S(1)}, u32[]{:S(2)}) copy-start(bf16[7,7,32,512]{3,2,1,0:T(8,128)(2,1)S(1)} %fusion.11.refs_7_) | copy-start | bytes 4816900
  177.0 9.4 %copy-start.10 = (bf16[1,16,288,512]{3,2,1,0:T(8,128)(2,1)}, bf16[1,16,288,512]{3,2,1,0:T(8,128)(2,1)S(1)}, u32[]{:S(2)}) copy-start(bf16[1,16,288,512]{3,2,1,0:T(8,128)(2,1)S(1)} %get-tuple-element.126) | copy-start | bytes 14155780
  209.7 11.4 %copy-start.2 = (bf16[7,7,32,512]{3,2,1,0:T(8,128)(2,1)}, bf16[7,7,32,512]{3,2,1,0:T(8,128)(2,1)S(1)}, u32[]{:S(2)}) copy-start(bf16[7,7,32,512]{3,2,1,0:T(8,128)(2,1)S(1)} %get-tuple-element.139.refs_5_) | copy-start | bytes 4816900
  209.7 15.6 %copy-start.22 = (bf16[2,49,2048]{2,0,1:T(2,128)(2,1)S(1)}, bf16[2,49,2048]{2,0,1:T(2,128)(2,1)}, u32[]{:S(2)}) copy-start(bf16[2,49,2048]{2,0,1:T(2,128)(2,1)} %param.37) | copy-start | bytes 1204228
  227.5 87.9 %copy-start.8 = (f32[7,7,32,512]{3,2,1,0:T(8,128)S(1)}, f32[7,7,32,512]{3,2,1,0:T(8,128)}, u32[]{:S(2)}) copy-start(f32[7,7,32,512]{3,2,1,0:T(8,128)} %copy-done.7) | copy-start | bytes 9633796
  227.5 102.4 %slice-start.2 = ((s8[4718592]{0:T(1024)(128)(4,1)}), s8[524288]{0:T(1024)(128)(4,1)S(1)}, s32[]{:S(2)}) async-start(s8[4718592]{0:T(1024)(128)(4,1)} %bitcast.160), calls=%async_computation.2 | async-start | bytes 1048576
  315.4 14.5 %slice-start.3 = ((s8[4718592]{0:T(1024)(128)(4,1)}), s8[4194304]{0:T(1024)(128)(4,1)S(1)}, s32[]{:S(2)}) async-start(s8[4718592]{0:T(1024)(128)(4,1)} %bitcast.160), calls=%async_computation.3 | async-start | bytes 8388608
  315.4 22.4 %slice-start = ((s8[4718592]{0:T(1024)(128)(4,1)}), s8[4194304]{0:T(1024)(128)(4,1)S(1)}, s32[]{:S(2)}) async-start(s8[4718592]{0:T(1024)(128)(4,1)} %bitcast.154), calls=%async_computation | async-start | bytes 8388608
  329.9 7.9 %copy-start.5 = (bf16[7,7,32,512]{3,2,1,0:T(8,128)(2,1)}, bf16[7,7,32,512]{3,2,1,0:T(8,128)(2,1)S(1)}, u32[]{:S(2)}) copy-start(bf16[7,7,32,512]{3,2,1,0:T(8,128)(2,1)S(1)} %get-tuple-element.124) | copy-start | bytes 4816900
  329.9 7.9 %slice-start.1 = ((s8[4718592]{0:T(1024)(128)(4,1)}), s8[524288]{0:T(1024)(128)(4,1)S(1)}, s32[]{:S(2)}) async-start(s8[4718592]{0:T(1024)(128)(4,1)} %bitcast.154), calls=%async_computation.1 | async-start | bytes 1048576
  345.6 1.9 copy-start.4
  345.6 2.9 copy-start.13
  361.5 1.6 copy-start.17
  362.5 10.1 %copy-start.9 = (bf16[7,7,32,512]{3,2,1,0:T(8,128)(2,1)}, bf16[7,7,32,512]{3,2,1,0:T(8,128)(2,1)S(1)}, u32[]{:S(2)}) copy-start(bf16[7,7,32,512]{3,2,1,0:T(8,128)(2,1)S(1)} %multiply_convert_fusion) | copy-start | bytes 4816900
  363.1 12.2 %copy-start.15 = (bf16[7,7,32,64]{3,2,1,0:T(8,128)(2,1)S(1)}, bf16[7,7,32,64]{3,2,1,0:T(8,128)(2,1)}, u32[]{:S(2)}) copy-start(bf16[7,7,32,64]{3,2,1,0:T(8,128)(2,1)} %copy-done.14) | copy-start | bytes 602116
  372.5 2.7 copy-start.6
  376.9 4.8 copy-start.12
  376.9 4.8 copy-start.26
  376.9 4.8 copy-start.28
  376.9 14.8 %copy-start.19 = (bf16[7,7,32,12]{2,3,1,0:T(8,128)(2,1)S(1)}, bf16[7,7,32,12]{2,3,1,0:T(8,128)(2,1)}, u32[]{:S(2)}) copy-start(bf16[7,7,32,12]{2,3,1,0:T(8,128)(2,1)} %copy-done.18) | copy-start | bytes 112900
  530.4 13.0 %copy-start.20 = (f32[2,49,1,2048]{3,2,1,0:T(1,128)S(1)}, f32[2,49,1,2048]{3,2,1,0:T(1,128)}, u32[]{:S(2)}) copy-start(f32[2,49,1,2048]{3,2,1,0:T(1,128)} %get-tuple-element.58) | copy-start | bytes 2408452
  530.4 19.4 %copy-start.24 = (f32[128,512]{1,0:T(8,128)S(1)}, f32[128,512]{1,0:T(8,128)}, u32[]{:S(2)}) copy-start(f32[128,512]{1,0:T(8,128)} %get-tuple-element.170) | copy-start | bytes 786436
  542.2 8.2 %copy-start.21 = (f32[288,512]{1,0:T(8,128)S(1)}, f32[288,512]{1,0:T(8,128)}, u32[]{:S(2)}) copy-start(f32[288,512]{1,0:T(8,128)} %get-tuple-element.175) | copy-start | bytes 1769476
  542.2 9.0 %copy-start.23 = (f32[32,2048]{1,0:T(8,128)S(1)}, f32[32,2048]{1,0:T(8,128)}, u32[]{:S(2)}) copy-start(f32[32,2048]{1,0:T(8,128)} %get-tuple-element.178) | copy-start | bytes 786436

commit v2 on v1

--- a/solution.py
+++ b/solution.py
@@ -52,13 +52,13 @@
         v = (self.iv + dv + size_c) % size_c
         return a * (size_b * size_c) + u * self.stride_u + v * self.stride_v
 
-    def greet(self):
+    def greet(self, more=()):
         size_a, size_b, size_c = self.dims
         peers = [(self.at(d, 0, 0), self.rep) for d in range(1, size_a)]
         peers += [(self.at(0, d, 0), self.rep) for d in range(1, size_b)]
         peers += [(self.at(0, 0, d), self.rep) for d in range(1, size_c)]
         peers += [(self.me, (self.rep + d) % self.reps) for d in range(1, self.reps)]
-        greet(peers)
+        greet(peers + list(more))
 
 
 def greet(peers):
@@ -91,110 +91,6 @@
     for ref, stacked in refs:
         out += [ref.at[j] for j in range(ref.shape[0])] if stacked else [ref]
     return out
-
-
-def gather_kernel(dims, reps, stacked, *refs):
-    number = len(stacked)
-    shards = views(zip(refs[:number], stacked))
-    fulls = views(zip(refs[number : 2 * number], stacked))
-    own_sem, a_sem, b_sem, c_sem, r_sem = refs[2 * number :]
-    count = len(shards)
-    size_a, size_b, size_c = dims
-    place = Place(dims, reps)
-    me, rep = place.me, place.rep
-    place.greet()
-    waits = []
-
-    def slot(k, index, which):
-        return fulls[k].at[index, :, columns(fulls[k].shape[-1] // reps, which)]
-
-    def push(k, da, du, dv, target, target_rep, sems):
-        index = place.at(-da, -du, -dv)
-        if (da, du, dv) == (0, 0, 0):
-            source = shards[k].at[:, columns(shards[k].shape[-1] // reps, rep)]
-        else:
-            source = slot(k, index, rep)
-        copy = remote(source, slot(k, index, rep), sems, target, target_rep)
-        copy.start()
-        waits.append(copy)
-
-    def landed(k, da, du, dv, which, sems):
-        there = slot(k, place.at(-da, -du, -dv), which)
-        remote(there, there, sems, me, rep).wait_recv()
-
-    def forward(k, da, du, dv):
-        if dv == 0 and du == 0:
-            for d in range(1, size_b):
-                push(k, da, 0, 0, place.at(0, d, 0), rep, b_sem.at[k, da, d - 1])
-        if dv == 0:
-            for d in range(1, size_c):
-                push(k, da, du, 0, place.at(0, 0, d), rep, c_sem.at[k, da, du, d - 1])
-        if (da, du, dv) != (0, 0, 0):
-            for d in range(1, reps):
-                push(k, da, du, dv, me, (rep + d) % reps, r_sem.at[k, da, du, dv, d - 1])
-
-    local = []
-    for k in range(count):
-        copy = pltpu.make_async_copy(shards[k], fulls[k].at[me], own_sem.at[k])
-        copy.start()
-        local.append(copy)
-    for k in range(count):
-        for d in range(1, size_a):
-            push(k, 0, 0, 0, place.at(d, 0, 0), rep, a_sem.at[k, d - 1])
-        forward(k, 0, 0, 0)
-    for step in range(count + 2):
-        if step < count:
-            for da in range(1, size_a):
-                landed(step, da, 0, 0, rep, a_sem.at[step, da - 1])
-                forward(step, da, 0, 0)
-        if 0 <= step - 1 < count:
-            for du in range(1, size_b):
-                for da in range(size_a):
-                    landed(step - 1, da, du, 0, rep, b_sem.at[step - 1, da, du - 1])
-                    forward(step - 1, da, du, 0)
-        if 0 <= step - 2 < count:
-            for dv in range(1, size_c):
-                for du in range(size_b):
-                    for da in range(size_a):
-                        landed(step - 2, da, du, dv, rep, c_sem.at[step - 2, da, du, dv - 1])
-                        forward(step - 2, da, du, dv)
-    for k in range(count):
-        for dv in range(size_c):
-            for du in range(size_b):
-                for da in range(size_a):
-                    if (da, du, dv) != (0, 0, 0):
-                        for d in range(1, reps):
-                            landed(k, da, du, dv, (rep + reps - d) % reps, r_sem.at[k, da, du, dv, d - 1])
-    for copy in waits:
-        copy.wait_send()
-    for copy in local:
-        copy.wait()
-
-
-def gather_all(shards, fsdp, reps, collective_id, name):
-    dims = factor_three(fsdp)
-    size_a, size_b, size_c = dims
-    stacked = [s.ndim == 3 for s in shards]
-    count = sum(s.shape[0] if s.ndim == 3 else 1 for s in shards)
-    return pl.pallas_call(
-        functools.partial(gather_kernel, dims, reps, stacked),
-        out_shape=[
-            jax.ShapeDtypeStruct(s.shape[:-2] + (fsdp,) + s.shape[-2:], s.dtype) for s in shards
-        ],
-        in_specs=[ANY] * len(shards),
-        out_specs=[ANY] * len(shards),
-        scratch_shapes=[
-            DMA((count,)),
-            DMA((count, max(size_a - 1, 1), 2)),
-            DMA((count, size_a, max(size_b - 1, 1), 2)),
-            DMA((count, size_a, size_b, max(size_c - 1, 1), 2)),
-            DMA((count, size_a, size_b, size_c, max(reps - 1, 1), 2)),
-        ],
-        compiler_params=pltpu.CompilerParams(
-            collective_id=collective_id, has_side_effects=True, vmem_limit_bytes=VMEM_LIMIT
-        ),
-        name=name,
-    )(*shards)
 
 
 def scatter_kernel(dims, reps, stacked, *refs):
@@ -442,6 +338,27 @@
     return [result[0, :width] for result in results[:2]] + [result[0, 0] for result in results[2:]]
 
 
+TANH_SCALE = 0.7978845608028654
+CUBIC = 0.044715
+
+
+def gelu_parts(x):
+    square = x * x
+    bend = jnp.tanh(TANH_SCALE * x * (1.0 + CUBIC * square))
+    half = 0.5 * (1.0 + bend)
+    slope = half + 0.5 * x * (1.0 - bend * bend) * (TANH_SCALE * (1.0 + 3.0 * CUBIC * square))
+    return x * half, slope
+
+
+def fold_rows(values):
+    groups, slots, width = values.shape
+    return jnp.sum(values.reshape(groups * slots // 8, 8, width), axis=0)
+
+
+def whole_row(values):
+    return jnp.sum(values, axis=0, keepdims=True)
+
+
 def dot(left, right):
     return jnp.dot(left, right, preferred_element_type=f32)
 
@@ -686,25 +603,344 @@
     )(small, block_low, grad_reduced, act_two, grad_expanded, modulated, grad_middle, change, grad_gate)
 
 
-TANH_SCALE = 0.7978845608028654
-CUBIC = 0.044715
-
-
-def gelu_parts(x):
-    square = x * x
-    bend = jnp.tanh(TANH_SCALE * x * (1.0 + CUBIC * square))
-    half = 0.5 * (1.0 + bend)
-    slope = half + 0.5 * x * (1.0 - bend * bend) * (TANH_SCALE * (1.0 + 3.0 * CUBIC * square))
-    return x * half, slope
-
-
-def fold_rows(values):
-    groups, slots, width = values.shape
-    return jnp.sum(values.reshape(groups * slots // 8, 8, width), axis=0)
-
-
-def whole_row(values):
-    return jnp.sum(values, axis=0, keepdims=True)
+class Gather:
+    def __init__(self, dims, reps, shards, fulls, buffers):
+        self.dims, self.reps, self.shards, self.fulls = dims, reps, shards, fulls
+        self.own_sem, self.a_sem, self.b_sem, self.c_sem, self.r_sem = buffers
+        self.place = Place(dims, reps)
+        self.waits, self.local = [], []
+
+    def slot(self, k, index, which):
+        full = self.fulls[k]
+        return full.at[index, :, columns(full.shape[-1] // self.reps, which)]
+
+    def push(self, k, da, du, dv, target, target_rep, sems):
+        index, rep = self.place.at(-da, -du, -dv), self.place.rep
+        if (da, du, dv) == (0, 0, 0):
+            source = self.shards[k].at[:, columns(self.shards[k].shape[-1] // self.reps, rep)]
+        else:
+            source = self.slot(k, index, rep)
+        copy = remote(source, self.slot(k, index, rep), sems, target, target_rep)
+        copy.start()
+        self.waits.append(copy)
+
+    def landed(self, k, da, du, dv, which, sems):
+        there = self.slot(k, self.place.at(-da, -du, -dv), which)
+        remote(there, there, sems, self.place.me, self.place.rep).wait_recv()
+
+    def forward(self, k, da, du, dv):
+        size_a, size_b, size_c = self.dims
+        place, rep = self.place, self.place.rep
+        if dv == 0 and du == 0:
+            for d in range(1, size_b):
+                self.push(k, da, 0, 0, place.at(0, d, 0), rep, self.b_sem.at[k, da, d - 1])
+        if dv == 0:
+            for d in range(1, size_c):
+                self.push(k, da, du, 0, place.at(0, 0, d), rep, self.c_sem.at[k, da, du, d - 1])
+        if (da, du, dv) != (0, 0, 0):
+            for d in range(1, self.reps):
+                self.push(k, da, du, dv, place.me, (rep + d) % self.reps, self.r_sem.at[k, da, du, dv, d - 1])
+
+    def begin(self, k):
+        place = self.place
+        copy = pltpu.make_async_copy(self.shards[k], self.fulls[k].at[place.me], self.own_sem.at[k])
+        copy.start()
+        self.local.append(copy)
+        for d in range(1, self.dims[0]):
+            self.push(k, 0, 0, 0, place.at(d, 0, 0), place.rep, self.a_sem.at[k, d - 1])
+        self.forward(k, 0, 0, 0)
+
+    def hop(self, k, lag):
+        size_a, size_b, size_c = self.dims
+        place, reps, rep = self.place, self.reps, self.place.rep
+        if lag == 0:
+            for da in range(1, size_a):
+                self.landed(k, da, 0, 0, rep, self.a_sem.at[k, da - 1])
+                self.forward(k, da, 0, 0)
+        elif lag == 1:
+            for du in range(1, size_b):
+                for da in range(size_a):
+                    self.landed(k, da, du, 0, rep, self.b_sem.at[k, da, du - 1])
+                    self.forward(k, da, du, 0)
+        elif lag == 2:
+            for dv in range(1, size_c):
+                for du in range(size_b):
+                    for da in range(size_a):
+                        self.landed(k, da, du, dv, rep, self.c_sem.at[k, da, du, dv - 1])
+                        self.forward(k, da, du, dv)
+        else:
+            for dv in range(size_c):
+                for du in range(size_b):
+                    for da in range(size_a):
+                        if (da, du, dv) != (0, 0, 0):
+                            for d in range(1, reps):
+                                self.landed(k, da, du, dv, (rep + reps - d) % reps, self.r_sem.at[k, da, du, dv, d - 1])
+            self.local[k].wait()
+
+    def finish(self):
+        for copy in self.waits:
+            copy.wait_send()
+
+
+def gather_buffers(dims, reps, count):
+    size_a, size_b, size_c = dims
+    return [
+        DMA((count,)),
+        DMA((count, max(size_a - 1, 1), 2)),
+        DMA((count, size_a, max(size_b - 1, 1), 2)),
+        DMA((count, size_a, size_b, max(size_c - 1, 1), 2)),
+        DMA((count, size_a, size_b, size_c, max(reps - 1, 1), 2)),
+    ]
+
+
+def head_kernel(dims, reps, sizes, stem_rows, *refs):
+    stem_own, reduce_own, diff_own, mid_own, expand_own = refs[:5]
+    lateral_own, wide_own, narrow_own, least_own, lhs, valid, pair, count, features = refs[5:14]
+    (lateral_out, vector_out, reduce_out, diff_out, mid_out, expand_out, block_in, block_low, stem_normed, pool_low, stem_inverse,
+     number_out, normed_one, inverse_one, act_one, change) = refs[14:30]
+    (small_own, small, stem_taps, reduce_full, tap_rows, lateral, stem_values, stem_act, loaded, wide, low, reduced) = refs[30:42]
+    load_sem, wide_sem, low_sem, out_sem = refs[42:46]
+    gather = Gather(
+        dims, reps, [small_own, stem_own, reduce_own, diff_own.at[0], diff_own.at[1], mid_own, expand_own],
+        [small, stem_taps, reduce_full, diff_out.at[0], diff_out.at[1], mid_out, expand_out], refs[46:51],
+    )
+    over = Exchange(sizes, reps, refs[51:])
+    fsdp = small.shape[0]
+    me = gather.place.me
+    stem_width = stem_rows * fsdp
+    lines, rows, mid_width = reduced.shape
+    clips, pixels, segs, width = features.shape
+    slots = valid.shape[0]
+    groups = rows // slots
+    step = 256
+    chunks = width // step
+    mask = valid[:, :1].reshape(1, slots, 1)
+    pairs = pair[:, :1].reshape(1, slots, 1)
+    own = count[:, :1]
+
+    def load(j):
+        cols = slice(j * step, (j + 1) * step)
+        return [
+            pltpu.make_async_copy(
+                features.at[clip, :, :, cols], loaded.at[j % 2, :, clip * segs : (clip + 1) * segs, :], load_sem.at[j % 2, clip]
+            )
+            for clip in range(clips)
+        ]
+
+    def grouped(values):
+        return values.reshape(groups, slots, values.shape[-1])
+
+    def moments(carry, origin):
+        away, squares = whole_row(carry[0]), whole_row(carry[1])
+        return [away + own * origin, jnp.maximum(squares - away * away / own, 0.0), count[...]]
+
+    def add_moments(carry, values, origin):
+        off = (grouped(values) - origin.reshape(1, 1, -1)) * mask
+        return carry[0] + fold_rows(off), carry[1] + fold_rows(off * off)
+
+    def blank(n):
+        return jnp.zeros((8, n), f32), jnp.zeros((8, n), f32)
+
+    for copy in load(0):
+        copy.start()
+
+    def placed(values, length):
+        share = values.shape[1]
+        one = lax.broadcasted_iota(jnp.int32, (share, length), 1) - me * share
+        hot = (one == lax.broadcasted_iota(jnp.int32, (share, length), 0)).astype(f32).astype(bf16)
+        return dot(values, hot)
+
+    least = placed(least_own[...], LANES * -(-stem_width // LANES))
+    narrow = placed(narrow_own[...], mid_width)
+    pieces = [narrow[n : n + 1] for n in range(narrow.shape[0])] + [least[n : n + 1] for n in range(least.shape[0])]
+    joined = jnp.concatenate(pieces, axis=1)
+    joined = jnp.concatenate([joined, jnp.zeros((1, -joined.shape[1] % width), f32)], axis=1)
+    small_rows = [lateral_own[...].astype(f32), placed(wide_own[...], width)]
+    small_rows += [joined[:, n * width : (n + 1) * width] for n in range(joined.shape[1] // width)]
+    taken = sum(row.shape[0] for row in small_rows)
+    small_rows.append(jnp.zeros((small_own.shape[0] - taken, width), f32))
+    small_own[...] = jnp.concatenate(small_rows, axis=0).astype(bf16)
+    gather.place.greet(over.peers)
+    for k in range(3):
+        gather.begin(k)
+    stem_act[...] = jnp.zeros(stem_act.shape, f32)
+    for lag in range(3):
+        gather.hop(0, lag)
+        gather.hop(1, lag)
+    for k in range(3, 7):
+        gather.begin(k)
+    gather.hop(0, 3)
+    gather.hop(1, 3)
+    vectors = jnp.zeros((taken - stem_rows, width), f32)
+    for device in range(fsdp):
+        values = small[device].astype(f32)
+        span = slice(device * stem_rows, (device + 1) * stem_rows)
+        lateral[span, :] = values[:stem_rows]
+        vectors = vectors + values[stem_rows:taken]
+        taps = stem_taps[device].astype(f32)
+        for x in range(GRID):
+            tap_rows[x, span, :] = taps[x * stem_rows : (x + 1) * stem_rows]
+    lateral_low = lateral[...].astype(bf16)
+    vector_out[...] = vectors
+    lateral_out[...] = lateral_low
+
+    def vector(position, length):
+        row, start = 2 + position // width, position % width
+        return vectors[row : row + 1, start : start + length]
+
+    gain_one, shift_one = vector(0, mid_width), vector(mid_width, mid_width)
+    start = mid_width * narrow.shape[0]
+    stem_gain, stem_shift = vector(start, stem_width), vector(start + least.shape[1], stem_width)
+    gather.hop(2, 0)
+
+    def stem_column(x, _):
+        stem_values[x] = dot_t(lhs[...], tap_rows[x].astype(bf16))
+        return 0
+
+    lax.fori_loop(0, GRID, stem_column, 0)
+    origin = stem_values[0, 0:1, :]
+    carry = lax.fori_loop(0, GRID, lambda x, c: add_moments(c, stem_values[x], origin), blank(stem_width))
+    gather.hop(3, 0)
+    gather.hop(2, 1)
+    total, squares, number = over.total(0, moments(carry, origin), True)
+    number_out[...] = number
+    number = number[:, :1]
+    centre, inverse = total / number, lax.rsqrt(squares / number + epsilon)
+    stem_inverse[...] = inverse
+    gather.hop(2, 2)
+
+    def stem_norm(x, _):
+        normed = (stem_values[x] - centre) * inverse
+        stem_normed[:, x] = grouped(normed)
+        zeta = mask * (grouped(normed) * stem_gain.reshape(1, 1, -1) + stem_shift.reshape(1, 1, -1))
+        stem_act[x + 1, 1 : GRID + 1] = gelu_parts(zeta)[0]
+        return 0
+
+    lax.fori_loop(0, GRID, stem_norm, 0)
+
+    def stem_pool(x, _):
+        total = stem_act[x] + stem_act[x + 1] + stem_act[x + 2]
+        total = total[0:GRID] + total[1 : GRID + 1] + total[2 : GRID + 2]
+        pool_low[:, x] = (total / 9.0).astype(bf16)
+        return 0
+
+    lax.fori_loop(0, GRID, stem_pool, 0)
+    gather.hop(4, 0)
+    gather.hop(3, 1)
+    gather.hop(2, 3)
+
+    later = [(5, 0), (4, 1), (3, 2), (6, 0), (5, 1), (4, 2)]
+    for j in range(chunks):
+        slot = j % 2
+        cols = slice(j * step, (j + 1) * step)
+        for copy in load(j + 1) if j + 1 < chunks else ():
+            copy.start()
+        for copy in load(j):
+            copy.wait()
+        out_wide = pltpu.make_async_copy(wide.at[slot], block_in.at[:, :, cols], wide_sem.at[slot])
+        out_low = pltpu.make_async_copy(low.at[slot], block_low.at[:, :, cols], low_sem.at[slot])
+
+        if j >= 2:
+            out_wide.wait()
+            out_low.wait()
+        shares = step // reduce_full.shape[1]
+        weight = reduce_full[j * shares : (j + 1) * shares].reshape(step, mid_width)
+
+        def line(y, _):
+            values = loaded[slot, pl.ds(y * groups, groups)].astype(f32).reshape(rows, step)
+            values = values + dot(pool_low[y].reshape(rows, stem_width), lateral_low[:, cols])
+            wide[slot, y] = values
+            rounded = values.astype(bf16)
+            low[slot, y] = rounded
+            product = dot(rounded, weight)
+            reduced[y] = product if j == 0 else reduced[y] + product
+            return 0
+
+        lax.fori_loop(0, lines, line, 0)
+        out_wide.start()
+        out_low.start()
+        if j < len(later):
+            gather.hop(*later[j])
+    pltpu.make_async_copy(reduce_full, reduce_out, out_sem).start()
+
+    origin = reduced[0, 0:1, :]
+    carry = lax.fori_loop(0, lines, lambda y, c: add_moments(c, reduced[y], origin), blank(mid_width))
+    total, squares, _ = over.total(1, moments(carry, origin), True)
+    centre, inverse = total / number, lax.rsqrt(squares / number + epsilon)
+    inverse_one[...] = inverse
+    gather.hop(6, 1)
+    gather.hop(5, 2)
+
+    def first(y, _):
+        normed = (reduced[y] - centre) * inverse
+        normed_one[y] = normed
+        zeta = mask * (grouped(normed) * gain_one.reshape(1, 1, -1) + shift_one.reshape(1, 1, -1))
+        act = gelu_parts(zeta)[0].reshape(rows, mid_width)
+        act_one[y] = act
+        change[y] = (pairs * grouped(pltpu.roll(act, rows - 1, 0) - act)).astype(bf16).reshape(rows, mid_width)
+        return 0
+
+    lax.fori_loop(0, lines, first, 0)
+    gather.hop(6, 2)
+    for k in range(3, 7):
+        gather.hop(k, 3)
+    for j in (chunks - 2, chunks - 1):
+        cols = slice(j * step, (j + 1) * step)
+        pltpu.make_async_copy(wide.at[j % 2], block_in.at[:, :, cols], wide_sem.at[j % 2]).wait()
+        pltpu.make_async_copy(low.at[j % 2], block_low.at[:, :, cols], low_sem.at[j % 2]).wait()
+    pltpu.make_async_copy(reduce_full, reduce_out, out_sem).wait()
+    gather.finish()
+    over.finish()
+
+
+def head(stem_taps, reduce_weight, diff_weight, mid_weight, expand_weight, lateral, wide, narrow, least, lhs, valid, pair, count, features, fsdp, reps, collective_id):
+    dims, sizes = factor_three(fsdp), stage_sizes(fsdp * reps)
+    shape = jax.ShapeDtypeStruct
+    clips, pixels, segs, width = features.shape
+    slots = clips * segs
+    mid_width = reduce_weight.shape[1]
+    stem_rows = lateral.shape[0]
+    stem_width = stem_rows * fsdp
+    rows = GRID * slots
+    step = 256
+    side = GRID + 2
+    lengths = narrow.shape[0] * mid_width + least.shape[0] * (-(-stem_width // LANES) * LANES)
+    vectors = 2 + -(-lengths // width)
+    small = shape((-(-(stem_rows + vectors) // 16) * 16, width), bf16)
+
+    def full(shard):
+        return shape(shard.shape[:-2] + (fsdp,) + shard.shape[-2:], shard.dtype)
+
+    def whole(shard):
+        return pltpu.VMEM((fsdp,) + shard.shape, shard.dtype)
+
+    return pl.pallas_call(
+        functools.partial(head_kernel, dims, reps, sizes, stem_rows),
+        out_shape=[
+            shape((stem_width, width), bf16), shape((vectors, width), f32),
+            full(reduce_weight), full(diff_weight), full(mid_weight), full(expand_weight),
+            shape((GRID, rows, width), f32), shape((GRID, rows, width), bf16),
+            shape((GRID, GRID, slots, stem_width), f32), shape((GRID, GRID, slots, stem_width), bf16),
+            shape((1, stem_width), f32), shape((1, LANES), f32),
+            shape((GRID, rows, mid_width), f32), shape((1, mid_width), f32), shape((GRID, rows, mid_width), f32),
+            shape((GRID, rows, mid_width), bf16),
+        ],
+        in_specs=[ANY] * 5 + [IN_VMEM] * 8 + [ANY],
+        out_specs=[IN_VMEM] * 2 + [ANY] * 6 + [IN_VMEM] * 8,
+        scratch_shapes=[
+            pltpu.VMEM(small.shape, bf16), whole(small), whole(stem_taps), whole(reduce_weight),
+            pltpu.VMEM((GRID, stem_width, stem_taps.shape[1]), f32), pltpu.VMEM((stem_width, width), f32),
+            pltpu.VMEM((GRID, rows, stem_width), f32), pltpu.VMEM((side, side, slots, stem_width), f32),
+            pltpu.VMEM((2, pixels, slots, step), bf16),
+            pltpu.VMEM((2, GRID, rows, step), f32), pltpu.VMEM((2, GRID, rows, step), bf16),
+            pltpu.VMEM((GRID, rows, mid_width), f32),
+            DMA((2, clips)), DMA((2,)), DMA((2,)), DMA(()),
+        ] + gather_buffers(dims, reps, 7) + exchange_buffers(sizes, 2, 2 * mid_width + LANES),
+        compiler_params=pltpu.CompilerParams(
+            collective_id=collective_id, has_side_effects=True, vmem_limit_bytes=VMEM_LIMIT
+        ),
+        name="head",
+    )(stem_taps, reduce_weight, diff_weight, mid_weight, expand_weight, lateral, wide, narrow, least, lhs, valid, pair, count, features)
 
 
 def tail_kernel(sizes, reps, clip_count, *refs):
@@ -972,46 +1208,44 @@
         count_float = seg_counts.astype(f32)
         local_count = jnp.sum(count_float) * pixels
 
-        vectors = [gain_three, shift_three, gain_one, shift_one, gate_shift, gain_two, shift_two, stem_gain, stem_shift]
-        row = jnp.concatenate(vectors)
-        small = jnp.concatenate(
-            [
-                lateral,
-                jnp.pad(stem_weight, ((0, 0), (0, feature_width - stem_depth))),
-                jnp.pad(row[None], ((0, 15 - 2 * stem_rows), (0, feature_width - row.shape[0]))),
-            ]
+        taps = jnp.pad(stem_weight.reshape(stem_rows, GRID, GRID, -1), ((0, 0), (0, 0), (3, 3), (0, 0)))
+        taps = jnp.stack([taps[:, :, 6 - x : 13 - x] for x in range(GRID)]).reshape(GRID * stem_rows, stem_depth)
+        taps = jnp.pad(taps, ((0, -taps.shape[0] % 16), (0, -stem_depth % (LANES * reps))))
+        moving = frames.astype(f32)
+        motion = (moving[:, :, 1:] - moving[:, :, :-1]) * valid_seg[:, :, None, None, None]
+        motion = jnp.transpose(motion.astype(bf16), (4, 0, 1, 2, 3)).reshape(GRID, GRID, slots, -1)
+        strips = jnp.transpose(motion, (0, 2, 1, 3)).reshape(GRID, slots, -1)
+        strips = jnp.pad(strips, ((3, 3), (0, 0), (0, 0)))
+        strips = jnp.concatenate([strips[dy : dy + GRID] for dy in range(GRID)], axis=-1).reshape(GRID * slots, -1)
+        strips = jnp.pad(strips, ((0, 0), (0, -stem_depth % (LANES * reps))))
+        lanes = lambda column: jnp.broadcast_to(column.reshape(-1, 1), (column.size, LANES))
+        (lateral_full, vectors, reduce_full, diff_full, mid_full, expand_full, block_in, block_low, stem_normed, pool_low,
+         stem_inverse, number, normed_one, inverse_one, act_one, change) = head(
+            taps, reduce_weight, diff_weight, mid_weight, expand_weight, lateral, jnp.stack([gain_three, shift_three]),
+            jnp.stack([gain_one, shift_one, gate_shift, gain_two, shift_two]), jnp.stack([stem_gain, stem_shift]),
+            strips, lanes(valid_seg), lanes(pair_seg), lanes(local_count), jnp.transpose(features, (0, 2, 1, 3)),
+            fsdp, reps, 1,
         )
-        small_full, reduce_full, diff_full, mid_full, expand_full = gather_all(
-            [small, reduce_weight, diff_weight, mid_weight, expand_weight], fsdp, reps, 1, "gather_weights"
+        row = vectors[2:].reshape(-1)
+        gain_one_full, shift_one_full, gate_full, gain_two_full, shift_two_full = (
+            row[n * mid_width : (n + 1) * mid_width] for n in range(5)
         )
-        lateral_full = small_full[:, :stem_rows].reshape(stem_width, feature_width)
-        stem_full = small_full[:, stem_rows : 2 * stem_rows, :stem_depth].reshape(stem_width, stem_depth)
-        full = []
-        start = 0
-        for vector in vectors:
-            size = vector.shape[0]
-            full.append(small_full[:, 2 * stem_rows, start : start + size].reshape(-1).astype(f32))
-            start += size
-        (gain_three_full, shift_three_full, gain_one_full, shift_one_full, gate_full, gain_two_full,
-         shift_two_full, stem_gain_full, stem_shift_full) = full
+        gain_three_full, shift_three_full = vectors[0], vectors[1]
+        start = 5 * mid_width
+        stem_gain_full = row[start : start + stem_width]
+        start += -(-stem_width // LANES) * LANES
+        stem_shift_full = row[start : start + stem_width]
         reduce_full = reduce_full.reshape(-1, mid_width)
         diff_full = diff_full.reshape(2, -1, mid_width)
         mid_full = mid_full.reshape(-1, mid_width)
         expand_full = expand_full.reshape(mid_width, -1)
-
-        def moments(values, collective_id, name):
-            total = jnp.sum(values * valid, axis=(0, 1, 2))
-            off = values - total / local_count
-            squares = jnp.sum(off * off * valid, axis=(0, 1, 2))
-            total, squares, count = exchange(
-                [total, squares, local_count], fsdp, reps, True, collective_id, name
-            )
-            centre = total / count
-            return centre, lax.rsqrt(squares / count + epsilon), count
-
-        def norm(values, stats, gain, shift):
-            normed = (values - stats[0]) * stats[1]
-            return valid * (gain * normed + shift), normed
+        cube = (GRID, GRID, slots, -1)
+        flat = (GRID, GRID * slots, -1)
+        normed_one, act_one, change = normed_one.reshape(cube), act_one.reshape(cube), change.reshape(cube)
+        stats_one = (None, inverse_one[0], number[0, 0])
+        stem_stats = (None, stem_inverse[0], number[0, 0])
+        zeta_one = valid * (gain_one_full * normed_one + shift_one_full)
+        stem_norm = valid * (stem_gain_full * stem_normed + stem_shift_full)
 
         def norm_back(grad_out, normed, stats, gain, collective_id, name):
             masked = grad_out * valid
@@ -1022,47 +1256,24 @@
             grad_in = valid * stats[1] * gain * (masked - shift_sum / stats[2] - normed * gain_sum / stats[2])
             return grad_in.astype(bf16), gain_sum, shift_sum
 
-        moving = frames.astype(f32)
-        motion = (moving[:, :, 1:] - moving[:, :, :-1]) * valid_seg[:, :, None, None, None]
-        motion = jnp.transpose(motion.astype(bf16), (4, 0, 1, 2, 3)).reshape(GRID, GRID, slots, -1)
-        stem_kernel = jnp.transpose(stem_full.reshape(stem_width, GRID, GRID, -1), (1, 2, 3, 0))
-        stem_pre = convolve(motion, stem_kernel, 3, 1)
-        stem_stats = moments(stem_pre, 2, "stem_moments")
-        stem_norm, stem_normed = norm(stem_pre, stem_stats, stem_gain_full, stem_shift_full)
-        pool_low = pool_mean(jax.nn.gelu(stem_norm)).astype(bf16)
-        turned = jnp.transpose(features.reshape(slots, GRID, GRID, feature_width), (1, 2, 0, 3))
-        block_in = turned.astype(f32) + project(pool_low, lateral_full)
-        block_low = block_in.astype(bf16)
-        reduced = project(block_low, reduce_full)
-        stats_one = moments(reduced, 3, "moments_one")
-        zeta_one, normed_one = norm(reduced, stats_one, gain_one_full, shift_one_full)
-        act_one = jax.nn.gelu(zeta_one)
-        def later_of(values):
-            grid = values.reshape(GRID, GRID, clip_count, seg_slots, -1)
-            return jnp.pad(grid[:, :, :, 1:], ((0, 0), (0, 0), (0, 0), (0, 1), (0, 0))).reshape(values.shape)
-
         def earlier_of(values):
             grid = values.reshape(GRID, GRID, clip_count, seg_slots, -1)
             return jnp.pad(grid[:, :, :, :-1], ((0, 0), (0, 0), (0, 0), (1, 0), (0, 0))).reshape(values.shape)
 
-        change = ((later_of(act_one) - act_one) * pair).astype(bf16)
         gate_pre = convolve(change, diff_full[0], 1, 1) + convolve(change, diff_full[1], 1, 2)
         gate = jax.nn.sigmoid(gate_pre + gate_full)
         modulated = (act_one * (1.0 + gate)).astype(bf16)
         middle = convolve(modulated, mid_full, 1, 1)
-        flat = (GRID, GRID * slots, -1)
-        lanes = lambda column: jnp.broadcast_to(column.reshape(-1, 1), (column.size, LANES))
         (pooled, grad_pre, grad_expanded, act_two, grad_middle, gain_three_sum, shift_three_sum, gain_two_sum,
          shift_two_sum) = tail(
             middle.reshape(flat), expand_full, lanes(valid_seg), lanes(valid_seg / count_float[:, None]), lanes(local_count),
             gain_two_full[None], shift_two_full[None], gain_three_full[None], shift_three_full[None],
-            pooled_grad.astype(f32)[:, :, None], block_in.reshape(flat), clip_count, fsdp, reps, 4,
+            pooled_grad.astype(f32)[:, :, None], block_in, clip_count, fsdp, reps, 4,
         )
         pooled = pooled.reshape(pooled_grad.shape).astype(bf16)
         gain_three_sum, shift_three_sum, gain_two_sum, shift_two_sum = (
             row[0] for row in (gain_three_sum, shift_three_sum, gain_two_sum, shift_two_sum)
         )
-        cube = (GRID, GRID, slots, -1)
         grad_pre, grad_expanded, act_two, grad_middle = (
             block.reshape(cube) for block in (grad_pre, grad_expanded, act_two, grad_middle)
         )
@@ -1101,7 +1312,7 @@
         conv_rows = mid_weight.shape[0]
         if conv_rows % 32 == 0:
             small_part, reduce_part, expand_part, mid_part, diff_one, diff_two = terms_all(
-                small_terms.reshape(-1, feature_width), block_low.reshape(flat), grad_reduced.reshape(flat),
+                small_terms.reshape(-1, feature_width), block_low, grad_reduced.reshape(flat),
                 act_two.reshape(flat), grad_expanded.reshape(flat), modulated, grad_middle.reshape(flat), change,
                 grad_gate.reshape(flat),
                 [small_terms.shape[1], reduce_weight.shape[0], expand_weight.shape[0], conv_rows], fsdp, reps, 10,
@@ -1113,7 +1324,7 @@
             small_part, reduce_part, expand_part, mid_part, diff_one, diff_two = scatter_all(
                 [
                     small_terms,
-                    owned(project_terms(block_low, grad_reduced, bf16), reduce_weight),
+                    owned(project_terms(block_low.reshape(cube), grad_reduced, bf16), reduce_weight),
                     owned(project_terms(act_two, grad_expanded, bf16), expand_weight),
                     owned(convolve_terms(modulated, grad_middle, 1, 1, bf16), mid_weight),
                     owned(convolve_terms(change, grad_gate, 1, 1, bf16), diff_weight),

time: 562 us -> 514 us (0.915); the launches traced: 552 us -> 510 us
  matrix products: 112 us -> 82.7 us
  local copies, waits for them, and re-layouts: 65.7 us -> 50.4 us
  Pallas kernels: 348 us -> 362 us
  other arithmetic: 24.8 us -> 12.7 us
    pallas_call x1, Pallas kernels: 93.2 us -> 131 us  [head(): pl.pallas_call(functools.partial(head_kernel, dims, reps, sizes, stem_row...]
    pallas_call x4 -> x2, Pallas kernels: 40.3 us -> 17.8 us  [exchange(): pl.pallas_call(functools.partial(exchange_kernel, sizes, reps, moments),...]
    conv_general_dilated x4 -> x3, matrix products: 49.7 us -> 34.3 us  [convolve(): lax.conv_general_dilated(source, kernel, (1, 1), pad_of(span * stride), r...]
    dot_general x2 -> x0, matrix products: 14.6 us -> none  [project(): jnp.einsum('yxnc,cd->yxnd', source, weight, preferred_element_type=f32)]
    convert_element_type x4 -> x0, other arithmetic: 8.12 us -> none  [the longest x1 4.67 us: shards(): change = ((later_of(act_one) - act_one) * pair).astype(bf16)]
    convert_element_type x8 -> x0, local copies, waits for them, and re-layouts: 6.04 us -> none  [the longest x1 4.32 us: shards(): block_in = turned.astype(f32) + project(pool_low, lateral_full)]
    unnamed x79 -> x91, local copies, waits for them, and re-layouts: 21 us -> 20.2 us
where the time goes in v2:
time: 514 us; the launch traced here: 510 us
  Pallas kernels  362 us (70%)
  matrix products  82.7 us (16%)
  local copies, waits for them, and re-layouts  50.4 us (10%)
  other arithmetic  12.7 us (2%)
    pallas_call x1, Pallas kernels, head(): pl.pallas_call(functools.partial(head_kernel, dims, reps, sizes, stem_row...  131 us
    pallas_call x1, Pallas kernels, terms_all(): pl.pallas_call(functools.partial(terms_kernel, dims, reps, rows), out_sha...  126 us
    pallas_call x1, Pallas kernels, tail(): pl.pallas_call(functools.partial(tail_kernel, sizes, reps, clip_count), o...  88 us
    conv_general_dilated x3, matrix products, convolve(): lax.conv_general_dilated(source, kernel, (1, 1), pad_of(span * stride), r...  34.3 us
    conv_general_dilated x3, matrix products, convolve_back(): lax.conv_general_dilated(grads, kernel, (1, 1), pad_of(span * stride), rh...  30.5 us
    unnamed x91, local copies, waits for them, and re-layouts  20.2 us
    pallas_call x2, Pallas kernels, exchange(): pl.pallas_call(functools.partial(exchange_kernel, sizes, reps, moments),...  17.8 us
    dot_general x2, matrix products, project_back(): jnp.einsum('yxnd,cd->yxnc', grads, weight, preferred_element_type=f32)  14.6 us

profile of v2, /device:TPU:0, one launch (start us, length us, event | category | flops | bytes accessed | tf_op | source)
XLA Modules:
  0.0 510.5 jit_solution(11849309108536025034)
XLA Ops:
  0.7 0.7 fusion.45
  1.4 0.9 convert_element_type.85
  2.4 0.3 copy.44
  2.8 0.2 reshape.344
  3.0 0.3 pad_slice_fusion
  4.1 0.2 copy.52
  4.6 0.2 concatenate.31
  4.8 0.8 pad.39.refs_9_
  6.1 0.2 reshape.343
  6.4 0.6 pad.37.refs_0_
  7.1 0.7 broadcast_in_dim.18.refs_10_.refs_2_
  8.0 0.7 broadcast_in_dim.20.refs_11_
  8.7 0.6 convert_reduce_fusion
  9.9 0.5 broadcast_in_dim.21.refs_12_.refs_4_
  10.4 0.6 stack.85.refs_7_
  11.1 0.5 pad_maximum_fusion.1.refs_6_
  11.6 0.5 pad_maximum_fusion.2.refs_8_
  12.1 130.7 %head.1 = (bf16[64,2048]{1,0:T(8,128)(2,1)}, f32[4,2048]{1,0:T(4,128)}, bf16[16,128,512]{2,1,0:T(8,128)(2,1)}, bf16[2,16,288,512]{3,2,1,0:T(8,128)(2,1)}, bf16[1...) custom-call(bf16[32,768]{1,0:T(8,128)(2,1)} %pad.37.refs_0_, ...), custom_call_target="tpu_custom_call" | custom-call | tf_op jit(solution)/shard_map/head/pallas_call | solution.py:917
  142.8 6.8 %fusion.57 = (bf16[1,16,288,512]{3,2,1,0:T(8,128)(2,1)S(1)}, bf16[1,16,288,512]{3,2,1,0:T(8,128)(2,1)}) fusion(bf16[2,16,288,512]{3,2,1,0:T(8,128)(2,1)} %get-tuple-element.54), kind=kLoop, calls=%fused_computation.109 | loop fusion | bytes 18874368 | tf_op jit(solution)/shard_map/slice | solution.py:1263
  149.6 14.5 %fusion.64 = f32[7,7,32,512]{3,2,1,0:T(8,128)S(1)} fusion(bf16[7,7,32,512]{3,2,1,0:T(8,128)(2,1)S(1)} %bitcast.152, bf16[3,3,512,512]{3,2,1,0:T(8,128)(2,1)} %bitcast.168), kind=kOutput, calls=%fused_computation.116 | convolution fusion | flops 6056574976 | bytes 9535488 | tf_op jit(solution)/shard_map/conv_general_dilated | solution.py:1146
  164.1 0.6 fusion.60
  164.7 10.2 %multiply_convert_fusion.1 = (bf16[7,7,32,512]{3,2,1,0:T(8,128)(2,1)S(1)}, f32[7,7,32,512]{3,2,1,0:T(8,128)}) fusion(f32[7,7,32,512]{3,2,1,0:T(8,128)S(1)} %bitcast.178, f32[512]{0:T(512)S(1)} %get-tuple-element.144, f32[7,7,32,512]{3,2,1,0:T(8,128)S(1)} %fusion.64, bf16[7,7,32,512]{3,2,1,0:T(8,128)(2,1)S(1)} %bitcast.153, ...), kind=kOutput, calls=%fused_computation.18 | convolution fusion | flops 4855037952 | bytes 17565696 | tf_op jit(solution)/shard_map/conv_general_dilated | solution.py:1146
  175.0 9.6 %fusion.65 = f32[7,7,32,512]{3,2,1,0:T(8,128)} fusion(bf16[7,7,32,512]{3,2,1,0:T(8,128)(2,1)S(1)} %get-tuple-element.149.refs_5_, bf16[3,3,512,512]{3,2,1,0:T(8,128)(2,1)S(1)} %bitcast.167), kind=kOutput, calls=%fused_computation.117 | convolution fusion | flops 6056574976 | bytes 9535488 | tf_op jit(solution)/shard_map/conv_general_dilated | solution.py:1146
  184.5 0.6 fusion.58
  185.3 0.7 broadcast_in_dim.22.refs_3_
  186.0 0.4 bitcast_convert_fusion
  186.4 1.7 copy.54.refs_9_
  188.2 88.0 %tail.1 = (f32[2,49,1,2048]{3,2,1,0:T(1,128)}, f32[7,224,2048]{2,1,0:T(8,128)}, bf16[7,224,2048]{2,1,0:T(8,128)(2,1)}, bf16[7,224,512]{2,1,0:T(8,128)(2,1)}, bf1...) custom-call(f32[7,224,512]{2,1,0:T(8,128)} %bitcast.174, ...), custom_call_target="tpu_custom_call" | custom-call | tf_op jit(solution)/shard_map/tail/pallas_call | solution.py:1115
  276.2 1.2 fusion.52
  277.4 1.2 fusion.50
  278.6 14.8 %fusion.54 = (bf16[512]{0:T(512)(128)(2,1)S(1)}, bf16[7,7,32,512]{3,2,1,0:T(8,128)(2,1)S(1)}, f32[7,7,32,512]{3,2,1,0:T(8,128)S(1)}) fusion(f32[7,7,32,512]{3,2,1,0:T(8,128)} %get-tuple-element.150, f32[7,7,32,512]{3,2,1,0:T(8,128)} %bitcast.177, bf16[7,7,32,512]{3,2,1,0:T(8,128)(2,1)} %bitcast.158, bf16[3,3,512,512]{3,2,1,0:T(8,128)(2,1)} %bitcast.164), kind=kOutput, calls=%fused_computation.107 | convolution fusion | flops 6061391360 | bytes 17564672 | tf_op jit(solution)/shard_map/conv_general_dilated | solution.py:1155
  293.5 7.9 %fusion.66 = f32[7,7,32,512]{3,2,1,0:T(8,128)S(1)} fusion(bf16[7,7,32,512]{3,2,1,0:T(8,128)(2,1)S(1)} %get-tuple-element.127, bf16[3,3,512,512]{3,2,1,0:T(8,128)(2,1)S(1)} %bitcast.171), kind=kOutput, calls=%fused_computation.118 | convolution fusion | flops 6056574976 | bytes 9535488 | tf_op jit(solution)/shard_map/conv_general_dilated | solution.py:1155
  301.4 7.8 %add_multiply_fusion = f32[7,7,32,512]{3,2,1,0:T(8,128)S(1)} fusion(f32[7,7,32,512]{3,2,1,0:T(8,128)S(1)} %fusion.66, bf16[7,7,32,512]{3,2,1,0:T(8,128)(2,1)S(1)} %get-tuple-element.127, bf16[3,3,512,512]{3,2,1,0:T(8,128)(2,1)S(1)} %bitcast.163, f32[32]{0:T(128)S(1)} %broadcast_in_dim.19), kind=kOutput, calls=%fused_computation.16 | convolution fusion | flops 4850221056 | bytes 12746880 | tf_op jit(solution)/shard_map/conv_general_dilated | solution.py:1155
  309.2 0.5 pad.40
  309.7 1.4 copy-done.6
  311.1 1.0 copy-done.7
  312.1 3.6 multiply_reduce_fusion
  315.7 8.6 %sums_one.1 = (f32[1,512]{1,0:T(1,128)S(1)}, f32[1,512]{1,0:T(1,128)S(1)}) custom-call(f32[1,512]{1,0:T(1,128)S(1)} %bitcast.149, f32[1,512]{1,0:T(1,128)S(1)} %bitcast.148), custom_call_target="tpu_custom_call" | custom-call | tf_op jit(solution)/shard_map/sums_one/pallas_call | solution.py:327
  324.5 1.0 multiply_convert_fusion
  325.5 0.6 copy-done.9
  326.1 9.9 %fusion.63 = (bf16[7,7,32,2048]{3,2,1,0:T(8,128)(2,1)S(1)}, f32[7,7,32,2048]{3,2,1,0:T(8,128)}) fusion(f32[7,7,32,2048]{3,2,1,0:T(8,128)} %bitcast.157, bf16[7,7,32,512]{3,2,1,0:T(8,128)(2,1)S(1)} %multiply_convert_fusion, bf16[2048,512,1,1]{1,0,3,2:T(8,128)(2,1)S(1)} %bitcast.179), kind=kOutput, calls=%fused_computation.115 | convolution fusion | flops 3294756864 | bytes 35815424 | tf_op jit(solution)/shard_map/yxnd,cd->yxnc/dot_general | solution.py:1178
  336.0 2.7 copy-done.3
  338.7 1.3 fusion.10
  340.3 4.7 fusion.27
  345.1 1.0 multiply_reduce_fusion.1
  346.1 9.2 %sums_stem.1 = (f32[1,128]{1,0:T(1,128)S(1)}, f32[1,128]{1,0:T(1,128)S(1)}) custom-call(f32[1,128]{1,0:T(1,128)S(1)} %pad.41.refs_0_, f32[1,128]{1,0:T(1,128)S(1)} %pad.42.refs_1_), custom_call_target="tpu_custom_call" | custom-call | tf_op jit(solution)/shard_map/sums_stem/pallas_call | solution.py:327
  355.4 2.0 fusion.26
  357.4 0.6 copy.59
  358.0 0.6 reshape.363
  358.8 1.5 copy.62
  360.3 126.0 %terms.1 = (f32[16,2048]{1,0:T(8,128)}, f32[128,512]{1,0:T(8,128)}, f32[32,2048]{1,0:T(8,128)}, f32[288,512]{1,0:T(8,128)}, f32[288,512]{1,0:T(8,128)}, /*index=5*/f32[288,512]{1,0:T(8,128)}) custom-call(bf16[256,2048]{1,0:T(8,128)(2,1)} %bitcast.176, bf16[7,224,2048]{2,1,0:T(8,128)(2,1)} %get-tuple-element.74.refs_1_, bf16[7,224,512]{2,1,0:T(8,128)(2,1)} %bitcast.159, ...), custom_call_target="tpu_custom_call" | custom-call | tf_op jit(solution)/shard_map/terms/pallas_call | solution.py:585
  486.3 2.3 pad_maximum_fusion
  488.7 0.6 fusion.48
  489.3 1.5 slice.141
  490.7 1.3 slice.140
  492.1 1.2 slice_bitcast_fusion.1
  493.3 0.6 fusion.46
  493.8 0.6 fusion.47
  494.4 11.9 %copy.63 = f32[2,16,49,2048]{3,1,2,0:T(8,128)} copy(f32[2,16,49,2048]{3,1,0,2:T(8,128)} %bitcast.154) | data formatting | bytes 25690112
  506.3 0.6 convert_element_type.92
  506.8 1.2 copy.78
  508.0 0.7 copy.88
  508.7 0.8 copy.89
  509.5 0.7 copy.90
  (117 shorter events, 3.1 us)
Async XLA Ops:
  0.7 5.0 copy-start.18
  2.7 5.2 %copy-start.26 = (s32[2]{0:T(128)S(1)}, s32[2]{0:T(128)}, u32[]{:S(2)}) copy-start(s32[2]{0:T(128)} %param.21) | copy-start | bytes 28
  2.7 7.8 %copy-start.21 = (bf16[32]{0:T(256)(128)(2,1)S(1)}, bf16[32]{0:T(256)(128)(2,1)}, u32[]{:S(2)}) copy-start(bf16[32]{0:T(256)(128)(2,1)} %param.27) | copy-start | bytes 196
  2.7 7.8 %copy-start.22 = (bf16[32]{0:T(256)(128)(2,1)S(1)}, bf16[32]{0:T(256)(128)(2,1)}, u32[]{:S(2)}) copy-start(bf16[32]{0:T(256)(128)(2,1)} %param.28) | copy-start | bytes 196
  2.7 7.7 %copy-start.23 = (bf16[32]{0:T(256)(128)(2,1)S(1)}, bf16[32]{0:T(256)(128)(2,1)}, u32[]{:S(2)}) copy-start(bf16[32]{0:T(256)(128)(2,1)} %param.30) | copy-start | bytes 196
  2.7 7.7 %copy-start.24 = (bf16[32]{0:T(256)(128)(2,1)S(1)}, bf16[32]{0:T(256)(128)(2,1)}, u32[]{:S(2)}) copy-start(bf16[32]{0:T(256)(128)(2,1)} %param.32) | copy-start | bytes 196
  2.7 7.7 %copy-start.25 = (bf16[32]{0:T(256)(128)(2,1)S(1)}, bf16[32]{0:T(256)(128)(2,1)}, u32[]{:S(2)}) copy-start(bf16[32]{0:T(256)(128)(2,1)} %param.33) | copy-start | bytes 196
  2.7 8.3 %copy-start.29 = (bf16[128]{0:T(256)(128)(2,1)S(1)}, bf16[128]{0:T(256)(128)(2,1)}, u32[]{:S(2)}) copy-start(bf16[128]{0:T(256)(128)(2,1)} %param.36) | copy-start | bytes 772
  2.7 8.3 %copy-start.30 = (bf16[128]{0:T(256)(128)(2,1)S(1)}, bf16[128]{0:T(256)(128)(2,1)}, u32[]{:S(2)}) copy-start(bf16[128]{0:T(256)(128)(2,1)} %param.35) | copy-start | bytes 772
  2.7 8.8 %copy-start.31 = (bf16[4]{0:T(256)(128)(2,1)S(1)}, bf16[4]{0:T(256)(128)(2,1)}, u32[]{:S(2)}) copy-start(bf16[4]{0:T(256)(128)(2,1)} %param.24) | copy-start | bytes 28
  2.8 8.8 %copy-start.32 = (bf16[4]{0:T(256)(128)(2,1)S(1)}, bf16[4]{0:T(256)(128)(2,1)}, u32[]{:S(2)}) copy-start(bf16[4]{0:T(256)(128)(2,1)} %param.23) | copy-start | bytes 28
  142.8 6.8 %copy-start = (bf16[7,224,512]{2,1,0:T(8,128)(2,1)S(1)}, bf16[7,224,512]{2,1,0:T(8,128)(2,1)}, u32[]{:S(2)}) copy-start(bf16[7,224,512]{2,1,0:T(8,128)(2,1)} %get-tuple-element.53) | copy-start | bytes 4816900
  149.6 15.2 %copy-start.5 = (bf16[1,16,288,512]{3,2,1,0:T(8,128)(2,1)}, bf16[1,16,288,512]{3,2,1,0:T(8,128)(2,1)S(1)}, u32[]{:S(2)}) copy-start(bf16[1,16,288,512]{3,2,1,0:T(8,128)(2,1)S(1)} %get-tuple-element.128) | copy-start | bytes 14155780
  149.6 14.5 %copy-start.17 = (f32[4,2048]{1,0:T(4,128)S(1)}, f32[4,2048]{1,0:T(4,128)}, u32[]{:S(2)}) copy-start(f32[4,2048]{1,0:T(4,128)} %get-tuple-element.55) | copy-start | bytes 98308
  149.6 15.1 %copy-start.8 = (f32[7,224,512]{2,1,0:T(8,128)S(1)}, f32[7,224,512]{2,1,0:T(8,128)}, u32[]{:S(2)}) copy-start(f32[7,224,512]{2,1,0:T(8,128)} %get-tuple-element.52) | copy-start | bytes 9633796
  149.6 25.4 %slice-start.2 = ((s8[4718592]{0:T(1024)(128)(4,1)}), s8[4194304]{0:T(1024)(128)(4,1)S(1)}, s32[]{:S(2)}) async-start(s8[4718592]{0:T(1024)(128)(4,1)} %bitcast.165), calls=%async_computation.2 | async-start | bytes 8388608
  164.7 10.2 %slice-start.3 = ((s8[4718592]{0:T(1024)(128)(4,1)}), s8[524288]{0:T(1024)(128)(4,1)S(1)}, s32[]{:S(2)}) async-start(s8[4718592]{0:T(1024)(128)(4,1)} %bitcast.165), calls=%async_computation.3 | async-start | bytes 1048576
  174.9 9.6 %copy-start.1 = (bf16[7,7,32,512]{3,2,1,0:T(8,128)(2,1)}, bf16[7,7,32,512]{3,2,1,0:T(8,128)(2,1)S(1)}, u32[]{:S(2)}) copy-start(bf16[7,7,32,512]{3,2,1,0:T(8,128)(2,1)S(1)} %get-tuple-element.149.refs_5_) | copy-start | bytes 4816900
  174.9 11.0 %copy-start.13 = (bf16[2,49,2048]{2,0,1:T(2,128)(2,1)S(1)}, bf16[2,49,2048]{2,0,1:T(2,128)(2,1)}, u32[]{:S(2)}) copy-start(bf16[2,49,2048]{2,0,1:T(2,128)(2,1)} %param.37) | copy-start | bytes 1204228
  188.2 105.3 %slice-start.4 = ((s8[4718592]{0:T(1024)(128)(4,1)}), s8[524288]{0:T(1024)(128)(4,1)S(1)}, s32[]{:S(2)}) async-start(s8[4718592]{0:T(1024)(128)(4,1)} %bitcast.169), calls=%async_computation.4 | async-start | bytes 1048576
  278.6 14.9 %slice-start.5 = ((s8[4718592]{0:T(1024)(128)(4,1)}), s8[4194304]{0:T(1024)(128)(4,1)S(1)}, s32[]{:S(2)}) async-start(s8[4718592]{0:T(1024)(128)(4,1)} %bitcast.169), calls=%async_computation.5 | async-start | bytes 8388608
  278.6 22.8 %slice-start = ((s8[4718592]{0:T(1024)(128)(4,1)}), s8[4194304]{0:T(1024)(128)(4,1)S(1)}, s32[]{:S(2)}) async-start(s8[4718592]{0:T(1024)(128)(4,1)} %bitcast.161), calls=%async_computation | async-start | bytes 8388608
  293.4 7.9 %copy-start.2 = (bf16[7,7,32,512]{3,2,1,0:T(8,128)(2,1)}, bf16[7,7,32,512]{3,2,1,0:T(8,128)(2,1)S(1)}, u32[]{:S(2)}) copy-start(bf16[7,7,32,512]{3,2,1,0:T(8,128)(2,1)S(1)} %get-tuple-element.127) | copy-start | bytes 4816900
  293.5 7.9 %slice-start.1 = ((s8[4718592]{0:T(1024)(128)(4,1)}), s8[524288]{0:T(1024)(128)(4,1)S(1)}, s32[]{:S(2)}) async-start(s8[4718592]{0:T(1024)(128)(4,1)} %bitcast.161), calls=%async_computation.1 | async-start | bytes 1048576
  309.2 1.9 copy-start.6
  309.2 2.9 copy-start.7
  312.1 12.2 %copy-start.19 = (f32[1,128]{1,0:T(1,128)S(1)}, f32[1,128]{1,0:T(1,128)}, u32[]{:S(2)}) copy-start(f32[1,128]{1,0:T(1,128)} %get-tuple-element.65) | copy-start | bytes 1540
  312.1 12.3 %copy-start.20 = (f32[1,512]{1,0:T(1,128)S(1)}, f32[1,512]{1,0:T(1,128)}, u32[]{:S(2)}) copy-start(f32[1,512]{1,0:T(1,128)} %get-tuple-element.61) | copy-start | bytes 6148
  324.5 1.6 copy-start.9
  325.5 10.5 %copy-start.4 = (bf16[7,7,32,512]{3,2,1,0:T(8,128)(2,1)}, bf16[7,7,32,512]{3,2,1,0:T(8,128)(2,1)S(1)}, u32[]{:S(2)}) copy-start(bf16[7,7,32,512]{3,2,1,0:T(8,128)(2,1)S(1)} %multiply_convert_fusion) | copy-start | bytes 4816900
  326.1 12.6 %copy-start.14 = (bf16[7,7,32,64]{3,2,1,0:T(8,128)(2,1)S(1)}, bf16[7,7,32,64]{3,2,1,0:T(8,128)(2,1)}, u32[]{:S(2)}) copy-start(bf16[7,7,32,64]{3,2,1,0:T(8,128)(2,1)} %get-tuple-element.68) | copy-start | bytes 602116
  336.0 2.7 copy-start.3
  338.7 1.6 copy-start.28
  340.3 4.8 copy-start.11
  340.3 15.0 %copy-start.27 = (f32[1,64]{1,0:T(1,128)S(1)}, f32[1,64]{1,0:T(1,128)}, u32[]{:S(2)}) copy-start(f32[1,64]{1,0:T(1,128)} %get-tuple-element.69) | copy-start | bytes 772
  494.4 11.9 %copy-start.10 = (f32[2,49,1,2048]{3,2,1,0:T(1,128)S(1)}, f32[2,49,1,2048]{3,2,1,0:T(1,128)}, u32[]{:S(2)}) copy-start(f32[2,49,1,2048]{3,2,1,0:T(1,128)} %get-tuple-element.59) | copy-start | bytes 2408452
  494.4 13.6 %copy-start.16 = (f32[128,512]{1,0:T(8,128)S(1)}, f32[128,512]{1,0:T(8,128)}, u32[]{:S(2)}) copy-start(f32[128,512]{1,0:T(8,128)} %get-tuple-element.186) | copy-start | bytes 786436
  506.3 2.4 copy-start.12
  506.3 3.3 copy-start.15

commit v3 on v2

--- a/solution.py
+++ b/solution.py
@@ -508,7 +508,7 @@
             source.at[:, :, j * step : (j + 1) * step], chunk.at[number % 2], chunk_sem.at[number % 2]
         )
 
-    gradients = [grad_reduced, act_two, grad_middle, grad_gate]
+    gradients = [grad_reduced, grad_middle, grad_gate, act_two]
 
     def turn(number):
         pltpu.make_async_copy(gradients[number], line, line_sem).wait()
@@ -526,29 +526,25 @@
         pltpu.make_async_copy(source, pads.at[index, inner, inner], pad_sem.at[index]).start()
     place.greet()
 
-    small_copy.wait()
-    scatter.cores(0)
-    turn(0)
-    for j in range(chunks):
-        if j + 1 < len(sources):
-            load(j + 1).start()
-        load(j).wait()
-        values = dot(turned[...], chunk[j % 2].reshape(-1, step))
-        terms[1][j * step : (j + 1) * step, :] = jnp.transpose(values).astype(bf16)
-    scatter.cores(1)
-    scatter.hop(0, 0)
-    turn(1)
-    for j in range(chunks):
-        number = chunks + j
+    def flow(*hops):
+        for k, lag in hops:
+            scatter.hop(k, lag)
+
+    def piece(number):
         if number + 1 < len(sources):
             load(number + 1).start()
         load(number).wait()
-        terms[2][:, j * step : (j + 1) * step] = dot(turned[...], chunk[number % 2].reshape(-1, step)).astype(bf16)
-    scatter.cores(2)
-    scatter.hop(1, 0)
-    scatter.hop(0, 1)
-
-    def taps(k, pad, stride):
+        return dot(turned[...], chunk[number % 2].reshape(-1, step))
+
+    def reduce_pieces(first, last):
+        for j in range(first, last):
+            terms[1][j * step : (j + 1) * step, :] = jnp.transpose(piece(j)).astype(bf16)
+
+    def expand_pieces(first, last):
+        for j in range(first, last):
+            terms[2][:, j * step : (j + 1) * step] = piece(chunks + j).astype(bf16)
+
+    def taps(k, pad, stride, first, last):
         def tap(t, _):
             top = ring + (t // 3 - 1) * stride
             left = ring + (t % 3 - 1) * stride
@@ -558,19 +554,48 @@
             terms[k][pl.ds(start, mid_width), :] = jnp.transpose(values).astype(bf16)
             return 0
 
-        lax.fori_loop(0, 9, tap, 0)
-        scatter.cores(k)
-
-    for k, pad, stride in ((3, 0, 1), (4, 1, 1), (5, 1, 2)):
-        if k < 5:
-            turn(k - 1)
-            pltpu.make_async_copy((modulated, change)[pad], pads.at[pad, inner, inner], pad_sem.at[pad]).wait()
-        taps(k, pad, stride)
-        for lag in range(4):
-            scatter.hop(k - 1 - lag, lag)
-    for k in range(6, 10):
-        for lag in range(4):
-            scatter.hop(k - 1 - lag, lag)
+        lax.fori_loop(first, last, tap, 0)
+
+    def padded(pad):
+        pltpu.make_async_copy((modulated, change)[pad], pads.at[pad, inner, inner], pad_sem.at[pad]).wait()
+
+    half = chunks // 2
+    small_copy.wait()
+    scatter.cores(0)
+    turn(0)
+    reduce_pieces(0, half)
+    flow((0, 0))
+    reduce_pieces(half, chunks)
+    scatter.cores(1)
+    turn(1)
+    padded(0)
+    taps(3, 0, 1, 0, 3)
+    flow((1, 0), (0, 1))
+    taps(3, 0, 1, 3, 6)
+    flow((1, 1), (0, 2))
+    taps(3, 0, 1, 6, 9)
+    scatter.cores(3)
+    turn(2)
+    padded(1)
+    flow((1, 2), (0, 3))
+    taps(4, 1, 1, 0, 3)
+    flow((3, 0))
+    taps(4, 1, 1, 3, 6)
+    flow((1, 3))
+    taps(4, 1, 1, 6, 9)
+    scatter.cores(4)
+    taps(5, 1, 2, 0, 3)
+    flow((4, 0), (3, 1))
+    taps(5, 1, 2, 3, 6)
+    taps(5, 1, 2, 6, 9)
+    scatter.cores(5)
+    turn(3)
+    flow((3, 2))
+    expand_pieces(0, half)
+    flow((5, 0), (4, 1))
+    expand_pieces(half, chunks)
+    scatter.cores(2)
+    flow((3, 3), (4, 2), (2, 0), (5, 1), (2, 1), (4, 3), (5, 2), (2, 2), (5, 3), (2, 3))
     scatter.finish(totals)
 
 
@@ -761,14 +786,20 @@
     small_rows.append(jnp.zeros((small_own.shape[0] - taken, width), f32))
     small_own[...] = jnp.concatenate(small_rows, axis=0).astype(bf16)
     gather.place.greet(over.peers)
-    for k in range(3):
-        gather.begin(k)
+    gather.begin(0)
+    gather.begin(1)
+    gather.begin(2)
+    gather.begin(3)
+    gather.begin(4)
+    gather.begin(5)
+    gather.begin(6)
     stem_act[...] = jnp.zeros(stem_act.shape, f32)
-    for lag in range(3):
-        gather.hop(0, lag)
-        gather.hop(1, lag)
-    for k in range(3, 7):
-        gather.begin(k)
+    gather.hop(0, 0)
+    gather.hop(1, 0)
+    gather.hop(0, 1)
+    gather.hop(1, 1)
+    gather.hop(0, 2)
+    gather.hop(1, 2)
     gather.hop(0, 3)
     gather.hop(1, 3)
     vectors = jnp.zeros((taken - stem_rows, width), f32)
@@ -792,6 +823,8 @@
     start = mid_width * narrow.shape[0]
     stem_gain, stem_shift = vector(start, stem_width), vector(start + least.shape[1], stem_width)
     gather.hop(2, 0)
+    gather.hop(3, 0)
+    gather.hop(2, 1)
 
     def stem_column(x, _):
         stem_values[x] = dot_t(lhs[...], tap_rows[x].astype(bf16))
@@ -800,14 +833,16 @@
     lax.fori_loop(0, GRID, stem_column, 0)
     origin = stem_values[0, 0:1, :]
     carry = lax.fori_loop(0, GRID, lambda x, c: add_moments(c, stem_values[x], origin), blank(stem_width))
-    gather.hop(3, 0)
-    gather.hop(2, 1)
+    gather.hop(4, 0)
+    gather.hop(3, 1)
     total, squares, number = over.total(0, moments(carry, origin), True)
     number_out[...] = number
     number = number[:, :1]
     centre, inverse = total / number, lax.rsqrt(squares / number + epsilon)
     stem_inverse[...] = inverse
+    gather.hop(5, 0)
     gather.hop(2, 2)
+    gather.hop(4, 1)
 
     def stem_norm(x, _):
         normed = (stem_values[x] - centre) * inverse
@@ -825,11 +860,9 @@
         return 0
 
     lax.fori_loop(0, GRID, stem_pool, 0)
-    gather.hop(4, 0)
-    gather.hop(3, 1)
     gather.hop(2, 3)
 
-    later = [(5, 0), (4, 1), (3, 2), (6, 0), (5, 1), (4, 2)]
+    later = [[], [(6, 0)], [(5, 1)], [], [(6, 1)], [(3, 2)], [], [(4, 2)]]
     for j in range(chunks):
         slot = j % 2
         cols = slice(j * step, (j + 1) * step)
@@ -859,8 +892,8 @@
         lax.fori_loop(0, lines, line, 0)
         out_wide.start()
         out_low.start()
-        if j < len(later):
-            gather.hop(*later[j])
+        for k, lag in later[j] if j < len(later) else ():
+            gather.hop(k, lag)
     pltpu.make_async_copy(reduce_full, reduce_out, out_sem).start()
 
     origin = reduced[0, 0:1, :]
@@ -868,7 +901,6 @@
     total, squares, _ = over.total(1, moments(carry, origin), True)
     centre, inverse = total / number, lax.rsqrt(squares / number + epsilon)
     inverse_one[...] = inverse
-    gather.hop(6, 1)
     gather.hop(5, 2)
 
     def first(y, _):
@@ -1131,6 +1163,92 @@
         compiler_params=pltpu.CompilerParams(collective_id=collective_id, has_side_effects=True, vmem_limit_bytes=VMEM_LIMIT),
         name="tail",
     )(middle, expand, valid, spread, count, gain_two, shift_two, gain_three, shift_three, pooled_grad, block_in)
+
+
+def back_kernel(clips, *refs):
+    grad_reduced, reduce_full, pool_low, lateral, grad_pre = refs[:5]
+    features_grad, lateral_terms, grad_act = refs[5:8]
+    loaded, sums, low, total, load_sem, out_sem = refs[8:]
+    lines, rows, mid_width = grad_reduced.shape
+    width = reduce_full.shape[0]
+    groups = GRID
+    slots = rows // groups
+    segs = slots // clips
+    step = 512
+
+    def load(y):
+        return pltpu.make_async_copy(grad_pre.at[y], loaded.at[y % 2], load_sem.at[y % 2])
+
+    def store(y):
+        slot = y % 2
+        return [
+            pltpu.make_async_copy(
+                sums.at[slot, :, clip * segs : (clip + 1) * segs, :],
+                features_grad.at[clip, pl.ds(y * groups, groups)],
+                out_sem.at[slot, clip],
+            )
+            for clip in range(clips)
+        ]
+
+    load(0).start()
+    total[...] = jnp.zeros(total.shape, f32)
+
+    def line(y, _):
+        slot = y % 2
+        load(y).wait()
+
+        @pl.when(y + 1 < lines)
+        def _():
+            load(y + 1).start()
+
+        @pl.when(y >= 2)
+        def _():
+            for copy in store(y - 2):
+                copy.wait()
+
+        for start in range(0, width, step):
+            cols = slice(start, start + step)
+            values = loaded[slot, :, cols] + dot_t(grad_reduced[y], reduce_full[cols, :])
+            sums[slot, :, :, cols] = values.reshape(groups, slots, step)
+            low[:, cols] = values.astype(bf16)
+        for copy in store(y):
+            copy.start()
+        grad_act[y] = dot_t(low[...], lateral[...])
+        turned = jnp.transpose(pool_low[y])
+        for start in range(0, width, step):
+            cols = slice(start, start + step)
+            total[:, cols] += dot(turned, low[:, cols])
+        return 0
+
+    lax.fori_loop(0, lines, line, 0)
+    lateral_terms[...] = total[...].astype(bf16)
+    for y in (lines - 2, lines - 1):
+        for copy in store(y):
+            copy.wait()
+
+
+def back(grad_reduced, reduce_full, pool_low, lateral, grad_pre, clips):
+    lines, rows, mid_width = grad_reduced.shape
+    width = reduce_full.shape[0]
+    slots = rows // GRID
+    stem_width = lateral.shape[0]
+    shape = jax.ShapeDtypeStruct
+    return pl.pallas_call(
+        functools.partial(back_kernel, clips),
+        out_shape=[
+            shape((clips, lines * GRID, slots // clips, width), f32), shape((stem_width, width), bf16),
+            shape((lines, rows, stem_width), f32),
+        ],
+        in_specs=[IN_VMEM] * 4 + [ANY],
+        out_specs=[ANY, IN_VMEM, IN_VMEM],
+        scratch_shapes=[
+            pltpu.VMEM((2, rows, width), f32), pltpu.VMEM((2, GRID, slots, width), f32), pltpu.VMEM((rows, width), bf16),
+            pltpu.VMEM((stem_width, width), f32), DMA((2,)), DMA((2, clips)),
+        ],
+        compiler_params=pltpu.CompilerParams(vmem_limit_bytes=VMEM_LIMIT),
+        cost_estimate=pl.CostEstimate(flops=4 * lines * rows * width * mid_width, bytes_accessed=8 * lines * rows * width, transcendentals=0),
+        name="back",
+    )(grad_reduced, reduce_full, pool_low, lateral, grad_pre)
 
 
 ORDER = ("HWNC", "HWIO", "HWNC")
@@ -1287,10 +1405,10 @@
         grad_reduced, gain_one_sum, shift_one_sum = norm_back(
             gelu_back(zeta_one, grad_act_one), normed_one, stats_one, gain_one_full, 8, "sums_one"
         )
-        features_grad = grad_pre + project_back(grad_reduced, reduce_full)
-        grad_lateral = features_grad.astype(bf16)
-        lateral_terms = project_terms(pool_low, grad_lateral, bf16)
-        grad_act = pool_mean(project_back(grad_lateral, lateral_full))
+        features_grad, lateral_terms, grad_act = back(
+            grad_reduced.reshape(flat), reduce_full, pool_low.reshape(flat), lateral_full, grad_pre.reshape(flat), clip_count
+        )
+        grad_act = pool_mean(grad_act.reshape(cube))
         grad_stem, stem_gain_sum, stem_shift_sum = norm_back(
             gelu_back(stem_norm, grad_act), stem_normed, stem_stats, stem_gain_full, 9, "sums_stem"
         )
@@ -1337,7 +1455,7 @@
             share = whole.shape[0] // fsdp
             return lax.dynamic_slice_in_dim(whole, lax.axis_index("fsdp") * share, share)
 
-        out = jnp.transpose(features_grad, (2, 0, 1, 3)).reshape(features.shape)
+        out = jnp.transpose(features_grad, (0, 2, 1, 3))
         return (
             pooled,
             out,

time: 514 us -> 482 us (0.938)
  matrix products: 82.7 us -> 66.9 us
  local copies, waits for them, and re-layouts: 50.4 us -> 35.2 us
    dot_general x3 -> x0, matrix products: 15.9 us -> none  [the longest x2 14.6 us: project_back(): jnp.einsum('yxnd,cd->yxnc', grads, weight, preferred_element_type=f32)]
    pallas_call x0 -> x1, Pallas kernels: none -> 15.9 us  [back(): pl.pallas_call(functools.partial(back_kernel, clips), out_shape=[shape((c...]
    unnamed x91 -> x82, local copies, waits for them, and re-layouts: 20.2 us -> 4.71 us
    pallas_call x1, Pallas kernels: 131 us -> 120 us  [head(): pl.pallas_call(functools.partial(head_kernel, dims, reps, sizes, stem_row...]
    pallas_call x1, Pallas kernels: 126 us -> 117 us  [terms_all(): pl.pallas_call(functools.partial(terms_kernel, dims, reps, rows), out_sha...]
where the time goes in v3:
time: 482 us; the launch traced here: 478 us
  Pallas kernels  358 us (74%)
  matrix products  66.9 us (14%)
  local copies, waits for them, and re-layouts  35.2 us (7%)
  other arithmetic  15.5 us (3%)
    pallas_call x1, Pallas kernels, head(): pl.pallas_call(functools.partial(head_kernel, dims, reps, sizes, stem_row...  120 us
    pallas_call x1, Pallas kernels, terms_all(): pl.pallas_call(functools.partial(terms_kernel, dims, reps, rows), out_sha...  117 us
    pallas_call x1, Pallas kernels, tail(): pl.pallas_call(functools.partial(tail_kernel, sizes, reps, clip_count), o...  87.8 us
    conv_general_dilated x3, matrix products, convolve(): lax.conv_general_dilated(source, kernel, (1, 1), pad_of(span * stride), r...  34.1 us
    conv_general_dilated x3, matrix products, convolve_back(): lax.conv_general_dilated(grads, kernel, (1, 1), pad_of(span * stride), rh...  30.8 us
    pallas_call x2, Pallas kernels, exchange(): pl.pallas_call(functools.partial(exchange_kernel, sizes, reps, moments),...  17.8 us
    pallas_call x1, Pallas kernels, back(): pl.pallas_call(functools.partial(back_kernel, clips), out_shape=[shape((c...  15.9 us

profile of v3, /device:TPU:0, one launch (start us, length us, event | category | flops | bytes accessed | tf_op | source)
XLA Modules:
  0.0 478.1 jit_solution(10077416514358071856)
XLA Ops:
  0.7 0.7 fusion.37
  1.4 0.9 convert_element_type.82
  2.4 0.3 copy.41
  2.8 0.2 reshape.345
  3.0 0.3 pad_slice_fusion
  3.3 0.2 copy.43
  3.4 0.2 copy.44
  3.6 0.2 copy.45
  3.8 0.2 copy.47
  4.0 0.2 copy.48
  4.1 0.2 copy.49
  4.6 0.2 concatenate.31
  4.8 0.8 pad.39.refs_9_
  6.1 0.2 reshape.344
  6.4 0.6 pad.37.refs_0_
  7.1 0.7 broadcast_in_dim.18.refs_10_.refs_2_
  8.0 0.7 broadcast_in_dim.20.refs_11_
  8.7 0.6 convert_reduce_fusion
  9.9 0.5 broadcast_in_dim.21.refs_12_.refs_4_
  10.4 0.6 stack.85.refs_7_
  11.1 0.5 pad_maximum_fusion.1.refs_6_
  11.6 0.5 pad_maximum_fusion.2.refs_8_
  12.1 120.0 %head.1 = (bf16[64,2048]{1,0:T(8,128)(2,1)}, f32[4,2048]{1,0:T(4,128)}, bf16[16,128,512]{2,1,0:T(8,128)(2,1)}, bf16[2,16,288,512]{3,2,1,0:T(8,128)(2,1)}, bf16[1...) custom-call(bf16[32,768]{1,0:T(8,128)(2,1)} %pad.37.refs_0_, ...), custom_call_target="tpu_custom_call" | custom-call | tf_op jit(solution)/shard_map/head/pallas_call | solution.py:949
  132.1 6.8 %fusion.49 = (bf16[1,16,288,512]{3,2,1,0:T(8,128)(2,1)S(1)}, bf16[1,16,288,512]{3,2,1,0:T(8,128)(2,1)}) fusion(bf16[2,16,288,512]{3,2,1,0:T(8,128)(2,1)} %get-tuple-element.57), kind=kLoop, calls=%fused_computation.102 | loop fusion | bytes 18874368 | tf_op jit(solution)/shard_map/slice | solution.py:1381
  138.9 14.3 %fusion.55 = f32[7,7,32,512]{3,2,1,0:T(8,128)S(1)} fusion(bf16[7,7,32,512]{3,2,1,0:T(8,128)(2,1)S(1)} %bitcast.135, bf16[3,3,512,512]{3,2,1,0:T(8,128)(2,1)} %bitcast.148), kind=kOutput, calls=%fused_computation.108 | convolution fusion | flops 6056574976 | bytes 9535488 | tf_op jit(solution)/shard_map/conv_general_dilated | solution.py:1264
  153.3 0.6 fusion.52
  153.9 10.2 %multiply_convert_fusion.1 = (bf16[7,7,32,512]{3,2,1,0:T(8,128)(2,1)S(1)}, f32[7,7,32,512]{3,2,1,0:T(8,128)}) fusion(f32[7,7,32,512]{3,2,1,0:T(8,128)S(1)} %bitcast.160, f32[512]{0:T(512)S(1)} %get-tuple-element.133, f32[7,7,32,512]{3,2,1,0:T(8,128)S(1)} %fusion.55, bf16[7,7,32,512]{3,2,1,0:T(8,128)(2,1)S(1)} %bitcast.136, ...), kind=kOutput, calls=%fused_computation.15 | convolution fusion | flops 4855037952 | bytes 17565696 | tf_op jit(solution)/shard_map/conv_general_dilated | solution.py:1264
  164.1 9.6 %fusion.56 = f32[7,7,32,512]{3,2,1,0:T(8,128)} fusion(bf16[7,7,32,512]{3,2,1,0:T(8,128)(2,1)S(1)} %get-tuple-element.138.refs_5_, bf16[3,3,512,512]{3,2,1,0:T(8,128)(2,1)S(1)} %bitcast.147), kind=kOutput, calls=%fused_computation.109 | convolution fusion | flops 6056574976 | bytes 9535488 | tf_op jit(solution)/shard_map/conv_general_dilated | solution.py:1264
  173.7 0.6 fusion.50
  174.5 0.7 broadcast_in_dim.22.refs_3_
  175.1 0.4 bitcast_convert_fusion
  175.6 1.7 copy.51.refs_9_
  177.3 87.8 %tail.1 = (f32[2,49,1,2048]{3,2,1,0:T(1,128)}, f32[7,224,2048]{2,1,0:T(8,128)}, bf16[7,224,2048]{2,1,0:T(8,128)(2,1)}, bf16[7,224,512]{2,1,0:T(8,128)(2,1)}, bf1...) custom-call(f32[7,224,512]{2,1,0:T(8,128)} %bitcast.154, ...), custom_call_target="tpu_custom_call" | custom-call | tf_op jit(solution)/shard_map/tail/pallas_call | solution.py:1147
  265.1 1.2 fusion.44
  266.3 1.2 fusion.42
  267.6 15.0 %fusion.46 = (bf16[512]{0:T(512)(128)(2,1)S(1)}, bf16[7,7,32,512]{3,2,1,0:T(8,128)(2,1)S(1)}, f32[7,7,32,512]{3,2,1,0:T(8,128)S(1)}) fusion(f32[7,7,32,512]{3,2,1,0:T(8,128)} %get-tuple-element.139, f32[7,7,32,512]{3,2,1,0:T(8,128)} %bitcast.159, bf16[7,7,32,512]{3,2,1,0:T(8,128)(2,1)} %bitcast.139, bf16[3,3,512,512]{3,2,1,0:T(8,128)(2,1)} %bitcast.144), kind=kOutput, calls=%fused_computation.100 | convolution fusion | flops 6061391360 | bytes 17564672 | tf_op jit(solution)/shard_map/conv_general_dilated | solution.py:1273
  282.6 7.9 %fusion.57 = f32[7,7,32,512]{3,2,1,0:T(8,128)S(1)} fusion(bf16[7,7,32,512]{3,2,1,0:T(8,128)(2,1)S(1)} %get-tuple-element.116, bf16[3,3,512,512]{3,2,1,0:T(8,128)(2,1)S(1)} %bitcast.151), kind=kOutput, calls=%fused_computation.110 | convolution fusion | flops 6056574976 | bytes 9535488 | tf_op jit(solution)/shard_map/conv_general_dilated | solution.py:1273
  290.6 7.9 %add_multiply_fusion = f32[7,7,32,512]{3,2,1,0:T(8,128)S(1)} fusion(f32[7,7,32,512]{3,2,1,0:T(8,128)S(1)} %fusion.57, bf16[7,7,32,512]{3,2,1,0:T(8,128)(2,1)S(1)} %get-tuple-element.116, bf16[3,3,512,512]{3,2,1,0:T(8,128)(2,1)S(1)} %bitcast.143, f32[32]{0:T(128)S(1)} %broadcast_in_dim.19), kind=kOutput, calls=%fused_computation.13 | convolution fusion | flops 4850221056 | bytes 12746880 | tf_op jit(solution)/shard_map/conv_general_dilated | solution.py:1273
  298.5 0.8 pad.40
  299.3 1.1 copy-done.4
  300.4 1.0 copy-done.5
  301.4 4.0 multiply_reduce_fusion
  305.4 9.1 %sums_one.1 = (f32[1,512]{1,0:T(1,128)S(1)}, f32[1,512]{1,0:T(1,128)S(1)}) custom-call(f32[1,512]{1,0:T(1,128)S(1)} %bitcast.132, f32[1,512]{1,0:T(1,128)S(1)} %bitcast.131), custom_call_target="tpu_custom_call" | custom-call | tf_op jit(solution)/shard_map/sums_one/pallas_call | solution.py:327
  314.6 2.2 multiply_convert_fusion
  316.8 15.9 %back.1 = (f32[2,49,16,2048]{3,2,1,0:T(8,128)}, bf16[64,2048]{1,0:T(8,128)(2,1)}, f32[7,224,64]{2,1,0:T(8,128)}) custom-call(bf16[7,224,512]{2,1,0:T(8,128)(2,1)} %bitcast.156, bf16[2048,512]{1,0:T(8,128)(2,1)} %bitcast.192, bf16[7,224,64]{2,1,0:T(8,128)(2,1)} %bitcast.193, bf16[64,2048]{1,0:T(8,128)(2,1)} %get-tuple-element.71.refs_3_, ...), custom_call_target="tpu_custom_call" | custom-call | flops 6576668672 | bytes 25690112 | tf_op jit(solution)/shard_map/back/pallas_call | solution.py:1236
  332.7 2.2 multiply_reduce_fusion.1
  334.9 8.7 %sums_stem.1 = (f32[1,128]{1,0:T(1,128)S(1)}, f32[1,128]{1,0:T(1,128)S(1)}) custom-call(f32[1,128]{1,0:T(1,128)S(1)} %pad.41.refs_0_, f32[1,128]{1,0:T(1,128)S(1)} %pad.42.refs_1_), custom_call_target="tpu_custom_call" | custom-call | tf_op jit(solution)/shard_map/sums_stem/pallas_call | solution.py:327
  343.8 2.0 fusion.20
  345.8 0.6 copy.54
  346.3 0.6 reshape.365
  347.4 1.5 copy.57
  349.0 116.8 %terms.1 = (f32[16,2048]{1,0:T(8,128)}, f32[128,512]{1,0:T(8,128)}, f32[32,2048]{1,0:T(8,128)}, f32[288,512]{1,0:T(8,128)}, f32[288,512]{1,0:T(8,128)}, /*index=5*/f32[288,512]{1,0:T(8,128)}) custom-call(bf16[256,2048]{1,0:T(8,128)(2,1)} %bitcast.158, bf16[7,224,2048]{2,1,0:T(8,128)(2,1)} %get-tuple-element.80.refs_1_, bf16[7,224,512]{2,1,0:T(8,128)(2,1)} %bitcast.157, ...), custom_call_target="tpu_custom_call" | custom-call | tf_op jit(solution)/shard_map/terms/pallas_call | solution.py:610
  465.8 2.4 pad_maximum_fusion
  468.2 0.6 fusion.40
  468.8 1.5 slice.141
  470.2 1.3 slice.140
  471.6 1.2 slice_bitcast_fusion.1
  472.8 0.6 fusion.38
  473.3 0.6 fusion.39
  473.9 0.6 convert_element_type.89
  474.5 1.2 copy.63
  475.6 0.7 copy.73
  476.3 0.8 copy.74
  477.2 0.7 copy.75
  (106 shorter events, 2.2 us)
Async XLA Ops:
  0.7 5.0 %copy-start.15 = (bf16[4,588]{1,0:T(4,128)(2,1)S(1)}, bf16[4,588]{1,0:T(4,128)(2,1)}, u32[]{:S(2)}) copy-start(bf16[4,588]{1,0:T(4,128)(2,1)} %param.22) | copy-start | bytes 14116
  2.7 5.2 %copy-start.23 = (s32[2]{0:T(128)S(1)}, s32[2]{0:T(128)}, u32[]{:S(2)}) copy-start(s32[2]{0:T(128)} %param.21) | copy-start | bytes 28
  2.7 7.8 %copy-start.18 = (bf16[32]{0:T(256)(128)(2,1)S(1)}, bf16[32]{0:T(256)(128)(2,1)}, u32[]{:S(2)}) copy-start(bf16[32]{0:T(256)(128)(2,1)} %param.27) | copy-start | bytes 196
  2.7 7.8 %copy-start.19 = (bf16[32]{0:T(256)(128)(2,1)S(1)}, bf16[32]{0:T(256)(128)(2,1)}, u32[]{:S(2)}) copy-start(bf16[32]{0:T(256)(128)(2,1)} %param.28) | copy-start | bytes 196
  2.7 7.7 %copy-start.20 = (bf16[32]{0:T(256)(128)(2,1)S(1)}, bf16[32]{0:T(256)(128)(2,1)}, u32[]{:S(2)}) copy-start(bf16[32]{0:T(256)(128)(2,1)} %param.30) | copy-start | bytes 196
  2.7 7.7 %copy-start.21 = (bf16[32]{0:T(256)(128)(2,1)S(1)}, bf16[32]{0:T(256)(128)(2,1)}, u32[]{:S(2)}) copy-start(bf16[32]{0:T(256)(128)(2,1)} %param.32) | copy-start | bytes 196
  2.7 7.7 %copy-start.22 = (bf16[32]{0:T(256)(128)(2,1)S(1)}, bf16[32]{0:T(256)(128)(2,1)}, u32[]{:S(2)}) copy-start(bf16[32]{0:T(256)(128)(2,1)} %param.33) | copy-start | bytes 196
  2.7 8.3 %copy-start.25 = (bf16[128]{0:T(256)(128)(2,1)S(1)}, bf16[128]{0:T(256)(128)(2,1)}, u32[]{:S(2)}) copy-start(bf16[128]{0:T(256)(128)(2,1)} %param.36) | copy-start | bytes 772
  2.7 8.3 %copy-start.26 = (bf16[128]{0:T(256)(128)(2,1)S(1)}, bf16[128]{0:T(256)(128)(2,1)}, u32[]{:S(2)}) copy-start(bf16[128]{0:T(256)(128)(2,1)} %param.35) | copy-start | bytes 772
  2.7 8.8 %copy-start.27 = (bf16[4]{0:T(256)(128)(2,1)S(1)}, bf16[4]{0:T(256)(128)(2,1)}, u32[]{:S(2)}) copy-start(bf16[4]{0:T(256)(128)(2,1)} %param.24) | copy-start | bytes 28
  2.8 8.8 %copy-start.28 = (bf16[4]{0:T(256)(128)(2,1)S(1)}, bf16[4]{0:T(256)(128)(2,1)}, u32[]{:S(2)}) copy-start(bf16[4]{0:T(256)(128)(2,1)} %param.23) | copy-start | bytes 28
  132.1 6.8 %copy-start = (bf16[7,224,512]{2,1,0:T(8,128)(2,1)S(1)}, bf16[7,224,512]{2,1,0:T(8,128)(2,1)}, u32[]{:S(2)}) copy-start(bf16[7,224,512]{2,1,0:T(8,128)(2,1)} %get-tuple-element.56) | copy-start | bytes 4816900
  138.9 15.0 %copy-start.3 = (bf16[1,16,288,512]{3,2,1,0:T(8,128)(2,1)}, bf16[1,16,288,512]{3,2,1,0:T(8,128)(2,1)S(1)}, u32[]{:S(2)}) copy-start(bf16[1,16,288,512]{3,2,1,0:T(8,128)(2,1)S(1)} %get-tuple-element.117) | copy-start | bytes 14155780
  138.9 14.3 %copy-start.14 = (f32[4,2048]{1,0:T(4,128)S(1)}, f32[4,2048]{1,0:T(4,128)}, u32[]{:S(2)}) copy-start(f32[4,2048]{1,0:T(4,128)} %get-tuple-element.58) | copy-start | bytes 98308
  138.9 15.0 %copy-start.6 = (f32[7,224,512]{2,1,0:T(8,128)S(1)}, f32[7,224,512]{2,1,0:T(8,128)}, u32[]{:S(2)}) copy-start(f32[7,224,512]{2,1,0:T(8,128)} %get-tuple-element.55) | copy-start | bytes 9633796
  138.9 25.2 %slice-start.2 = ((s8[4718592]{0:T(1024)(128)(4,1)}), s8[4194304]{0:T(1024)(128)(4,1)S(1)}, s32[]{:S(2)}) async-start(s8[4718592]{0:T(1024)(128)(4,1)} %bitcast.145), calls=%async_computation.2 | async-start | bytes 8388608
  153.9 10.2 %slice-start.3 = ((s8[4718592]{0:T(1024)(128)(4,1)}), s8[524288]{0:T(1024)(128)(4,1)S(1)}, s32[]{:S(2)}) async-start(s8[4718592]{0:T(1024)(128)(4,1)} %bitcast.145), calls=%async_computation.3 | async-start | bytes 1048576
  164.1 9.6 %copy-start.1 = (bf16[7,7,32,512]{3,2,1,0:T(8,128)(2,1)}, bf16[7,7,32,512]{3,2,1,0:T(8,128)(2,1)S(1)}, u32[]{:S(2)}) copy-start(bf16[7,7,32,512]{3,2,1,0:T(8,128)(2,1)S(1)} %get-tuple-element.138.refs_5_) | copy-start | bytes 4816900
  164.1 11.0 %copy-start.10 = (bf16[2,49,2048]{2,0,1:T(2,128)(2,1)S(1)}, bf16[2,49,2048]{2,0,1:T(2,128)(2,1)}, u32[]{:S(2)}) copy-start(bf16[2,49,2048]{2,0,1:T(2,128)(2,1)} %param.37) | copy-start | bytes 1204228
  177.3 105.3 %slice-start.4 = ((s8[4718592]{0:T(1024)(128)(4,1)}), s8[524288]{0:T(1024)(128)(4,1)S(1)}, s32[]{:S(2)}) async-start(s8[4718592]{0:T(1024)(128)(4,1)} %bitcast.149), calls=%async_computation.4 | async-start | bytes 1048576
  267.6 15.0 %slice-start.5 = ((s8[4718592]{0:T(1024)(128)(4,1)}), s8[4194304]{0:T(1024)(128)(4,1)S(1)}, s32[]{:S(2)}) async-start(s8[4718592]{0:T(1024)(128)(4,1)} %bitcast.149), calls=%async_computation.5 | async-start | bytes 8388608
  267.6 23.0 %slice-start = ((s8[4718592]{0:T(1024)(128)(4,1)}), s8[4194304]{0:T(1024)(128)(4,1)S(1)}, s32[]{:S(2)}) async-start(s8[4718592]{0:T(1024)(128)(4,1)} %bitcast.141), calls=%async_computation | async-start | bytes 8388608
  282.6 8.0 %copy-start.2 = (bf16[7,7,32,512]{3,2,1,0:T(8,128)(2,1)}, bf16[7,7,32,512]{3,2,1,0:T(8,128)(2,1)S(1)}, u32[]{:S(2)}) copy-start(bf16[7,7,32,512]{3,2,1,0:T(8,128)(2,1)S(1)} %get-tuple-element.116) | copy-start | bytes 4816900
  282.6 7.9 %slice-start.1 = ((s8[4718592]{0:T(1024)(128)(4,1)}), s8[524288]{0:T(1024)(128)(4,1)S(1)}, s32[]{:S(2)}) async-start(s8[4718592]{0:T(1024)(128)(4,1)} %bitcast.141), calls=%async_computation.1 | async-start | bytes 1048576
  298.5 1.9 copy-start.4
  298.5 2.9 copy-start.5
  301.4 13.1 %copy-start.16 = (f32[1,128]{1,0:T(1,128)S(1)}, f32[1,128]{1,0:T(1,128)}, u32[]{:S(2)}) copy-start(f32[1,128]{1,0:T(1,128)} %get-tuple-element.67) | copy-start | bytes 1540
  301.4 13.1 %copy-start.17 = (f32[1,512]{1,0:T(1,128)S(1)}, f32[1,512]{1,0:T(1,128)}, u32[]{:S(2)}) copy-start(f32[1,512]{1,0:T(1,128)} %get-tuple-element.63) | copy-start | bytes 6148
  316.8 15.9 %copy-start.8 = (f32[7,7,32,64]{3,2,1,0:T(8,128)S(1)}, f32[7,7,32,64]{3,2,1,0:T(8,128)}, u32[]{:S(2)}) copy-start(f32[7,7,32,64]{3,2,1,0:T(8,128)} %get-tuple-element.77) | copy-start | bytes 1204228
  316.8 26.9 %copy-start.24 = (f32[1,64]{1,0:T(1,128)S(1)}, f32[1,64]{1,0:T(1,128)}, u32[]{:S(2)}) copy-start(f32[1,64]{1,0:T(1,128)} %get-tuple-element.75) | copy-start | bytes 772
  334.9 12.0 %copy-start.11 = (bf16[64,2048]{1,0:T(8,128)(2,1)S(1)}, bf16[64,2048]{1,0:T(8,128)(2,1)}, u32[]{:S(2)}) copy-start(bf16[64,2048]{1,0:T(8,128)(2,1)} %get-tuple-element.74) | copy-start | bytes 786436
  349.0 125.0 %copy-start.7 = (f32[2,49,1,2048]{3,2,1,0:T(1,128)S(1)}, f32[2,49,1,2048]{3,2,1,0:T(1,128)}, u32[]{:S(2)}) copy-start(f32[2,49,1,2048]{3,2,1,0:T(1,128)} %get-tuple-element.62) | copy-start | bytes 2408452
  465.7 9.9 %copy-start.13 = (f32[128,512]{1,0:T(8,128)S(1)}, f32[128,512]{1,0:T(8,128)}, u32[]{:S(2)}) copy-start(f32[128,512]{1,0:T(8,128)} %get-tuple-element.173) | copy-start | bytes 786436
  465.8 10.6 %copy-start.9 = (f32[288,512]{1,0:T(8,128)S(1)}, f32[288,512]{1,0:T(8,128)}, u32[]{:S(2)}) copy-start(f32[288,512]{1,0:T(8,128)} %get-tuple-element.178) | copy-start | bytes 1769476
  465.8 11.4 %copy-start.12 = (f32[32,2048]{1,0:T(8,128)S(1)}, f32[32,2048]{1,0:T(8,128)}, u32[]{:S(2)}) copy-start(f32[32,2048]{1,0:T(8,128)} %get-tuple-element.181) | copy-start | bytes 786436

commit v4 on v3

--- a/solution.py
+++ b/solution.py
@@ -399,17 +399,16 @@
                     yield da, du, dv
 
     def cores(self, k):
-        place = self.place
-        for da, du, dv in self.order():
+        rep, reps = self.place.rep, self.reps
+        for d in range(1, reps):
+            other = (rep + d) % reps
+            source = self.terms[k].at[:, columns(self.terms[k].shape[1] // reps, other)]
+            self.push(source, self.from_rep[k].at[d - 1], self.r_sem.at[k, d - 1], self.place.me, other)
+
+    def hop(self, k, lag):
+        if lag == 0:
             for d in range(1, self.reps):
-                other = (place.rep + d) % self.reps
-                index = Place(self.dims, self.reps, other).at(da, du, dv)
-                self.push(
-                    self.part(k, index, other), self.from_rep[k].at[d - 1, index],
-                    self.r_sem.at[k, da, du, dv, d - 1], place.me, other,
-                )
-
-    def hop(self, k, lag):
+                self.landed(self.from_rep[k].at[d - 1], self.r_sem.at[k, d - 1])
         if 0 <= k < len(self.terms):
             for da, du, dv in self.order():
                 if lag == (0 if dv else 1 if du else 2 if da else 3):
@@ -420,10 +419,14 @@
         place, reps, rep = self.place, self.reps, self.place.rep
         index = place.at(da, du, dv)
         mine = self.part(k, index, rep)
-        total = mine[...].astype(f32)
-        for d in range(1, reps):
-            self.landed(self.from_rep[k].at[d - 1, index], self.r_sem.at[k, da, du, dv, d - 1])
-            total = total + self.from_rep[k][d - 1, index].astype(f32)
+        rows = self.rows[k]
+        span = pl.ds(pl.multiple_of(index * rows, rows), rows)
+        if dv and reps == 2:
+            total = mine[...] + self.from_rep[k][0, span]
+        else:
+            total = mine[...].astype(f32)
+            for d in range(1, reps):
+                total = total + self.from_rep[k][d - 1, span].astype(f32)
         if dv == 0:
             for e in range(1, size_c):
                 self.landed(self.from_v[k].at[e - 1, da, du], self.v_sem.at[k, da, du, e - 1])
@@ -455,7 +458,11 @@
             for d in range(1, self.reps):
                 self.landed(self.share[k].at[(self.place.rep + self.reps - d) % self.reps], self.s_sem.at[k, d - 1])
             for which in range(self.reps):
-                total[:, which * width : (which + 1) * width] = self.share[k][which].astype(f32)
+                start = which * width
+                for ref, row in total if isinstance(total, list) else [(total, 0)]:
+                    height, length = ref.shape[0], min(ref.shape[1] - start, width)
+                    if length > 0:
+                        ref[:, start : start + length] = self.share[k][which, row : row + height, :length].astype(f32)
         for copy in self.waits:
             copy.wait_send()
 
@@ -469,13 +476,13 @@
         return [pltpu.VMEM(lead + (rows, width // reps), bf16) for rows, width in shapes]
 
     return (
-        buffers(others, size_a * size_b * size_c)
+        [pltpu.VMEM((others, size_a * size_b * size_c * rows, width // reps), bf16) for rows, width in shapes]
         + buffers(max(size_c - 1, 1), size_a, size_b)
         + buffers(max(size_b - 1, 1), size_a)
         + buffers(max(size_a - 1, 1))
         + buffers(reps)
         + [
-            DMA((count, size_a, size_b, size_c, others, 2)),
+            DMA((count, others, 2)),
             DMA((count, size_a, size_b, max(size_c - 1, 1), 2)),
             DMA((count, size_a, max(size_b - 1, 1), 2)),
             DMA((count, max(size_a - 1, 1), 2)),
@@ -486,10 +493,15 @@
 
 def terms_kernel(dims, reps, rows, *refs):
     (small, block_low, grad_reduced, act_two, grad_expanded, modulated, grad_middle, change, grad_gate) = refs[:9]
-    totals = refs[9:15]
-    terms = refs[15:21]
-    pads, line, turned, chunk, pad_sem, line_sem, chunk_sem, small_sem = refs[21:29]
-    scatter = Scatter(dims, reps, terms, rows, refs[29:])
+    lateral_total, stem_total, gate_total, reduce_total, expand_total, mid_total, diff_total = refs[9:16]
+    stem_rows = stem_total.shape[0]
+    totals = [
+        [(lateral_total, 0), (stem_total, stem_rows), (gate_total, 2 * stem_rows)],
+        reduce_total, expand_total, mid_total, diff_total.at[0], diff_total.at[1],
+    ]
+    terms = refs[16:22]
+    pads, line, turned, chunk, pad_sem, line_sem, chunk_sem, small_sem = refs[22:30]
+    scatter = Scatter(dims, reps, terms, rows, refs[30:])
     slots, mid_width = modulated.shape[2:]
     lines = block_low.shape[0]
     width = block_low.shape[2]
@@ -508,7 +520,7 @@
             source.at[:, :, j * step : (j + 1) * step], chunk.at[number % 2], chunk_sem.at[number % 2]
         )
 
-    gradients = [grad_reduced, grad_middle, grad_gate, act_two]
+    gradients = [grad_middle, grad_gate, grad_reduced, act_two]
 
     def turn(number):
         pltpu.make_async_copy(gradients[number], line, line_sem).wait()
@@ -563,25 +575,19 @@
     small_copy.wait()
     scatter.cores(0)
     turn(0)
-    reduce_pieces(0, half)
-    flow((0, 0))
-    reduce_pieces(half, chunks)
-    scatter.cores(1)
-    turn(1)
     padded(0)
     taps(3, 0, 1, 0, 3)
-    flow((1, 0), (0, 1))
+    flow((0, 0))
     taps(3, 0, 1, 3, 6)
-    flow((1, 1), (0, 2))
+    flow((0, 1))
     taps(3, 0, 1, 6, 9)
     scatter.cores(3)
-    turn(2)
+    turn(1)
     padded(1)
-    flow((1, 2), (0, 3))
     taps(4, 1, 1, 0, 3)
-    flow((3, 0))
+    flow((3, 0), (0, 2))
     taps(4, 1, 1, 3, 6)
-    flow((1, 3))
+    flow((0, 3))
     taps(4, 1, 1, 6, 9)
     scatter.cores(4)
     taps(5, 1, 2, 0, 3)
@@ -589,17 +595,22 @@
     taps(5, 1, 2, 3, 6)
     taps(5, 1, 2, 6, 9)
     scatter.cores(5)
+    turn(2)
+    flow((3, 2))
+    reduce_pieces(0, half)
+    flow((5, 0), (4, 1))
+    reduce_pieces(half, chunks)
+    scatter.cores(1)
     turn(3)
-    flow((3, 2))
     expand_pieces(0, half)
-    flow((5, 0), (4, 1))
+    flow((1, 0), (4, 2), (3, 3))
     expand_pieces(half, chunks)
     scatter.cores(2)
-    flow((3, 3), (4, 2), (2, 0), (5, 1), (2, 1), (4, 3), (5, 2), (2, 2), (5, 3), (2, 3))
+    flow((5, 1), (2, 0), (1, 1), (5, 2), (4, 3), (2, 1), (1, 2), (5, 3), (2, 2), (1, 3), (2, 3))
     scatter.finish(totals)
 
 
-def terms_all(small, block_low, grad_reduced, act_two, grad_expanded, modulated, grad_middle, change, grad_gate, rows, fsdp, reps, collective_id):
+def terms_all(small, block_low, grad_reduced, act_two, grad_expanded, modulated, grad_middle, change, grad_gate, rows, stem_rows, stem_depth, fsdp, reps, collective_id):
     dims = factor_three(fsdp)
     lines, line_rows, width = block_low.shape
     mid_width = act_two.shape[-1]
@@ -609,9 +620,12 @@
     side = GRID + 4
     return pl.pallas_call(
         functools.partial(terms_kernel, dims, reps, rows),
-        out_shape=[jax.ShapeDtypeStruct(shape, f32) for shape in shapes],
+        out_shape=[
+            jax.ShapeDtypeStruct(shape, f32)
+            for shape in [(stem_rows, width), (stem_rows, stem_depth), (1, mid_width // fsdp)] + shapes[1:4] + [(2,) + shapes[4]]
+        ],
         in_specs=[ANY] * 9,
-        out_specs=[IN_VMEM] * 6,
+        out_specs=[IN_VMEM] * 7,
         scratch_shapes=[pltpu.VMEM((fsdp * a, b), bf16) for a, b in shapes]
         + [
             pltpu.VMEM((2, side, side, slots, mid_width), bf16),
@@ -635,71 +649,81 @@
         self.place = Place(dims, reps)
         self.waits, self.local = [], []
 
-    def slot(self, k, index, which):
+    def slot(self, k, da, du, dv, which):
         full = self.fulls[k]
-        return full.at[index, :, columns(full.shape[-1] // self.reps, which)]
+        index = self.place.at(-(da or 0), -du, -dv)
+        others = self.dims[1] * self.dims[2]
+        cols = columns(full.shape[-1] // self.reps, which)
+        if da is None:
+            return full.at[:, index % others, :, cols]
+        return full.at[index // others, index % others, :, cols]
 
     def push(self, k, da, du, dv, target, target_rep, sems):
-        index, rep = self.place.at(-da, -du, -dv), self.place.rep
+        there = self.slot(k, da, du, dv, self.place.rep)
         if (da, du, dv) == (0, 0, 0):
-            source = self.shards[k].at[:, columns(self.shards[k].shape[-1] // self.reps, rep)]
+            source = self.shards[k].at[:, columns(self.shards[k].shape[-1] // self.reps, self.place.rep)]
         else:
-            source = self.slot(k, index, rep)
-        copy = remote(source, self.slot(k, index, rep), sems, target, target_rep)
+            source = there
+        copy = remote(source, there, sems, target, target_rep)
         copy.start()
         self.waits.append(copy)
 
     def landed(self, k, da, du, dv, which, sems):
-        there = self.slot(k, self.place.at(-da, -du, -dv), which)
+        there = self.slot(k, da, du, dv, which)
         remote(there, there, sems, self.place.me, self.place.rep).wait_recv()
 
-    def forward(self, k, da, du, dv):
-        size_a, size_b, size_c = self.dims
-        place, rep = self.place, self.place.rep
-        if dv == 0 and du == 0:
-            for d in range(1, size_b):
-                self.push(k, da, 0, 0, place.at(0, d, 0), rep, self.b_sem.at[k, da, d - 1])
-        if dv == 0:
-            for d in range(1, size_c):
-                self.push(k, da, du, 0, place.at(0, 0, d), rep, self.c_sem.at[k, da, du, d - 1])
-        if (da, du, dv) != (0, 0, 0):
-            for d in range(1, self.reps):
-                self.push(k, da, du, dv, place.me, (rep + d) % self.reps, self.r_sem.at[k, da, du, dv, d - 1])
+    def along_u(self, k, da):
+        for d in range(1, self.dims[1]):
+            self.push(k, da, 0, 0, self.place.at(0, d, 0), self.place.rep, self.b_sem.at[k, da, d - 1])
+
+    def along_v(self, k, da, du):
+        for d in range(1, self.dims[2]):
+            self.push(k, da, du, 0, self.place.at(0, 0, d), self.place.rep, self.c_sem.at[k, da or 0, du, d - 1])
+
+    def to_reps(self, k, da, du, dv):
+        for d in range(1, self.reps):
+            self.push(
+                k, da, du, dv, self.place.me, (self.place.rep + d) % self.reps, self.r_sem.at[k, da or 0, du, dv, d - 1]
+            )
 
     def begin(self, k):
         place = self.place
-        copy = pltpu.make_async_copy(self.shards[k], self.fulls[k].at[place.me], self.own_sem.at[k])
+        others = self.dims[1] * self.dims[2]
+        copy = pltpu.make_async_copy(self.shards[k], self.fulls[k].at[place.me // others, place.me % others], self.own_sem.at[k])
         copy.start()
         self.local.append(copy)
         for d in range(1, self.dims[0]):
             self.push(k, 0, 0, 0, place.at(d, 0, 0), place.rep, self.a_sem.at[k, d - 1])
-        self.forward(k, 0, 0, 0)
+        self.along_u(k, 0)
+        self.along_v(k, 0, 0)
 
     def hop(self, k, lag):
         size_a, size_b, size_c = self.dims
-        place, reps, rep = self.place, self.reps, self.place.rep
+        reps, rep = self.reps, self.place.rep
         if lag == 0:
             for da in range(1, size_a):
                 self.landed(k, da, 0, 0, rep, self.a_sem.at[k, da - 1])
-                self.forward(k, da, 0, 0)
+                self.along_u(k, da)
+                self.along_v(k, da, 0)
+                self.to_reps(k, da, 0, 0)
         elif lag == 1:
             for du in range(1, size_b):
                 for da in range(size_a):
                     self.landed(k, da, du, 0, rep, self.b_sem.at[k, da, du - 1])
-                    self.forward(k, da, du, 0)
+                self.along_v(k, None, du)
+                self.to_reps(k, None, du, 0)
         elif lag == 2:
             for dv in range(1, size_c):
                 for du in range(size_b):
-                    for da in range(size_a):
-                        self.landed(k, da, du, dv, rep, self.c_sem.at[k, da, du, dv - 1])
-                        self.forward(k, da, du, dv)
+                    for da in range(size_a) if du == 0 else (None,):
+                        self.landed(k, da, du, dv, rep, self.c_sem.at[k, da or 0, du, dv - 1])
+                    self.to_reps(k, None, du, dv)
         else:
             for dv in range(size_c):
                 for du in range(size_b):
-                    for da in range(size_a):
-                        if (da, du, dv) != (0, 0, 0):
-                            for d in range(1, reps):
-                                self.landed(k, da, du, dv, (rep + reps - d) % reps, self.r_sem.at[k, da, du, dv, d - 1])
+                    for da in range(1, size_a) if du == dv == 0 else (None,):
+                        for d in range(1, reps):
+                            self.landed(k, da, du, dv, (rep + reps - d) % reps, self.r_sem.at[k, da or 0, du, dv, d - 1])
             self.local[k].wait()
 
     def finish(self):
@@ -730,7 +754,8 @@
         [small, stem_taps, reduce_full, diff_out.at[0], diff_out.at[1], mid_out, expand_out], refs[46:51],
     )
     over = Exchange(sizes, reps, refs[51:])
-    fsdp = small.shape[0]
+    others = small.shape[1]
+    fsdp = small.shape[0] * others
     me = gather.place.me
     stem_width = stem_rows * fsdp
     lines, rows, mid_width = reduced.shape
@@ -804,11 +829,11 @@
     gather.hop(1, 3)
     vectors = jnp.zeros((taken - stem_rows, width), f32)
     for device in range(fsdp):
-        values = small[device].astype(f32)
+        values = small[device // others, device % others].astype(f32)
         span = slice(device * stem_rows, (device + 1) * stem_rows)
         lateral[span, :] = values[:stem_rows]
         vectors = vectors + values[stem_rows:taken]
-        taps = stem_taps[device].astype(f32)
+        taps = stem_taps[device // others, device % others].astype(f32)
         for x in range(GRID):
             tap_rows[x, span, :] = taps[x * stem_rows : (x + 1) * stem_rows]
     lateral_low = lateral[...].astype(bf16)
@@ -876,8 +901,9 @@
         if j >= 2:
             out_wide.wait()
             out_low.wait()
-        shares = step // reduce_full.shape[1]
-        weight = reduce_full[j * shares : (j + 1) * shares].reshape(step, mid_width)
+        shares = step // reduce_full.shape[2]
+        start = j * shares % others
+        weight = reduce_full[j * shares // others, start : start + shares].reshape(step, mid_width)
 
         def line(y, _):
             values = loaded[slot, pl.ds(y * groups, groups)].astype(f32).reshape(rows, step)
@@ -927,6 +953,7 @@
 
 def head(stem_taps, reduce_weight, diff_weight, mid_weight, expand_weight, lateral, wide, narrow, least, lhs, valid, pair, count, features, fsdp, reps, collective_id):
     dims, sizes = factor_three(fsdp), stage_sizes(fsdp * reps)
+    split = (dims[0], dims[1] * dims[2])
     shape = jax.ShapeDtypeStruct
     clips, pixels, segs, width = features.shape
     slots = clips * segs
@@ -941,10 +968,10 @@
     small = shape((-(-(stem_rows + vectors) // 16) * 16, width), bf16)
 
     def full(shard):
-        return shape(shard.shape[:-2] + (fsdp,) + shard.shape[-2:], shard.dtype)
+        return shape(shard.shape[:-2] + split + shard.shape[-2:], shard.dtype)
 
     def whole(shard):
-        return pltpu.VMEM((fsdp,) + shard.shape, shard.dtype)
+        return pltpu.VMEM(split + shard.shape, shard.dtype)
 
     return pl.pallas_call(
         functools.partial(head_kernel, dims, reps, sizes, stem_rows),
@@ -1035,12 +1062,11 @@
     def expand_chunk(j, _):
         cols = pl.ds(pl.multiple_of(j * step, step), step)
         weight = expand[:, cols]
-        origin = dot(act_two[0, 0:16, :], weight)[0:1]
+        wide[:, :, cols] = dot(act_two[...].reshape(lines * rows, mid_width), weight).reshape(lines, rows, step)
+        origin = wide[0, 0:1, cols]
 
         def line(y, carry):
-            values = dot(act_two[y], weight)
-            wide[y, :, cols] = values
-            return gather_moments(carry, values, origin)
+            return gather_moments(carry, wide[y, :, cols], origin)
 
         total, squares = moments(lax.fori_loop(0, lines, line, blank(step)), origin)
         totals[0, :, cols] = total
@@ -1098,29 +1124,31 @@
     totals[1] = totals[1] * gain_three[...]
 
     def out_low(y):
-        return pltpu.make_async_copy(low.at[y % 2], grad_expanded.at[y], low_sem.at[y % 2])
-
-    def back_three(y, carry):
-        slot = y % 2
-
-        @pl.when(y >= 2)
-        def _():
-            out_low(y - 2).wait()
-
+        return pltpu.make_async_copy(low.at[y], grad_expanded.at[y], low_sem.at[y])
+
+    def back_three(y, _):
         def chunk(j, _):
             cols = pl.ds(pl.multiple_of(j * step, step), step)
             grad = wide_grad[y, :, cols] - totals[2, :, cols] - wide[y, :, cols] * totals[3, :, cols]
-            low[slot, :, cols] = (mask * grouped(grad * totals[1, :, cols])).astype(bf16).reshape(rows, step)
+            low[y, :, cols] = (mask * grouped(grad * totals[1, :, cols])).astype(bf16).reshape(rows, step)
             return 0
 
         lax.fori_loop(0, chunks, chunk, 0)
         out_low(y).start()
+        return 0
+
+    lax.fori_loop(0, lines, back_three, 0)
+    for start in range(0, mid_width, step):
+        values = dot_t(low[...].reshape(lines * rows, width), expand[start : start + step, :])
+        narrow_grad[:, :, start : start + step] = values.reshape(lines, rows, step)
+
+    def slopes(y, carry):
         normed = narrow[y]
-        grad = grouped(dot_t(low[slot], expand[...])) * gelu_parts(zeta_two(normed))[1] * mask
+        grad = grouped(narrow_grad[y]) * gelu_parts(zeta_two(normed))[1] * mask
         narrow_grad[y] = grad.reshape(rows, mid_width)
         return carry[0] + fold_rows(grad), carry[1] + fold_rows(grad * grouped(normed))
 
-    carry = lax.fori_loop(0, lines, back_three, blank(mid_width))
+    carry = lax.fori_loop(0, lines, slopes, blank(mid_width))
     shift_sum, gain_sum = over.total(3, [whole_row(carry[0]), whole_row(carry[1])], False)
     shift_two_sum[...] = shift_sum
     gain_two_sum[...] = gain_sum
@@ -1133,8 +1161,7 @@
 
     lax.fori_loop(0, lines, back_two, 0)
     lax.fori_loop(0, lines, lambda y, _: (out_pre(y).wait(), 0)[1], 0)
-    for y in (lines - 2, lines - 1):
-        out_low(y).wait()
+    lax.fori_loop(0, lines, lambda y, _: (out_low(y).wait(), 0)[1], 0)
     over.finish()
 
 
@@ -1156,9 +1183,9 @@
         scratch_shapes=[
             pltpu.VMEM((lines, rows, width), f32), pltpu.VMEM((lines, rows, width), f32),
             pltpu.VMEM((lines, rows, mid_width), f32), pltpu.VMEM((lines, rows, mid_width), f32),
-            pltpu.VMEM((2, rows, width), f32), pltpu.VMEM((2, rows, width), bf16),
+            pltpu.VMEM((2, rows, width), f32), pltpu.VMEM((lines, rows, width), bf16),
             pltpu.VMEM((4, 1, width), f32), pltpu.VMEM((2, 8, width), f32),
-            DMA((2,)), DMA((lines,)), DMA((2,)),
+            DMA((2,)), DMA((lines,)), DMA((lines,)),
         ] + exchange_buffers(sizes, 4, 2 * width + LANES),
         compiler_params=pltpu.CompilerParams(collective_id=collective_id, has_side_effects=True, vmem_limit_bytes=VMEM_LIMIT),
         name="tail",
@@ -1429,11 +1456,12 @@
 
         conv_rows = mid_weight.shape[0]
         if conv_rows % 32 == 0:
-            small_part, reduce_part, expand_part, mid_part, diff_one, diff_two = terms_all(
+            lateral_part, stem_part, gate_part, reduce_part, expand_part, mid_part, diff_part = terms_all(
                 small_terms.reshape(-1, feature_width), block_low, grad_reduced.reshape(flat),
                 act_two.reshape(flat), grad_expanded.reshape(flat), modulated, grad_middle.reshape(flat), change,
                 grad_gate.reshape(flat),
-                [small_terms.shape[1], reduce_weight.shape[0], expand_weight.shape[0], conv_rows], fsdp, reps, 10,
+                [small_terms.shape[1], reduce_weight.shape[0], expand_weight.shape[0], conv_rows], stem_rows, stem_depth,
+                fsdp, reps, 10,
             )
         else:
             def owned(terms, shard):
@@ -1450,6 +1478,9 @@
                 ],
                 fsdp, reps, 11, "scatter_terms",
             )
+            lateral_part, gate_part = small_part[:stem_rows], small_part[2 * stem_rows, :gate_rows]
+            stem_part = small_part[stem_rows : 2 * stem_rows, :stem_depth]
+            diff_part = jnp.stack([diff_one, diff_two])
 
         def own_share(whole):
             share = whole.shape[0] // fsdp
@@ -1459,15 +1490,15 @@
         return (
             pooled,
             out,
-            small_part[stem_rows : 2 * stem_rows, :stem_depth],
+            stem_part,
             own_share(stem_gain_sum),
             own_share(stem_shift_sum),
-            small_part[:stem_rows],
+            lateral_part,
             reduce_part,
             own_share(gain_one_sum),
             own_share(shift_one_sum),
-            jnp.stack([diff_one, diff_two]),
-            small_part[2 * stem_rows, :gate_rows],
+            diff_part,
+            gate_part.reshape(-1),
             mid_part,
             own_share(gain_two_sum),
             own_share(shift_two_sum),

time: 482 us -> 473 us (0.981)
  Pallas kernels: 358 us -> 351 us
    pallas_call x1, Pallas kernels: 117 us -> 112 us  [terms_all(): pl.pallas_call(functools.partial(terms_kernel, dims, reps, rows), out_sha...]
    unnamed x82 -> x88, local copies, waits for them, and re-layouts: 4.71 us -> 9.88 us
where the time goes in v4:
time: 473 us; the launch traced here: 469 us
  Pallas kernels  351 us (74%)
  matrix products  66.9 us (14%)
  local copies, waits for them, and re-layouts  36.4 us (8%)
  other arithmetic  13.1 us (3%)
    pallas_call x1, Pallas kernels, head(): pl.pallas_call(functools.partial(head_kernel, dims, reps, sizes, stem_row...  120 us
    pallas_call x1, Pallas kernels, terms_all(): pl.pallas_call(functools.partial(terms_kernel, dims, reps, rows), out_sha...  112 us
    pallas_call x1, Pallas kernels, tail(): pl.pallas_call(functools.partial(tail_kernel, sizes, reps, clip_count), o...  85.5 us
    conv_general_dilated x3, matrix products, convolve(): lax.conv_general_dilated(source, kernel, (1, 1), pad_of(span * stride), r...  34.1 us
    conv_general_dilated x3, matrix products, convolve_back(): lax.conv_general_dilated(grads, kernel, (1, 1), pad_of(span * stride), rh...  30.8 us
    pallas_call x2, Pallas kernels, exchange(): pl.pallas_call(functools.partial(exchange_kernel, sizes, reps, moments),...  17.8 us
    pallas_call x1, Pallas kernels, back(): pl.pallas_call(functools.partial(back_kernel, clips), out_shape=[shape((c...  15.9 us
    unnamed x88, local copies, waits for them, and re-layouts  9.88 us

profile of v4, /device:TPU:0, one launch (start us, length us, event | category | flops | bytes accessed | tf_op | source)
XLA Modules:
  0.0 469.2 jit_solution(7389019385242465233)
XLA Ops:
  0.7 0.7 fusion.37
  1.4 0.9 convert_element_type.82
  2.4 0.3 copy.41
  2.8 0.2 reshape.348
  3.0 0.3 pad_slice_fusion
  3.3 0.2 copy.43
  3.4 0.2 copy.44
  3.6 0.2 copy.45
  3.8 0.2 copy.47
  4.0 0.2 copy.48
  4.1 0.2 copy.49
  4.6 0.2 concatenate.31
  4.8 0.8 pad.39.refs_9_
  6.1 0.2 reshape.347
  6.4 0.6 pad.37.refs_0_
  7.1 0.7 broadcast_in_dim.18.refs_10_.refs_2_
  8.0 0.7 broadcast_in_dim.20.refs_11_
  8.7 0.6 convert_reduce_fusion
  9.9 0.5 broadcast_in_dim.21.refs_12_.refs_4_
  10.4 0.6 stack.76.refs_7_
  11.1 0.5 pad_maximum_fusion.refs_6_
  11.6 0.5 pad_maximum_fusion.1.refs_8_
  12.1 120.0 %head.1 = (bf16[64,2048]{1,0:T(8,128)(2,1)}, f32[4,2048]{1,0:T(4,128)}, bf16[4,4,128,512]{3,2,1,0:T(8,128)(2,1)}, bf16[2,4,4,288,512]{4,3,2,1,0:T(8,128)(2,1)}, ...) custom-call(bf16[32,768]{1,0:T(8,128)(2,1)} %pad.37.refs_0_, ...), custom_call_target="tpu_custom_call" | custom-call | tf_op jit(solution)/shard_map/head/pallas_call | solution.py:976
  132.1 6.8 %fusion.49 = (bf16[1,4,4,288,512]{4,3,2,1,0:T(8,128)(2,1)S(1)}, bf16[1,4,4,288,512]{4,3,2,1,0:T(8,128)(2,1)}) fusion(bf16[2,4,4,288,512]{4,3,2,1,0:T(8,128)(2,1)} %get-tuple-element.58), kind=kLoop, calls=%fused_computation.100 | loop fusion | bytes 18874368 | tf_op jit(solution)/shard_map/slice | solution.py:1408
  138.9 14.3 %fusion.55 = f32[7,7,32,512]{3,2,1,0:T(8,128)S(1)} fusion(bf16[7,7,32,512]{3,2,1,0:T(8,128)(2,1)S(1)} %bitcast.132, bf16[3,3,512,512]{3,2,1,0:T(8,128)(2,1)} %bitcast.145), kind=kOutput, calls=%fused_computation.106 | convolution fusion | flops 6056574976 | bytes 9535488 | tf_op jit(solution)/shard_map/conv_general_dilated | solution.py:1291
  153.2 0.6 fusion.52
  153.8 10.2 %multiply_convert_fusion.1 = (bf16[7,7,32,512]{3,2,1,0:T(8,128)(2,1)S(1)}, f32[7,7,32,512]{3,2,1,0:T(8,128)}) fusion(f32[7,7,32,512]{3,2,1,0:T(8,128)S(1)} %bitcast.157, f32[512]{0:T(512)S(1)} %get-tuple-element.135, f32[7,7,32,512]{3,2,1,0:T(8,128)S(1)} %fusion.55, bf16[7,7,32,512]{3,2,1,0:T(8,128)(2,1)S(1)} %bitcast.133, ...), kind=kOutput, calls=%fused_computation.15 | convolution fusion | flops 4855037952 | bytes 17565696 | tf_op jit(solution)/shard_map/conv_general_dilated | solution.py:1291
  164.1 9.6 %fusion.56 = f32[7,7,32,512]{3,2,1,0:T(8,128)} fusion(bf16[7,7,32,512]{3,2,1,0:T(8,128)(2,1)S(1)} %get-tuple-element.140.refs_5_, bf16[3,3,512,512]{3,2,1,0:T(8,128)(2,1)S(1)} %bitcast.144), kind=kOutput, calls=%fused_computation.107 | convolution fusion | flops 6056574976 | bytes 9535488 | tf_op jit(solution)/shard_map/conv_general_dilated | solution.py:1291
  173.6 0.6 fusion.50
  174.4 0.7 broadcast_in_dim.22.refs_3_
  175.1 0.4 bitcast_convert_fusion
  175.5 1.7 copy.51.refs_9_
  177.3 85.5 %tail.1 = (f32[2,49,1,2048]{3,2,1,0:T(1,128)}, f32[7,224,2048]{2,1,0:T(8,128)}, bf16[7,224,2048]{2,1,0:T(8,128)(2,1)}, bf16[7,224,512]{2,1,0:T(8,128)(2,1)}, bf1...) custom-call(f32[7,224,512]{2,1,0:T(8,128)} %bitcast.151, ...), custom_call_target="tpu_custom_call" | custom-call | tf_op jit(solution)/shard_map/tail/pallas_call | solution.py:1174
  262.8 1.2 fusion.44
  264.0 1.2 fusion.42
  265.2 15.0 %fusion.46 = (bf16[512]{0:T(512)(128)(2,1)S(1)}, bf16[7,7,32,512]{3,2,1,0:T(8,128)(2,1)S(1)}, f32[7,7,32,512]{3,2,1,0:T(8,128)S(1)}) fusion(f32[7,7,32,512]{3,2,1,0:T(8,128)} %get-tuple-element.141, f32[7,7,32,512]{3,2,1,0:T(8,128)} %bitcast.156, bf16[7,7,32,512]{3,2,1,0:T(8,128)(2,1)} %bitcast.136, bf16[3,3,512,512]{3,2,1,0:T(8,128)(2,1)} %bitcast.141), kind=kOutput, calls=%fused_computation.98 | convolution fusion | flops 6061391360 | bytes 17564672 | tf_op jit(solution)/shard_map/conv_general_dilated | solution.py:1300
  280.3 7.9 %fusion.57 = f32[7,7,32,512]{3,2,1,0:T(8,128)S(1)} fusion(bf16[7,7,32,512]{3,2,1,0:T(8,128)(2,1)S(1)} %get-tuple-element.118, bf16[3,3,512,512]{3,2,1,0:T(8,128)(2,1)S(1)} %bitcast.148), kind=kOutput, calls=%fused_computation.108 | convolution fusion | flops 6056574976 | bytes 9535488 | tf_op jit(solution)/shard_map/conv_general_dilated | solution.py:1300
  288.2 7.9 %add_multiply_fusion = f32[7,7,32,512]{3,2,1,0:T(8,128)S(1)} fusion(f32[7,7,32,512]{3,2,1,0:T(8,128)S(1)} %fusion.57, bf16[7,7,32,512]{3,2,1,0:T(8,128)(2,1)S(1)} %get-tuple-element.118, bf16[3,3,512,512]{3,2,1,0:T(8,128)(2,1)S(1)} %bitcast.140, f32[32]{0:T(128)S(1)} %broadcast_in_dim.19), kind=kOutput, calls=%fused_computation.13 | convolution fusion | flops 4850221056 | bytes 12746880 | tf_op jit(solution)/shard_map/conv_general_dilated | solution.py:1300
  296.2 0.8 pad.40
  296.9 1.1 copy-done.4
  298.1 1.0 copy-done.5
  299.0 4.0 multiply_reduce_fusion
  303.0 9.1 %sums_one.1 = (f32[1,512]{1,0:T(1,128)S(1)}, f32[1,512]{1,0:T(1,128)S(1)}) custom-call(f32[1,512]{1,0:T(1,128)S(1)} %bitcast.129, f32[1,512]{1,0:T(1,128)S(1)} %bitcast.128), custom_call_target="tpu_custom_call" | custom-call | tf_op jit(solution)/shard_map/sums_one/pallas_call | solution.py:327
  312.3 2.2 multiply_convert_fusion
  314.4 15.9 %back.1 = (f32[2,49,16,2048]{3,2,1,0:T(8,128)}, bf16[64,2048]{1,0:T(8,128)(2,1)}, f32[7,224,64]{2,1,0:T(8,128)}) custom-call(bf16[7,224,512]{2,1,0:T(8,128)(2,1)} %bitcast.153, bf16[2048,512]{1,0:T(8,128)(2,1)} %bitcast.187, bf16[7,224,64]{2,1,0:T(8,128)(2,1)} %bitcast.188, bf16[64,2048]{1,0:T(8,128)(2,1)} %get-tuple-element.72.refs_3_, ...), custom_call_target="tpu_custom_call" | custom-call | flops 6576668672 | bytes 25690112 | tf_op jit(solution)/shard_map/back/pallas_call | solution.py:1263
  330.4 2.2 multiply_reduce_fusion.1
  332.6 8.7 %sums_stem.1 = (f32[1,128]{1,0:T(1,128)S(1)}, f32[1,128]{1,0:T(1,128)S(1)}) custom-call(f32[1,128]{1,0:T(1,128)S(1)} %pad.41.refs_0_, f32[1,128]{1,0:T(1,128)S(1)} %pad.42.refs_1_), custom_call_target="tpu_custom_call" | custom-call | tf_op jit(solution)/shard_map/sums_stem/pallas_call | solution.py:327
  341.4 2.0 fusion.20
  343.4 0.6 copy.54
  344.0 0.6 reshape.368
  345.0 1.5 copy.57
  346.6 111.5 %terms.1 = (f32[4,2048]{1,0:T(4,128)}, f32[4,588]{1,0:T(4,128)}, f32[1,32]{1,0:T(1,128)}, f32[128,512]{1,0:T(8,128)}, f32[32,2048]{1,0:T(8,128)}, /*index=5*/f32[288,512]{1,0:T(8,128)}, f32[2,288,512]{2,1,0:T(8,128)}) custom-call(bf16[256,2048]{1,0:T(8,128)(2,1)} %bitcast.155, bf16[7,224,2048]{2,1,0:T(8,128)(2,1)} %get-tuple-element.81.refs_1_, ...), custom_call_target="tpu_custom_call" | custom-call | tf_op jit(solution)/shard_map/terms/pallas_call | solution.py:621
  458.1 0.6 fusion.40
  458.7 0.6 fusion.38
  459.3 0.6 fusion.39
  459.9 0.6 convert_element_type.89
  460.4 1.2 copy.63
  461.6 1.3 copy.77
  462.9 1.4 copy.78
  464.3 1.7 copy.79
  466.0 1.0 copy.80
  467.0 0.5 copy.81
  467.5 0.8 copy.82
  468.3 0.7 copy.83
  (108 shorter events, 2.2 us)
Async XLA Ops:
  0.7 5.0 %copy-start.15 = (bf16[4,588]{1,0:T(4,128)(2,1)S(1)}, bf16[4,588]{1,0:T(4,128)(2,1)}, u32[]{:S(2)}) copy-start(bf16[4,588]{1,0:T(4,128)(2,1)} %param.22) | copy-start | bytes 14116
  2.7 5.2 %copy-start.23 = (s32[2]{0:T(128)S(1)}, s32[2]{0:T(128)}, u32[]{:S(2)}) copy-start(s32[2]{0:T(128)} %param.21) | copy-start | bytes 28
  2.7 7.8 %copy-start.18 = (bf16[32]{0:T(256)(128)(2,1)S(1)}, bf16[32]{0:T(256)(128)(2,1)}, u32[]{:S(2)}) copy-start(bf16[32]{0:T(256)(128)(2,1)} %param.27) | copy-start | bytes 196
  2.7 7.8 %copy-start.19 = (bf16[32]{0:T(256)(128)(2,1)S(1)}, bf16[32]{0:T(256)(128)(2,1)}, u32[]{:S(2)}) copy-start(bf16[32]{0:T(256)(128)(2,1)} %param.28) | copy-start | bytes 196
  2.7 7.7 %copy-start.20 = (bf16[32]{0:T(256)(128)(2,1)S(1)}, bf16[32]{0:T(256)(128)(2,1)}, u32[]{:S(2)}) copy-start(bf16[32]{0:T(256)(128)(2,1)} %param.30) | copy-start | bytes 196
  2.7 7.7 %copy-start.21 = (bf16[32]{0:T(256)(128)(2,1)S(1)}, bf16[32]{0:T(256)(128)(2,1)}, u32[]{:S(2)}) copy-start(bf16[32]{0:T(256)(128)(2,1)} %param.32) | copy-start | bytes 196
  2.7 7.7 %copy-start.22 = (bf16[32]{0:T(256)(128)(2,1)S(1)}, bf16[32]{0:T(256)(128)(2,1)}, u32[]{:S(2)}) copy-start(bf16[32]{0:T(256)(128)(2,1)} %param.33) | copy-start | bytes 196
  2.7 8.3 %copy-start.25 = (bf16[128]{0:T(256)(128)(2,1)S(1)}, bf16[128]{0:T(256)(128)(2,1)}, u32[]{:S(2)}) copy-start(bf16[128]{0:T(256)(128)(2,1)} %param.36) | copy-start | bytes 772
  2.7 8.3 %copy-start.26 = (bf16[128]{0:T(256)(128)(2,1)S(1)}, bf16[128]{0:T(256)(128)(2,1)}, u32[]{:S(2)}) copy-start(bf16[128]{0:T(256)(128)(2,1)} %param.35) | copy-start | bytes 772
  2.7 8.8 %copy-start.27 = (bf16[4]{0:T(256)(128)(2,1)S(1)}, bf16[4]{0:T(256)(128)(2,1)}, u32[]{:S(2)}) copy-start(bf16[4]{0:T(256)(128)(2,1)} %param.24) | copy-start | bytes 28
  2.8 8.8 %copy-start.28 = (bf16[4]{0:T(256)(128)(2,1)S(1)}, bf16[4]{0:T(256)(128)(2,1)}, u32[]{:S(2)}) copy-start(bf16[4]{0:T(256)(128)(2,1)} %param.23) | copy-start | bytes 28
  132.1 6.8 %copy-start = (bf16[7,224,512]{2,1,0:T(8,128)(2,1)S(1)}, bf16[7,224,512]{2,1,0:T(8,128)(2,1)}, u32[]{:S(2)}) copy-start(bf16[7,224,512]{2,1,0:T(8,128)(2,1)} %get-tuple-element.57) | copy-start | bytes 4816900
  138.9 15.0 %copy-start.3 = (bf16[1,4,4,288,512]{4,3,2,1,0:T(8,128)(2,1)}, bf16[1,4,4,288,512]{4,3,2,1,0:T(8,128)(2,1)S(1)}, u32[]{:S(2)}) copy-start(bf16[1,4,4,288,512]{4,3,2,1,0:T(8,128)(2,1)S(1)} %get-tuple-element.119) | copy-start | bytes 14155780
  138.9 14.3 %copy-start.14 = (f32[4,2048]{1,0:T(4,128)S(1)}, f32[4,2048]{1,0:T(4,128)}, u32[]{:S(2)}) copy-start(f32[4,2048]{1,0:T(4,128)} %get-tuple-element.59) | copy-start | bytes 98308
  138.9 15.0 %copy-start.6 = (f32[7,224,512]{2,1,0:T(8,128)S(1)}, f32[7,224,512]{2,1,0:T(8,128)}, u32[]{:S(2)}) copy-start(f32[7,224,512]{2,1,0:T(8,128)} %get-tuple-element.56) | copy-start | bytes 9633796
  138.9 25.2 %slice-start.2 = ((s8[4718592]{0:T(1024)(128)(4,1)}), s8[4194304]{0:T(1024)(128)(4,1)S(1)}, s32[]{:S(2)}) async-start(s8[4718592]{0:T(1024)(128)(4,1)} %bitcast.142), calls=%async_computation.2 | async-start | bytes 8388608
  153.8 10.2 %slice-start.3 = ((s8[4718592]{0:T(1024)(128)(4,1)}), s8[524288]{0:T(1024)(128)(4,1)S(1)}, s32[]{:S(2)}) async-start(s8[4718592]{0:T(1024)(128)(4,1)} %bitcast.142), calls=%async_computation.3 | async-start | bytes 1048576
  164.0 9.6 %copy-start.1 = (bf16[7,7,32,512]{3,2,1,0:T(8,128)(2,1)}, bf16[7,7,32,512]{3,2,1,0:T(8,128)(2,1)S(1)}, u32[]{:S(2)}) copy-start(bf16[7,7,32,512]{3,2,1,0:T(8,128)(2,1)S(1)} %get-tuple-element.140.refs_5_) | copy-start | bytes 4816900
  164.1 11.0 %copy-start.11 = (bf16[2,49,2048]{2,0,1:T(2,128)(2,1)S(1)}, bf16[2,49,2048]{2,0,1:T(2,128)(2,1)}, u32[]{:S(2)}) copy-start(bf16[2,49,2048]{2,0,1:T(2,128)(2,1)} %param.37) | copy-start | bytes 1204228
  177.3 103.0 %slice-start.4 = ((s8[4718592]{0:T(1024)(128)(4,1)}), s8[524288]{0:T(1024)(128)(4,1)S(1)}, s32[]{:S(2)}) async-start(s8[4718592]{0:T(1024)(128)(4,1)} %bitcast.146), calls=%async_computation.4 | async-start | bytes 1048576
  265.2 15.0 %slice-start.5 = ((s8[4718592]{0:T(1024)(128)(4,1)}), s8[4194304]{0:T(1024)(128)(4,1)S(1)}, s32[]{:S(2)}) async-start(s8[4718592]{0:T(1024)(128)(4,1)} %bitcast.146), calls=%async_computation.5 | async-start | bytes 8388608
  265.2 23.0 %slice-start = ((s8[4718592]{0:T(1024)(128)(4,1)}), s8[4194304]{0:T(1024)(128)(4,1)S(1)}, s32[]{:S(2)}) async-start(s8[4718592]{0:T(1024)(128)(4,1)} %bitcast.138), calls=%async_computation | async-start | bytes 8388608
  280.2 8.0 %copy-start.2 = (bf16[7,7,32,512]{3,2,1,0:T(8,128)(2,1)}, bf16[7,7,32,512]{3,2,1,0:T(8,128)(2,1)S(1)}, u32[]{:S(2)}) copy-start(bf16[7,7,32,512]{3,2,1,0:T(8,128)(2,1)S(1)} %get-tuple-element.118) | copy-start | bytes 4816900
  280.3 7.9 %slice-start.1 = ((s8[4718592]{0:T(1024)(128)(4,1)}), s8[524288]{0:T(1024)(128)(4,1)S(1)}, s32[]{:S(2)}) async-start(s8[4718592]{0:T(1024)(128)(4,1)} %bitcast.138), calls=%async_computation.1 | async-start | bytes 1048576
  296.2 1.9 copy-start.4
  296.2 2.9 copy-start.5
  299.0 13.1 %copy-start.16 = (f32[1,128]{1,0:T(1,128)S(1)}, f32[1,128]{1,0:T(1,128)}, u32[]{:S(2)}) copy-start(f32[1,128]{1,0:T(1,128)} %get-tuple-element.68) | copy-start | bytes 1540
  299.0 13.2 %copy-start.17 = (f32[1,512]{1,0:T(1,128)S(1)}, f32[1,512]{1,0:T(1,128)}, u32[]{:S(2)}) copy-start(f32[1,512]{1,0:T(1,128)} %get-tuple-element.64) | copy-start | bytes 6148
  314.4 15.9 %copy-start.9 = (f32[7,7,32,64]{3,2,1,0:T(8,128)S(1)}, f32[7,7,32,64]{3,2,1,0:T(8,128)}, u32[]{:S(2)}) copy-start(f32[7,7,32,64]{3,2,1,0:T(8,128)} %get-tuple-element.78) | copy-start | bytes 1204228
  314.4 26.9 %copy-start.24 = (f32[1,64]{1,0:T(1,128)S(1)}, f32[1,64]{1,0:T(1,128)}, u32[]{:S(2)}) copy-start(f32[1,64]{1,0:T(1,128)} %get-tuple-element.76) | copy-start | bytes 772
  332.5 12.0 %copy-start.12 = (bf16[64,2048]{1,0:T(8,128)(2,1)S(1)}, bf16[64,2048]{1,0:T(8,128)(2,1)}, u32[]{:S(2)}) copy-start(bf16[64,2048]{1,0:T(8,128)(2,1)} %get-tuple-element.75) | copy-start | bytes 786436
  346.6 113.3 %copy-start.8 = (f32[2,49,1,2048]{3,2,1,0:T(1,128)S(1)}, f32[2,49,1,2048]{3,2,1,0:T(1,128)}, u32[]{:S(2)}) copy-start(f32[2,49,1,2048]{3,2,1,0:T(1,128)} %get-tuple-element.63) | copy-start | bytes 2408452
  458.1 7.9 %copy-start.7 = (f32[2,288,512]{2,1,0:T(8,128)S(1)}, f32[2,288,512]{2,1,0:T(8,128)}, u32[]{:S(2)}) copy-start(f32[2,288,512]{2,1,0:T(8,128)} %get-tuple-element.178) | copy-start | bytes 3538948
  458.1 8.9 %copy-start.29 = (f32[1,32]{1,0:T(1,128)S(1)}, f32[1,32]{1,0:T(1,128)}, u32[]{:S(2)}) copy-start(f32[1,32]{1,0:T(1,128)} %get-tuple-element.88) | copy-start | bytes 388
  458.1 9.4 %copy-start.10 = (f32[288,512]{1,0:T(8,128)S(1)}, f32[288,512]{1,0:T(8,128)}, u32[]{:S(2)}) copy-start(f32[288,512]{1,0:T(8,128)} %get-tuple-element.180) | copy-start | bytes 1769476
  459.9 8.4 %copy-start.13 = (f32[32,2048]{1,0:T(8,128)S(1)}, f32[32,2048]{1,0:T(8,128)}, u32[]{:S(2)}) copy-start(f32[32,2048]{1,0:T(8,128)} %get-tuple-element.183) | copy-start | bytes 786436

commit v5 on v4

--- a/solution.py
+++ b/solution.py
@@ -584,22 +584,21 @@
     scatter.cores(3)
     turn(1)
     padded(1)
-    taps(4, 1, 1, 0, 3)
+    taps(4, 1, 1, 0, 2)
     flow((3, 0), (0, 2))
-    taps(4, 1, 1, 3, 6)
+    taps(4, 1, 1, 2, 6)
     flow((0, 3))
     taps(4, 1, 1, 6, 9)
     scatter.cores(4)
-    taps(5, 1, 2, 0, 3)
+    taps(5, 1, 2, 0, 2)
     flow((4, 0), (3, 1))
-    taps(5, 1, 2, 3, 6)
+    taps(5, 1, 2, 2, 6)
     taps(5, 1, 2, 6, 9)
     scatter.cores(5)
     turn(2)
-    flow((3, 2))
-    reduce_pieces(0, half)
-    flow((5, 0), (4, 1))
-    reduce_pieces(half, chunks)
+    reduce_pieces(0, 2)
+    flow((5, 0), (3, 2), (4, 1))
+    reduce_pieces(2, chunks)
     scatter.cores(1)
     turn(3)
     expand_pieces(0, half)
@@ -745,15 +744,15 @@
 def head_kernel(dims, reps, sizes, stem_rows, *refs):
     stem_own, reduce_own, diff_own, mid_own, expand_own = refs[:5]
     lateral_own, wide_own, narrow_own, least_own, lhs, valid, pair, count, features = refs[5:14]
-    (lateral_out, vector_out, reduce_out, diff_out, mid_out, expand_out, block_in, block_low, stem_normed, pool_low, stem_inverse,
-     number_out, normed_one, inverse_one, act_one, change) = refs[14:30]
-    (small_own, small, stem_taps, reduce_full, tap_rows, lateral, stem_values, stem_act, loaded, wide, low, reduced) = refs[30:42]
-    load_sem, wide_sem, low_sem, out_sem = refs[42:46]
+    (lateral_out, vector_out, reduce_out, diff_first, diff_second, mid_out, expand_out, block_in, block_low, stem_normed, pool_low, stem_inverse,
+     number_out, normed_one, inverse_one, act_one, change) = refs[14:31]
+    (small_own, small, stem_taps, reduce_full, tap_rows, lateral, stem_values, stem_act, loaded, wide, low, reduced) = refs[31:43]
+    load_sem, wide_sem, low_sem, out_sem = refs[43:47]
     gather = Gather(
         dims, reps, [small_own, stem_own, reduce_own, diff_own.at[0], diff_own.at[1], mid_own, expand_own],
-        [small, stem_taps, reduce_full, diff_out.at[0], diff_out.at[1], mid_out, expand_out], refs[46:51],
+        [small, stem_taps, reduce_full, diff_first, diff_second, mid_out, expand_out], refs[47:52],
     )
-    over = Exchange(sizes, reps, refs[51:])
+    over = Exchange(sizes, reps, refs[52:])
     others = small.shape[1]
     fsdp = small.shape[0] * others
     me = gather.place.me
@@ -977,7 +976,7 @@
         functools.partial(head_kernel, dims, reps, sizes, stem_rows),
         out_shape=[
             shape((stem_width, width), bf16), shape((vectors, width), f32),
-            full(reduce_weight), full(diff_weight), full(mid_weight), full(expand_weight),
+            full(reduce_weight), *[full(shape(diff_weight.shape[1:], diff_weight.dtype))] * 2, full(mid_weight), full(expand_weight),
             shape((GRID, rows, width), f32), shape((GRID, rows, width), bf16),
             shape((GRID, GRID, slots, stem_width), f32), shape((GRID, GRID, slots, stem_width), bf16),
             shape((1, stem_width), f32), shape((1, LANES), f32),
@@ -985,7 +984,7 @@
             shape((GRID, rows, mid_width), bf16),
         ],
         in_specs=[ANY] * 5 + [IN_VMEM] * 8 + [ANY],
-        out_specs=[IN_VMEM] * 2 + [ANY] * 6 + [IN_VMEM] * 8,
+        out_specs=[IN_VMEM] * 2 + [ANY] * 7 + [IN_VMEM] * 8,
         scratch_shapes=[
             pltpu.VMEM(small.shape, bf16), whole(small), whole(stem_taps), whole(reduce_weight),
             pltpu.VMEM((GRID, stem_width, stem_taps.shape[1]), f32), pltpu.VMEM((stem_width, width), f32),
@@ -1364,7 +1363,7 @@
         strips = jnp.concatenate([strips[dy : dy + GRID] for dy in range(GRID)], axis=-1).reshape(GRID * slots, -1)
         strips = jnp.pad(strips, ((0, 0), (0, -stem_depth % (LANES * reps))))
         lanes = lambda column: jnp.broadcast_to(column.reshape(-1, 1), (column.size, LANES))
-        (lateral_full, vectors, reduce_full, diff_full, mid_full, expand_full, block_in, block_low, stem_normed, pool_low,
+        (lateral_full, vectors, reduce_full, diff_first, diff_second, mid_full, expand_full, block_in, block_low, stem_normed, pool_low,
          stem_inverse, number, normed_one, inverse_one, act_one, change) = head(
             taps, reduce_weight, diff_weight, mid_weight, expand_weight, lateral, jnp.stack([gain_three, shift_three]),
             jnp.stack([gain_one, shift_one, gate_shift, gain_two, shift_two]), jnp.stack([stem_gain, stem_shift]),
@@ -1381,7 +1380,7 @@
         start += -(-stem_width // LANES) * LANES
         stem_shift_full = row[start : start + stem_width]
         reduce_full = reduce_full.reshape(-1, mid_width)
-        diff_full = diff_full.reshape(2, -1, mid_width)
+        diff_full = [diff_first.reshape(-1, mid_width), diff_second.reshape(-1, mid_width)]
         mid_full = mid_full.reshape(-1, mid_width)
         expand_full = expand_full.reshape(mid_width, -1)
         cube = (GRID, GRID, slots, -1)

time: 473 us -> 472 us (level); the launches traced: 469 us -> 462 us
  local copies, waits for them, and re-layouts: 36.4 us -> 28.7 us
    slice x1 -> x0, local copies, waits for them, and re-layouts: 6.78 us -> none  [shards(): diff_full[1]]
    unnamed x88 -> x80, local copies, waits for them, and re-layouts: 9.88 us -> 8.89 us
where the time goes in v5:
time: 472 us; the launch traced here: 462 us
  Pallas kernels  348 us (74%)
  matrix products  69.3 us (15%)
  local copies, waits for them, and re-layouts  28.7 us (6%)
  other arithmetic  14.1 us (3%)
    pallas_call x1, Pallas kernels, head(): pl.pallas_call(functools.partial(head_kernel, dims, reps, sizes, stem_row...  120 us
    pallas_call x1, Pallas kernels, terms_all(): pl.pallas_call(functools.partial(terms_kernel, dims, reps, rows), out_sha...  109 us
    pallas_call x1, Pallas kernels, tail(): pl.pallas_call(functools.partial(tail_kernel, sizes, reps, clip_count), o...  85.4 us
    conv_general_dilated x3, matrix products, convolve_back(): lax.conv_general_dilated(grads, kernel, (1, 1), pad_of(span * stride), rh...  35.5 us
    conv_general_dilated x3, matrix products, convolve(): lax.conv_general_dilated(source, kernel, (1, 1), pad_of(span * stride), r...  31.8 us
    pallas_call x2, Pallas kernels, exchange(): pl.pallas_call(functools.partial(exchange_kernel, sizes, reps, moments),...  17.8 us
    pallas_call x1, Pallas kernels, back(): pl.pallas_call(functools.partial(back_kernel, clips), out_shape=[shape((c...  15.9 us

profile of v5, /device:TPU:0, one launch (start us, length us, event | category | flops | bytes accessed | tf_op | source)
XLA Modules:
  0.0 462.5 jit_solution(17765344324706322604)
XLA Ops:
  0.7 0.7 fusion.37
  1.4 0.9 convert_element_type.82
  2.4 0.3 copy.41
  2.8 0.2 reshape.343
  3.0 0.3 pad_slice_fusion
  3.3 0.2 copy.43
  3.4 0.2 copy.44
  3.6 0.2 copy.45
  3.8 0.2 copy.47
  4.0 0.2 copy.48
  4.1 0.2 copy.49
  4.3 0.1 concatenate.27
  4.6 0.2 concatenate.31
  4.8 0.8 pad.39.refs_9_
  6.1 0.2 reshape.342
  6.4 0.6 pad.37.refs_0_
  7.1 0.7 broadcast_in_dim.18.refs_10_.refs_2_
  8.0 0.7 broadcast_in_dim.20.refs_11_
  8.7 0.6 convert_reduce_fusion
  9.9 0.5 broadcast_in_dim.21.refs_12_.refs_4_
  10.4 0.6 stack.76.refs_7_
  11.1 0.5 pad_maximum_fusion.refs_6_
  11.6 0.5 pad_maximum_fusion.1.refs_8_
  12.1 119.7 %head.1 = (bf16[64,2048]{1,0:T(8,128)(2,1)}, f32[4,2048]{1,0:T(4,128)}, bf16[4,4,128,512]{3,2,1,0:T(8,128)(2,1)}, bf16[4,4,288,512]{3,2,1,0:T(8,128)(2,1)}, bf16...) custom-call(bf16[32,768]{1,0:T(8,128)(2,1)} %pad.37.refs_0_, ...), custom_call_target="tpu_custom_call" | custom-call | tf_op jit(solution)/shard_map/head/pallas_call | solution.py:975
  131.9 13.7 %fusion.54 = f32[7,7,32,512]{3,2,1,0:T(8,128)S(1)} fusion(bf16[7,7,32,512]{3,2,1,0:T(8,128)(2,1)} %bitcast.131, bf16[3,3,512,512]{3,2,1,0:T(8,128)(2,1)} %bitcast.151), kind=kOutput, calls=%fused_computation.105 | convolution fusion | flops 6056574976 | bytes 9535488 | tf_op jit(solution)/shard_map/conv_general_dilated | solution.py:1290
  145.6 0.6 fusion.51
  146.2 8.6 %multiply_convert_fusion.1 = (bf16[7,7,32,512]{3,2,1,0:T(8,128)(2,1)S(1)}, f32[7,7,32,512]{3,2,1,0:T(8,128)S(1)}) fusion(f32[7,7,32,512]{3,2,1,0:T(8,128)S(1)} %bitcast.155, f32[512]{0:T(512)S(1)} %get-tuple-element.135, f32[7,7,32,512]{3,2,1,0:T(8,128)S(1)} %fusion.54, bf16[7,7,32,512]{3,2,1,0:T(8,128)(2,1)S(1)} %bitcast.133, ...), kind=kOutput, calls=%fused_computation.15 | convolution fusion | flops 4855037952 | bytes 17565696 | tf_op jit(solution)/shard_map/conv_general_dilated | solution.py:1290
  154.8 9.5 %fusion.55 = f32[7,7,32,512]{3,2,1,0:T(8,128)} fusion(bf16[7,7,32,512]{3,2,1,0:T(8,128)(2,1)S(1)} %get-tuple-element.140.refs_5_, bf16[3,3,512,512]{3,2,1,0:T(8,128)(2,1)S(1)} %bitcast.140), kind=kOutput, calls=%fused_computation.106 | convolution fusion | flops 6056574976 | bytes 9535488 | tf_op jit(solution)/shard_map/conv_general_dilated | solution.py:1290
  164.4 0.6 fusion.49
  165.1 0.7 broadcast_in_dim.22.refs_3_
  165.8 1.4 bitcast_convert_fusion
  167.3 1.7 copy.51.refs_9_
  169.0 85.4 %tail.1 = (f32[2,49,1,2048]{3,2,1,0:T(1,128)}, f32[7,224,2048]{2,1,0:T(8,128)}, bf16[7,224,2048]{2,1,0:T(8,128)(2,1)}, bf16[7,224,512]{2,1,0:T(8,128)(2,1)}, bf1...) custom-call(f32[7,224,512]{2,1,0:T(8,128)} %bitcast.143, ...), custom_call_target="tpu_custom_call" | custom-call | tf_op jit(solution)/shard_map/tail/pallas_call | solution.py:1173
  254.4 1.2 fusion.44
  255.6 1.3 fusion.42
  256.8 14.4 %fusion.46 = (bf16[512]{0:T(512)(128)(2,1)S(1)}, bf16[7,7,32,512]{3,2,1,0:T(8,128)(2,1)S(1)}, f32[7,7,32,512]{3,2,1,0:T(8,128)S(1)}) fusion(f32[7,7,32,512]{3,2,1,0:T(8,128)S(1)} %get-tuple-element.141, f32[7,7,32,512]{3,2,1,0:T(8,128)} %bitcast.154, bf16[7,7,32,512]{3,2,1,0:T(8,128)(2,1)} %bitcast.136, bf16[3,3,512,512]{3,2,1,0:T(8,128)(2,1)} %bitcast.137), kind=kOutput, calls=%fused_computation.98 | convolution fusion | flops 6061391360 | bytes 17564672 | tf_op jit(solution)/shard_map/conv_general_dilated | solution.py:1299
  271.2 13.2 %fusion.56 = f32[7,7,32,512]{3,2,1,0:T(8,128)S(1)} fusion(bf16[7,7,32,512]{3,2,1,0:T(8,128)(2,1)S(1)} %get-tuple-element.120, bf16[3,3,512,512]{3,2,1,0:T(8,128)(2,1)} %bitcast.152), kind=kOutput, calls=%fused_computation.107 | convolution fusion | flops 6056574976 | bytes 9535488 | tf_op jit(solution)/shard_map/conv_general_dilated | solution.py:1299
  284.5 7.9 %add_multiply_fusion = f32[7,7,32,512]{3,2,1,0:T(8,128)S(1)} fusion(f32[7,7,32,512]{3,2,1,0:T(8,128)S(1)} %fusion.56, bf16[7,7,32,512]{3,2,1,0:T(8,128)(2,1)S(1)} %get-tuple-element.120, bf16[3,3,512,512]{3,2,1,0:T(8,128)(2,1)S(1)} %bitcast.150, f32[32]{0:T(128)S(1)} %broadcast_in_dim.19), kind=kOutput, calls=%fused_computation.13 | convolution fusion | flops 4850221056 | bytes 12746880 | tf_op jit(solution)/shard_map/conv_general_dilated | solution.py:1299
  292.5 0.8 pad.40
  293.2 1.1 copy-done.3
  294.4 4.0 multiply_reduce_fusion
  298.4 9.1 %sums_one.1 = (f32[1,512]{1,0:T(1,128)S(1)}, f32[1,512]{1,0:T(1,128)S(1)}) custom-call(f32[1,512]{1,0:T(1,128)S(1)} %bitcast.129, f32[1,512]{1,0:T(1,128)S(1)} %bitcast.128), custom_call_target="tpu_custom_call" | custom-call | tf_op jit(solution)/shard_map/sums_one/pallas_call | solution.py:327
  307.7 2.2 multiply_convert_fusion
  309.8 15.9 %back.1 = (f32[2,49,16,2048]{3,2,1,0:T(8,128)}, bf16[64,2048]{1,0:T(8,128)(2,1)}, f32[7,224,64]{2,1,0:T(8,128)}) custom-call(bf16[7,224,512]{2,1,0:T(8,128)(2,1)} %bitcast.145, bf16[2048,512]{1,0:T(8,128)(2,1)} %bitcast.185, bf16[7,224,64]{2,1,0:T(8,128)(2,1)} %bitcast.186, bf16[64,2048]{1,0:T(8,128)(2,1)} %get-tuple-element.74.refs_3_, ...), custom_call_target="tpu_custom_call" | custom-call | flops 6576668672 | bytes 25690112 | tf_op jit(solution)/shard_map/back/pallas_call | solution.py:1262
  325.8 2.1 multiply_reduce_fusion.1
  327.9 8.7 %sums_stem.1 = (f32[1,128]{1,0:T(1,128)S(1)}, f32[1,128]{1,0:T(1,128)S(1)}) custom-call(f32[1,128]{1,0:T(1,128)S(1)} %pad.41.refs_0_, f32[1,128]{1,0:T(1,128)S(1)} %pad.42.refs_1_), custom_call_target="tpu_custom_call" | custom-call | tf_op jit(solution)/shard_map/sums_stem/pallas_call | solution.py:327
  336.7 2.0 fusion.20
  338.7 0.6 copy.54
  339.3 0.6 reshape.363
  340.0 0.2 copy.55
  340.4 1.5 copy.57
  341.9 109.5 %terms.1 = (f32[4,2048]{1,0:T(4,128)}, f32[4,588]{1,0:T(4,128)}, f32[1,32]{1,0:T(1,128)}, f32[128,512]{1,0:T(8,128)}, f32[32,2048]{1,0:T(8,128)}, /*index=5*/f32[288,512]{1,0:T(8,128)}, f32[2,288,512]{2,1,0:T(8,128)}) custom-call(bf16[256,2048]{1,0:T(8,128)(2,1)} %bitcast.153, bf16[7,224,2048]{2,1,0:T(8,128)(2,1)} %get-tuple-element.83.refs_1_, ...), custom_call_target="tpu_custom_call" | custom-call | tf_op jit(solution)/shard_map/terms/pallas_call | solution.py:620
  451.4 0.6 fusion.40
  452.0 0.6 fusion.38
  452.6 0.6 fusion.39
  453.2 0.6 convert_element_type.89
  453.7 1.2 copy.63
  454.9 1.3 copy.77
  456.2 1.4 copy.78
  457.6 1.7 copy.79
  459.3 1.0 copy.80
  460.3 0.5 copy.81
  460.8 0.8 copy.82
  461.6 0.7 copy.83
  (98 shorter events, 1.9 us)
Async XLA Ops:
  0.7 5.0 %copy-start.13 = (bf16[4,588]{1,0:T(4,128)(2,1)S(1)}, bf16[4,588]{1,0:T(4,128)(2,1)}, u32[]{:S(2)}) copy-start(bf16[4,588]{1,0:T(4,128)(2,1)} %param.22) | copy-start | bytes 14116
  2.7 5.2 %copy-start.21 = (s32[2]{0:T(128)S(1)}, s32[2]{0:T(128)}, u32[]{:S(2)}) copy-start(s32[2]{0:T(128)} %param.21) | copy-start | bytes 28
  2.7 7.8 %copy-start.16 = (bf16[32]{0:T(256)(128)(2,1)S(1)}, bf16[32]{0:T(256)(128)(2,1)}, u32[]{:S(2)}) copy-start(bf16[32]{0:T(256)(128)(2,1)} %param.27) | copy-start | bytes 196
  2.7 7.8 %copy-start.17 = (bf16[32]{0:T(256)(128)(2,1)S(1)}, bf16[32]{0:T(256)(128)(2,1)}, u32[]{:S(2)}) copy-start(bf16[32]{0:T(256)(128)(2,1)} %param.28) | copy-start | bytes 196
  2.7 7.7 %copy-start.18 = (bf16[32]{0:T(256)(128)(2,1)S(1)}, bf16[32]{0:T(256)(128)(2,1)}, u32[]{:S(2)}) copy-start(bf16[32]{0:T(256)(128)(2,1)} %param.30) | copy-start | bytes 196
  2.7 7.7 %copy-start.19 = (bf16[32]{0:T(256)(128)(2,1)S(1)}, bf16[32]{0:T(256)(128)(2,1)}, u32[]{:S(2)}) copy-start(bf16[32]{0:T(256)(128)(2,1)} %param.32) | copy-start | bytes 196
  2.7 7.7 %copy-start.20 = (bf16[32]{0:T(256)(128)(2,1)S(1)}, bf16[32]{0:T(256)(128)(2,1)}, u32[]{:S(2)}) copy-start(bf16[32]{0:T(256)(128)(2,1)} %param.33) | copy-start | bytes 196
  2.7 8.3 %copy-start.23 = (bf16[128]{0:T(256)(128)(2,1)S(1)}, bf16[128]{0:T(256)(128)(2,1)}, u32[]{:S(2)}) copy-start(bf16[128]{0:T(256)(128)(2,1)} %param.36) | copy-start | bytes 772
  2.7 8.3 %copy-start.24 = (bf16[128]{0:T(256)(128)(2,1)S(1)}, bf16[128]{0:T(256)(128)(2,1)}, u32[]{:S(2)}) copy-start(bf16[128]{0:T(256)(128)(2,1)} %param.35) | copy-start | bytes 772
  2.7 8.8 %copy-start.25 = (bf16[4]{0:T(256)(128)(2,1)S(1)}, bf16[4]{0:T(256)(128)(2,1)}, u32[]{:S(2)}) copy-start(bf16[4]{0:T(256)(128)(2,1)} %param.24) | copy-start | bytes 28
  2.8 8.8 %copy-start.26 = (bf16[4]{0:T(256)(128)(2,1)S(1)}, bf16[4]{0:T(256)(128)(2,1)}, u32[]{:S(2)}) copy-start(bf16[4]{0:T(256)(128)(2,1)} %param.23) | copy-start | bytes 28
  131.8 13.7 %copy-start.12 = (f32[4,2048]{1,0:T(4,128)S(1)}, f32[4,2048]{1,0:T(4,128)}, u32[]{:S(2)}) copy-start(f32[4,2048]{1,0:T(4,128)} %get-tuple-element.61) | copy-start | bytes 98308
  131.8 14.4 %copy-start = (bf16[7,224,512]{2,1,0:T(8,128)(2,1)S(1)}, bf16[7,224,512]{2,1,0:T(8,128)(2,1)}, u32[]{:S(2)}) copy-start(bf16[7,224,512]{2,1,0:T(8,128)(2,1)} %get-tuple-element.58) | copy-start | bytes 4816900
  131.8 14.3 %copy-start.4 = (bf16[4,4,288,512]{3,2,1,0:T(8,128)(2,1)S(1)}, bf16[4,4,288,512]{3,2,1,0:T(8,128)(2,1)}, u32[]{:S(2)}) copy-start(bf16[4,4,288,512]{3,2,1,0:T(8,128)(2,1)} %get-tuple-element.60) | copy-start | bytes 14155780
  131.8 14.3 %copy-start.5 = (f32[7,224,512]{2,1,0:T(8,128)S(1)}, f32[7,224,512]{2,1,0:T(8,128)}, u32[]{:S(2)}) copy-start(f32[7,224,512]{2,1,0:T(8,128)} %get-tuple-element.57) | copy-start | bytes 9633796
  131.9 22.9 %slice-start = ((s8[4718592]{0:T(1024)(128)(4,1)}), s8[4194304]{0:T(1024)(128)(4,1)S(1)}, s32[]{:S(2)}) async-start(s8[4718592]{0:T(1024)(128)(4,1)} %bitcast.138), calls=%async_computation | async-start | bytes 8388608
  146.2 8.6 %slice-start.1 = ((s8[4718592]{0:T(1024)(128)(4,1)}), s8[524288]{0:T(1024)(128)(4,1)S(1)}, s32[]{:S(2)}) async-start(s8[4718592]{0:T(1024)(128)(4,1)} %bitcast.138), calls=%async_computation.1 | async-start | bytes 1048576
  154.8 9.6 %copy-start.1 = (bf16[7,7,32,512]{3,2,1,0:T(8,128)(2,1)}, bf16[7,7,32,512]{3,2,1,0:T(8,128)(2,1)S(1)}, u32[]{:S(2)}) copy-start(bf16[7,7,32,512]{3,2,1,0:T(8,128)(2,1)S(1)} %get-tuple-element.140.refs_5_) | copy-start | bytes 4816900
  256.8 27.6 %slice-start.2 = ((s8[4718592]{0:T(1024)(128)(4,1)}), s8[4194304]{0:T(1024)(128)(4,1)S(1)}, s32[]{:S(2)}) async-start(s8[4718592]{0:T(1024)(128)(4,1)} %bitcast.148), calls=%async_computation.2 | async-start | bytes 8388608
  271.2 13.3 %copy-start.2 = (bf16[7,7,32,512]{3,2,1,0:T(8,128)(2,1)}, bf16[7,7,32,512]{3,2,1,0:T(8,128)(2,1)S(1)}, u32[]{:S(2)}) copy-start(bf16[7,7,32,512]{3,2,1,0:T(8,128)(2,1)S(1)} %get-tuple-element.120) | copy-start | bytes 4816900
  271.2 13.3 %slice-start.3 = ((s8[4718592]{0:T(1024)(128)(4,1)}), s8[524288]{0:T(1024)(128)(4,1)S(1)}, s32[]{:S(2)}) async-start(s8[4718592]{0:T(1024)(128)(4,1)} %bitcast.148), calls=%async_computation.3 | async-start | bytes 1048576
  292.4 1.9 copy-start.3
  294.4 13.2 %copy-start.14 = (f32[1,128]{1,0:T(1,128)S(1)}, f32[1,128]{1,0:T(1,128)}, u32[]{:S(2)}) copy-start(f32[1,128]{1,0:T(1,128)} %get-tuple-element.70) | copy-start | bytes 1540
  294.4 13.2 %copy-start.15 = (f32[1,512]{1,0:T(1,128)S(1)}, f32[1,512]{1,0:T(1,128)}, u32[]{:S(2)}) copy-start(f32[1,512]{1,0:T(1,128)} %get-tuple-element.66) | copy-start | bytes 6148
  309.8 15.9 %copy-start.8 = (f32[7,7,32,64]{3,2,1,0:T(8,128)S(1)}, f32[7,7,32,64]{3,2,1,0:T(8,128)}, u32[]{:S(2)}) copy-start(f32[7,7,32,64]{3,2,1,0:T(8,128)} %get-tuple-element.80) | copy-start | bytes 1204228
  309.8 26.8 %copy-start.22 = (f32[1,64]{1,0:T(1,128)S(1)}, f32[1,64]{1,0:T(1,128)}, u32[]{:S(2)}) copy-start(f32[1,64]{1,0:T(1,128)} %get-tuple-element.78) | copy-start | bytes 772
  327.9 12.0 %copy-start.10 = (bf16[64,2048]{1,0:T(8,128)(2,1)S(1)}, bf16[64,2048]{1,0:T(8,128)(2,1)}, u32[]{:S(2)}) copy-start(bf16[64,2048]{1,0:T(8,128)(2,1)} %get-tuple-element.77) | copy-start | bytes 786436
  341.9 111.3 %copy-start.7 = (f32[2,49,1,2048]{3,2,1,0:T(1,128)S(1)}, f32[2,49,1,2048]{3,2,1,0:T(1,128)}, u32[]{:S(2)}) copy-start(f32[2,49,1,2048]{3,2,1,0:T(1,128)} %get-tuple-element.65) | copy-start | bytes 2408452
  451.4 7.9 %copy-start.6 = (f32[2,288,512]{2,1,0:T(8,128)S(1)}, f32[2,288,512]{2,1,0:T(8,128)}, u32[]{:S(2)}) copy-start(f32[2,288,512]{2,1,0:T(8,128)} %get-tuple-element.178) | copy-start | bytes 3538948
  451.4 8.9 %copy-start.27 = (f32[1,32]{1,0:T(1,128)S(1)}, f32[1,32]{1,0:T(1,128)}, u32[]{:S(2)}) copy-start(f32[1,32]{1,0:T(1,128)} %get-tuple-element.90) | copy-start | bytes 388
  451.4 9.4 %copy-start.9 = (f32[288,512]{1,0:T(8,128)S(1)}, f32[288,512]{1,0:T(8,128)}, u32[]{:S(2)}) copy-start(f32[288,512]{1,0:T(8,128)} %get-tuple-element.180) | copy-start | bytes 1769476
  453.2 8.4 %copy-start.11 = (f32[32,2048]{1,0:T(8,128)S(1)}, f32[32,2048]{1,0:T(8,128)}, u32[]{:S(2)}) copy-start(f32[32,2048]{1,0:T(8,128)} %get-tuple-element.183) | copy-start | bytes 786436
